TPU v7x, 128 devices: a whole 4x4x4 slice. The times are simulated.
128 devices in a mesh: seq: 8 (over z, x_hi), tensor: 4 (over y), section: 4 (over x_lo, core).
Axes of the slice: x: 4 (x_hi: 2, x_lo: 2; x = x_hi * 2 + x_lo), y: 4, z: 4, core: 2. Of those that a mesh axis runs over, the one named last changes fastest.
Arguments:
- dna_bases: int32 [8, 2048, 32], P('seq', 'section'), may hold values from 0 to 3
- stem_weight: bfloat16 [128, 1536], replicated, may hold values from -1 to 1
- conv_weight: bfloat16 [3, 1536, 1536], P(None, None, 'tensor'), may hold values from -0.09375 to 0.09375
- query_weight: bfloat16 [1536, 512], P(None, 'tensor'), may hold values from -0.15625 to 0.15625
- key_weight: bfloat16 [1536, 512], P(None, 'tensor'), may hold values from -0.15625 to 0.15625
- value_weight: bfloat16 [1536, 1536], P(None, 'tensor'), may hold values from -0.15625 to 0.15625
- out_weight: bfloat16 [1536, 1536], P('tensor'), may hold values from -0.15625 to 0.15625
- cotangent: bfloat16 [8, 2048, 1536], P('seq', 'section', 'tensor'), may hold values from -6 to 6
Outputs:
- conv_grad: float32 [1536, 3, 1536], P(('seq', 'section'), None, 'tensor')
All inputs are finite; a program needn't handle non-finite values.
Results may differ from a plain program's by a relative error of at most 0.013.
Values may be sent and summed in bfloat16 or wider, within the bound.
No kernel may reach another device: no remote copies, remote signals or barrier semaphores. Data moves between devices by JAX's collectives and lax.ppermute only.
A program may use at most 128 MiB of HBM per device.

v0:
```python
import math

import jax
import jax.numpy as jnp
from jax import lax
from jax.sharding import PartitionSpec as P

KEY_SIZE = 64
VALUE_SIZE = 192
DILATION = 32


EPSILON = 1e-06
SHARPNESS = 3.0


def extended(cells, sides, width):
    for axis, dim in sides:
        count = lax.axis_size(axis)
        ends = count - 1
        head = lax.slice_in_dim(cells, 0, width, axis=dim)
        tail = lax.slice_in_dim(cells, cells.shape[dim] - width, cells.shape[dim], axis=dim)
        cells = jnp.concatenate(
            [
                lax.ppermute(tail, axis, [(i, (i + 1) % count) for i in range(ends)]),
                cells,
                lax.ppermute(head, axis, [((i + 1) % count, i) for i in range(ends)]),
            ],
            axis=dim,
        )
    return cells


def unit_rows(raw_rows, head_size):
    shaped = raw_rows.reshape(raw_rows.shape[0], -1, head_size)
    factor = lax.rsqrt(jnp.mean(shaped * shaped, axis=-1, keepdims=True) + EPSILON)
    return ((shaped * factor).reshape(raw_rows.shape), factor)


def unit_back(grad_rows, normed, factor, head_size):
    grad_heads = grad_rows.reshape(grad_rows.shape[0], -1, head_size)
    norm_heads = normed.reshape(grad_heads.shape)
    row_mean = jnp.mean(grad_heads * norm_heads, axis=-1, keepdims=True)
    return (factor * (grad_heads - norm_heads * row_mean)).reshape(grad_rows.shape)


def body(
    dna_bases,
    stem_weight,
    conv_weight,
    query_weight,
    key_weight,
    value_weight,
    out_weight,
    cotangent,
):
    bases_here = dna_bases[0]
    cotangent_here = cotangent[0]
    local_rows, base_count = bases_here.shape
    own_width = conv_weight.shape[2]
    local_heads = query_weight.shape[1] // KEY_SIZE
    letters = jnp.arange(4, dtype=jnp.int32)
    onehot = (
        (bases_here[:, :, None] == letters[None, None, :])
        .reshape(local_rows, 4 * base_count)
        .astype(jnp.bfloat16)
    )
    stem_out = jnp.dot(onehot, stem_weight, preferred_element_type=jnp.float32)
    activated = jax.nn.gelu(stem_out, approximate=True).astype(jnp.bfloat16)
    padded = extended(activated, (("section", 0),), DILATION)
    windows = [padded[offset * DILATION : offset * DILATION + local_rows] for offset in range(3)]
    conv_out = jnp.zeros((local_rows, own_width), jnp.float32)
    for offset in range(3):
        conv_out = conv_out + jnp.dot(
            windows[offset], conv_weight[offset], preferred_element_type=jnp.float32
        )
    own_stem = lax.dynamic_slice_in_dim(
        stem_out, lax.axis_index("tensor") * own_width, own_width, 1
    )
    hidden_own = (own_stem + conv_out).astype(jnp.bfloat16)
    hidden_all, grad_all = (
        lax.all_gather(hidden_own, "tensor", axis=1, tiled=True),
        lax.all_gather(cotangent_here, "tensor", axis=1, tiled=True),
    )
    query_raw = jnp.dot(hidden_all, query_weight, preferred_element_type=jnp.float32)
    key_raw = jnp.dot(hidden_all, key_weight, preferred_element_type=jnp.float32)
    values = jnp.dot(hidden_all, value_weight, preferred_element_type=jnp.float32).astype(
        jnp.bfloat16
    )
    query_unit, query_factor = unit_rows(query_raw, KEY_SIZE)
    key_unit, key_factor = unit_rows(key_raw, KEY_SIZE)
    query_bf = query_unit.astype(jnp.bfloat16)
    key_bf = key_unit.astype(jnp.bfloat16)
    out_grad = jnp.einsum(
        "tc,vc->tv", grad_all, out_weight, preferred_element_type=jnp.float32
    ).astype(jnp.bfloat16)
    keys_all, values_all = (
        lax.all_gather(key_bf, "section", axis=0, tiled=True),
        lax.all_gather(values, "section", axis=0, tiled=True),
    )
    score_scale = SHARPNESS / math.sqrt(KEY_SIZE)
    query_parts, softmax_list, score_list, total_list, inner_list = ([], [], [], [], [])
    for head_index in range(local_heads):
        key_cols = slice(head_index * KEY_SIZE, (head_index + 1) * KEY_SIZE)
        value_cols = slice(head_index * VALUE_SIZE, (head_index + 1) * VALUE_SIZE)
        key_head = keys_all[:, key_cols]
        value_head = values_all[:, value_cols]
        grad_head = out_grad[:, value_cols]
        scores = (
            jnp.einsum(
                "td,jd->tj", query_bf[:, key_cols], key_head, preferred_element_type=jnp.float32
            )
            * score_scale
        )
        exponent = jnp.exp(scores)
        totals = jnp.sum(exponent, axis=1, keepdims=True)
        softmax_out = exponent / totals
        softmax_bf = softmax_out.astype(jnp.bfloat16)
        head_out = jnp.dot(softmax_bf, value_head, preferred_element_type=jnp.float32).astype(
            jnp.bfloat16
        )
        row_inner = jnp.sum(
            grad_head.astype(jnp.float32) * head_out.astype(jnp.float32), axis=1, keepdims=True
        )
        prob_grad = jnp.einsum(
            "tv,jv->tj", grad_head, value_head, preferred_element_type=jnp.float32
        )
        score_grad = (softmax_out * (prob_grad - row_inner) * score_scale).astype(jnp.bfloat16)
        query_parts.append(jnp.dot(score_grad, key_head, preferred_element_type=jnp.float32))
        softmax_list.append(softmax_bf)
        score_list.append(score_grad)
        total_list.append(totals)
        inner_list.append(row_inner)
    query_grad = jnp.concatenate(query_parts, axis=1)
    key_pieces = []
    value_pieces = []
    for head_index in range(local_heads):
        key_cols = slice(head_index * KEY_SIZE, (head_index + 1) * KEY_SIZE)
        value_cols = slice(head_index * VALUE_SIZE, (head_index + 1) * VALUE_SIZE)
        score_cols = score_list[head_index]
        softmax_cols = softmax_list[head_index]
        key_pieces.append(
            jnp.einsum(
                "tj,td->jd", score_cols, query_bf[:, key_cols], preferred_element_type=jnp.float32
            )
        )
        value_pieces.append(
            jnp.einsum(
                "tj,tv->jv",
                softmax_cols,
                out_grad[:, value_cols],
                preferred_element_type=jnp.float32,
            )
        )
    key_sums = lax.psum_scatter(
        jnp.concatenate(key_pieces + value_pieces, axis=1),
        "section",
        scatter_dimension=0,
        tiled=True,
    )
    key_grad = key_sums[:, : local_heads * KEY_SIZE]
    value_grad = key_sums[:, local_heads * KEY_SIZE :]
    query_back = unit_back(query_grad, query_unit, query_factor, KEY_SIZE).astype(jnp.bfloat16)
    key_back = unit_back(key_grad, key_unit, key_factor, KEY_SIZE).astype(jnp.bfloat16)
    value_back = value_grad.astype(jnp.bfloat16)
    partial_grad = jnp.einsum(
        "th,ch->tc", query_back, query_weight, preferred_element_type=jnp.float32
    )
    partial_grad = partial_grad + jnp.einsum(
        "th,ch->tc", key_back, key_weight, preferred_element_type=jnp.float32
    )
    partial_grad = partial_grad + jnp.einsum(
        "tv,cv->tc", value_back, value_weight, preferred_element_type=jnp.float32
    )
    hidden_grad = lax.psum_scatter(partial_grad, "tensor", scatter_dimension=1, tiled=True)
    hidden_grad = (hidden_grad + cotangent_here.astype(jnp.float32)).astype(jnp.bfloat16)
    group_size = lax.axis_size("seq") * lax.axis_size("section")
    tap_parts = []
    for offset in range(3):
        window_cols = windows[offset]
        tap_parts.append(
            jnp.einsum("ti,to->io", window_cols, hidden_grad, preferred_element_type=jnp.float32)
        )
    summed = lax.psum_scatter(
        jnp.stack(tap_parts, axis=1), ("seq", "section"), scatter_dimension=0, tiled=True
    )
    return summed * (1.0 / math.sqrt(local_rows * group_size))


def solution(mesh):
    in_specs = (
        P("seq", "section", None),
        P(),
        P(None, None, "tensor"),
        P(None, "tensor"),
        P(None, "tensor"),
        P(None, "tensor"),
        P("tensor", None),
        P("seq", "section", "tensor"),
    )
    out_specs = P(("seq", "section"), None, "tensor")
    return jax.shard_map(body, mesh=mesh, in_specs=in_specs, out_specs=out_specs, check_vma=False)
```

profile of v0, /device:TPU:0, one launch (start us, length us, event | category | flops | bytes accessed | tf_op | source)
XLA Modules:
  0.0 307.6 jit_solution(4530694085952661593)
XLA Ops:
  8.4 3.8 %fusion.12 = (bf16[512,1536]{1,0:T(8,128)(2,1)S(1)}, f32[512,1536]{1,0:T(8,128)}) fusion(bf16[128,1536]{1,0:T(8,128)(2,1)} %param.9, s32[512,128]{0,1:T(8,128)S(1)} %eq.24, s32[128]{0:T(128)S(1)} %eq.26), kind=kOutput, calls=%fused_computation.20 | convolution fusion | flops 208470016 | bytes 5374464 | tf_op jit(solution)/shard_map/dot_general | solution.py:68
  12.3 1.3 collective-permute-start
  13.6 1.3 collective-permute-start.1
  14.9 3.1 %fusion.23 = f32[512,384]{1,0:T(8,128)} fusion(bf16[512,1536]{1,0:T(8,128)(2,1)S(1)} %get-tuple-element.7, bf16[3,1536,384]{2,1,0:T(8,128)(2,1)} %param.10), kind=kOutput, calls=%fused_computation.36 | convolution fusion | flops 603979776 | bytes 3538944 | tf_op jit(solution)/shard_map/dot_general | solution.py:74
  18.6 2.3 fusion.21
  20.9 3.4 %fusion.17 = bf16[512,384]{1,0:T(8,128)(2,1)} fusion(f32[512,384]{1,0:T(8,128)S(1)} %fusion.21, f32[512,384]{1,0:T(8,128)S(1)} %copy-done.26, bf16[3,1536,384]{2,1,0:T(8,128)(2,1)} %param.10, bf16[512,1536]{1,0:T(8,128)(2,1)S(1)} %get-tuple-element.7, bf16[32,1536]{1,0:T(8,128)(2,1)S(1)} %collective-permute-done, f32[512,1536]{1,0:T(8,128)} %get-tuple-element.8, ...), kind=kOutput, calls=%fused_computation.31 | convolution fusion | flops 607911936 | bytes 5603332 | tf_op jit(solution)/shard_map/dot_general | solution.py:74
  24.4 13.7 %all-gather.9.cloned.1.call-done = bf16[1,512,1536]{2,1,0:T(8,128)(2,1)} async-done(((bf16[1,512,384]{2,1,0:T(8,128)(2,1)}), bf16[1,512,1536]{2,1,0:T(8,128)(2,1)}) %all-gather.9.cloned.1.call-update) | async-done | bytes 1572880 | tf_op jit(solution)/shard_map/all_gather | solution.py:83
  38.1 3.3 %fusion.18 = bf16[512,384]{0,1:T(8,128)(2,1)} fusion(bf16[384,1536]{1,0:T(8,128)(2,1)} %param.14, bf16[1,512,1536]{2,1,0:T(8,128)(2,1)} %all-gather.9.cloned.1.call-done), kind=kOutput, calls=%fused_computation.32 | convolution fusion | flops 604176384 | bytes 3145728 | tf_op jit(solution)/shard_map/tc,vc->tv/dot_general | solution.py:94
  41.4 25.0 %all-gather.5.cloned.1.call-done = bf16[512,1536]{1,0:T(8,128)(2,1)} async-done(((bf16[512,384]{1,0:T(8,128)(2,1)}), bf16[512,1536]{1,0:T(8,128)(2,1)}) %all-gather.5.cloned.1.call-update) | async-done | bytes 1572880 | tf_op jit(solution)/shard_map/all_gather | solution.py:82
  66.4 2.1 multiply_reduce_fusion.3
  68.5 3.3 %convolution_convert_fusion = bf16[512,384]{1,0:T(8,128)(2,1)} fusion(bf16[512,1536]{1,0:T(8,128)(2,1)} %all-gather.5.cloned.1.call-done, bf16[1536,384]{1,0:T(8,128)(2,1)S(1)} %copy-done), kind=kOutput, calls=%fused_computation.33 | convolution fusion | flops 604176384 | bytes 3145728 | tf_op jit(solution)/shard_map/dot_general | solution.py:87
  71.9 1.7 multiply_reduce_fusion.2
  73.7 7.3 %all_gather.13 = bf16[2048,128]{0,1:T(8,128)(2,1)S(1)} all-gather(bf16[512,128]{0,1:T(8,128)(2,1)S(1)} %fusion.54), channel_id=1, replica_groups=mesh['seq'=8,'tensor'=4,'section'=4] {'section'}, dimensions={0}, use_global_device_ids=true | all-gather | bytes 655360 | tf_op jit(solution)/shard_map/all_gather | solution.py:98
  83.2 2.4 fusion.35
  85.6 2.2 fusion.38
  87.8 8.9 %all-gather.7.cloned.1.call-done = bf16[2048,384]{1,0:T(8,128)(2,1)} async-done(((bf16[512,384]{1,0:T(8,128)(2,1)}), bf16[2048,384]{1,0:T(8,128)(2,1)}) %all-gather.7.cloned.1.call-update) | async-done | bytes 1572880 | tf_op jit(solution)/shard_map/all_gather | solution.py:99
  96.7 4.0 %fusion.33 = f32[512]{0:T(512)S(1)} fusion(bf16[2048,384]{1,0:T(8,128)(2,1)} %all-gather.7.cloned.1.call-done, bf16[512,384]{0,1:T(8,128)(2,1)S(1)} %copy-done.27, f32[512,2048]{1,0:T(8,128)} %copy-done.7, f32[512]{0:T(512)S(1)} %get-tuple-element.13), kind=kOutput, calls=%fused_computation.48 | convolution fusion | flops 406289920 | bytes 5443584 | tf_op jit(solution)/shard_map/dot_general | solution.py:119
  101.0 1.6 multiply_convert_fusion
  104.4 1.7 multiply_convert_fusion.1
  106.2 1.3 copy-done.2
  108.9 2.2 pad_maximum_fusion.1
  111.4 1.8 fusion.55
  113.2 2.4 fusion.59
  115.7 2.3 fusion.83
  118.0 39.5 %reduce-scatter.4.cloned.1.call-done = f32[512,512]{0,1:T(8,128)} async-done(((f32[2048,512]{0,1:T(8,128)}), f32[512,512]{0,1:T(8,128)}) %reduce-scatter.4.cloned.1.call-update) | async-done | bytes 1048592 | tf_op jit(solution)/shard_map/reduce_scatter | solution.py:155
  158.7 2.2 fusion.46
  161.9 2.2 fusion.4
  164.3 39.4 %reduce-scatter.6.cloned.1.call-done = f32[512,384]{1,0:T(8,128)} async-done(((f32[512,1536]{1,0:T(8,128)}), f32[512,384]{1,0:T(8,128)}) %reduce-scatter.6.cloned.1.call-update) | async-done | bytes 786448 | tf_op jit(solution)/shard_map/reduce_scatter | solution.py:175
  203.6 1.2 fusion.45
  207.9 3.3 %pad_maximum_fusion = f32[1536,3,384]{2,0,1:T(8,128)} fusion(f32[1536,1,384]{2,0,1:T(8,128)S(1)} %convolution_bitcast_fusion, f32[1536,1,384]{2,0,1:T(8,128)S(1)} %convolution_bitcast_fusion.1, f32[1536,1,384]{2,0,1:T(8,128)S(1)} %convolution_bitcast_fusion.2), kind=kLoop, calls=%fused_computation | loop fusion | flops 3538944 | bytes 14155776 | tf_op jit(solution)/shard_map/stack | solution.py:185
  211.3 87.9 %reduce-scatter.8.cloned.1.call-done = f32[48,3,384]{2,0,1:T(8,128)} async-done(((f32[1536,3,384]{2,0,1:T(8,128)}), f32[48,3,384]{2,0,1:T(8,128)}) %reduce-scatter.8.cloned.1.call-update) | async-done | bytes 221200 | tf_op jit(solution)/shard_map/reduce_scatter | solution.py:184
  299.1 1.6 broadcast_multiply_fusion
  (94 shorter events, 14.0 us)
Async XLA Ops:
  6.5 61.9 %copy-start = (bf16[1536,384]{1,0:T(8,128)(2,1)S(1)}, bf16[1536,384]{1,0:T(8,128)(2,1)}, u32[]{:S(2)}) copy-start(bf16[1536,384]{1,0:T(8,128)(2,1)} %param.13) | copy-start | bytes 3538948
  6.5 31.5 %all-gather.9.cloned.1.call-start = ((), (), s32[]{:S(2)}) async-start(), calls=%async_computation.8 | async-start | bytes 1966080 | tf_op jit(solution)/shard_map/all_gather | solution.py:83
  7.3 59.1 %all-gather.5.cloned.1.call-start = ((), (), s32[]{:S(2)}) async-start(), calls=%async_computation.3 | async-start | bytes 1966080 | tf_op jit(solution)/shard_map/all_gather | solution.py:82
  12.3 8.6 %copy-start.19 = (bf16[512,1536]{1,0:T(8,128)(2,1)}, bf16[512,1536]{1,0:T(8,128)(2,1)S(1)}, u32[]{:S(2)}) copy-start(bf16[512,1536]{1,0:T(8,128)(2,1)S(1)} %get-tuple-element.7) | copy-start | bytes 4718596
  12.3 8.6 %collective-permute-start = (bf16[32,1536]{1,0:T(8,128)(2,1)S(1)}, bf16[32,1536]{1,0:T(8,128)(2,1)S(1)}, u32[]{:S(2)}, u32[]{:S(2)}) collective-permute-start(bf16[32,1536]{1,0:T(8,128)(2,1)S(1)} %get-tuple-element.5), channel_id=1, source_target_pairs={{0,1},{1,2},{2,3},{4,5},{5,6},{6,7},{8,9},{9,10},{10,11},{12,13},{... | collective-permute-start | bytes 294920 | tf_op jit(solution)/shard_map/ppermute | solution.py:25
  13.6 5.0 %collective-permute-start.1 = (bf16[32,1536]{1,0:T(8,128)(2,1)S(1)}, bf16[32,1536]{1,0:T(8,128)(2,1)S(1)}, u32[]{:S(2)}, u32[]{:S(2)}) collective-permute-start(bf16[32,1536]{1,0:T(8,128)(2,1)S(1)} %get-tuple-element.6), channel_id=1, source_target_pairs={{1,0},{2,1},{3,2},{5,4},{6,5},{7,6},{9,8},{10,9},{11,10},{13,12},{... | collective-permute-start | bytes 294920 | tf_op jit(solution)/shard_map/ppermute | solution.py:27
  18.0 2.9 copy-start.26
  18.6 5.7 %copy-start.24 = (bf16[32,1536]{1,0:T(8,128)(2,1)}, bf16[32,1536]{1,0:T(8,128)(2,1)S(1)}, u32[]{:S(2)}) copy-start(bf16[32,1536]{1,0:T(8,128)(2,1)S(1)} %collective-permute-done.1) | copy-start | bytes 294916
  20.9 3.4 %copy-start.22 = (bf16[32,1536]{1,0:T(8,128)(2,1)}, bf16[32,1536]{1,0:T(8,128)(2,1)S(1)}, u32[]{:S(2)}) copy-start(bf16[32,1536]{1,0:T(8,128)(2,1)S(1)} %collective-permute-done) | copy-start | bytes 294916
  24.3 42.1 %copy-start.15 = (bf16[1536,128]{1,0:T(8,128)(2,1)S(1)}, bf16[1536,128]{1,0:T(8,128)(2,1)}, u32[]{:S(2)}) copy-start(bf16[1536,128]{1,0:T(8,128)(2,1)} %param.11) | copy-start | bytes 1179652
  24.3 72.4 %all-gather.7.cloned.1.call-start = ((), (), s32[]{:S(2)}) async-start(), calls=%async_computation.4 | async-start | bytes 1966080 | tf_op jit(solution)/shard_map/all_gather | solution.py:99
  68.5 3.4 %copy-start.3 = (bf16[512,1536]{1,0:T(8,128)(2,1)S(1)}, bf16[512,1536]{1,0:T(8,128)(2,1)}, u32[]{:S(2)}) copy-start(bf16[512,1536]{1,0:T(8,128)(2,1)} %all-gather.5.cloned.1.call-done) | copy-start | bytes 4718596
  71.8 85.8 %reduce-scatter.4.cloned.1.call-start = ((), (), s32[]{:S(2)}) async-start(), calls=%async_computation.5 | async-start | bytes 5242880 | tf_op jit(solution)/shard_map/reduce_scatter | solution.py:155
  71.9 10.0 %copy-start.17 = (bf16[512,128]{0,1:T(8,128)(2,1)}, bf16[512,128]{0,1:T(8,128)(2,1)S(1)}, u32[]{:S(2)}) copy-start(bf16[512,128]{0,1:T(8,128)(2,1)S(1)} %fusion.53) | copy-start | bytes 393220
  73.6 9.1 %copy-start.9 = (f32[512,128]{0,1:T(8,128)}, f32[512,128]{0,1:T(8,128)S(1)}, u32[]{:S(2)}) copy-start(f32[512,128]{0,1:T(8,128)S(1)} %get-tuple-element.10) | copy-start | bytes 786436
  81.0 1.8 copy-start.4
  81.9 3.8 %copy-start.7 = (f32[512,2048]{1,0:T(8,128)}, f32[512,2048]{1,0:T(8,128)S(1)}, u32[]{:S(2)}) copy-start(f32[512,2048]{1,0:T(8,128)S(1)} %get-tuple-element.14) | copy-start | bytes 12582916
  82.7 2.9 copy-start.5
  96.7 4.0 %copy-start.8 = (f32[512,2048]{1,0:T(8,128)S(1)}, f32[512,2048]{1,0:T(8,128)}, u32[]{:S(2)}) copy-start(f32[512,2048]{1,0:T(8,128)} %copy-done.7) | copy-start | bytes 12582916
  96.7 4.2 %copy-start.21 = (bf16[2048,384]{1,0:T(8,128)(2,1)S(1)}, bf16[2048,384]{1,0:T(8,128)(2,1)}, u32[]{:S(2)}) copy-start(bf16[2048,384]{1,0:T(8,128)(2,1)} %all-gather.7.cloned.1.call-done) | copy-start | bytes 4718596
  96.7 4.3 %copy-start.28 = (bf16[512,384]{0,1:T(8,128)(2,1)S(1)}, bf16[512,384]{0,1:T(8,128)(2,1)}, u32[]{:S(2)}) copy-start(bf16[512,384]{0,1:T(8,128)(2,1)} %fusion.18) | copy-start | bytes 1179652
  101.0 1.6 copy-start.18
  101.0 2.3 copy-start.6
  104.4 3.6 %copy-start.13 = (f32[2048,192]{0,1:T(8,128)S(1)}, f32[2048,192]{0,1:T(8,128)}, u32[]{:S(2)}) copy-start(f32[2048,192]{0,1:T(8,128)} %fusion.38) | copy-start | bytes 4718596
  111.1 92.5 %reduce-scatter.6.cloned.1.call-start = ((), (), s32[]{:S(2)}) async-start(), calls=%async_computation.6 | async-start | bytes 3932160 | tf_op jit(solution)/shard_map/reduce_scatter | solution.py:175
  111.4 4.3 %copy-start.16 = (bf16[1536,128]{1,0:T(8,128)(2,1)S(1)}, bf16[1536,128]{1,0:T(8,128)(2,1)}, u32[]{:S(2)}) copy-start(bf16[1536,128]{1,0:T(8,128)(2,1)} %param.11) | copy-start | bytes 1179652
  113.2 44.4 %copy-start.10 = (f32[512,128]{0,1:T(8,128)S(1)}, f32[512,128]{0,1:T(8,128)}, u32[]{:S(2)}) copy-start(f32[512,128]{0,1:T(8,128)} %copy-done.9) | copy-start | bytes 786436
  118.0 43.9 %copy-start.11 = (bf16[1536,128]{1,0:T(8,128)(2,1)S(1)}, bf16[1536,128]{1,0:T(8,128)(2,1)}, u32[]{:S(2)}) copy-start(bf16[1536,128]{1,0:T(8,128)(2,1)} %param.12) | copy-start | bytes 1179652
  157.6 4.4 %copy-start.1 = (f32[512,1536]{1,0:T(8,128)S(1)}, f32[512,1536]{1,0:T(8,128)}, u32[]{:S(2)}) copy-start(f32[512,1536]{1,0:T(8,128)} %fusion.83) | copy-start | bytes 9437188
  164.2 39.4 %copy-start.14 = (bf16[1,512,384]{2,1,0:T(8,128)(2,1)S(1)}, bf16[1,512,384]{2,1,0:T(8,128)(2,1)}, u32[]{:S(2)}) copy-start(bf16[1,512,384]{2,1,0:T(8,128)(2,1)} %param.15) | copy-start | bytes 1179652
  164.2 40.6 %copy-start.20 = (bf16[512,1536]{1,0:T(8,128)(2,1)S(1)}, bf16[512,1536]{1,0:T(8,128)(2,1)}, u32[]{:S(2)}) copy-start(bf16[512,1536]{1,0:T(8,128)(2,1)} %copy-done.19) | copy-start | bytes 4718596
  164.2 134.9 %reduce-scatter.8.cloned.1.call-start = ((), (), s32[]{:S(2)}) async-start(), calls=%async_computation.7 | async-start | bytes 7299072 | tf_op jit(solution)/shard_map/reduce_scatter | solution.py:184
  (5 other events, 6.1 us)
Sparse Core Ops, SparseCore 0:
  9.0 28.9 all-gather.8
  39.8 26.5 all-gather.4
  71.9 24.7 all-gather.6
  111.3 46.2 reduce-scatter.3
  164.3 39.2 reduce-scatter.5
  211.4 87.6 reduce-scatter.7
where the time goes:
time: 308 us
  waiting for transfers between devices  216 us (70%)
  matrix products  52.6 us (17%)
  between operations  13.9 us (5%)
  other arithmetic  10.7 us (3%)
  blocking collectives  7.33 us (2%)
  local copies, waits for them, and re-layouts  4.31 us (1%)
    reduce_scatter x1, waiting for transfers between devices, body(): lax.psum_scatter(jnp.stack(tap_parts, axis=1), ('seq', 'section'), scatte...  87.9 us
    reduce_scatter x1, waiting for transfers between devices, body(): lax.psum_scatter(jnp.concatenate(key_pieces + value_pieces, axis=1), 'sec...  39.5 us
    reduce_scatter x1, waiting for transfers between devices, body(): lax.psum_scatter(partial_grad, 'tensor', scatter_dimension=1, tiled=True)  39.4 us
    all_gather x1, waiting for transfers between devices, body(): lax.all_gather(hidden_own, 'tensor', axis=1, tiled=True)  25 us
    all_gather x1, waiting for transfers between devices, body(): lax.all_gather(cotangent_here, 'tensor', axis=1, tiled=True)  13.7 us
    all_gather x1, waiting for transfers between devices, body(): lax.all_gather(values, 'section', axis=0, tiled=True)  8.93 us
    dot_general x3, matrix products, body(): jnp.dot(windows[offset], conv_weight[offset], preferred_element_type=jnp....  8.79 us
    all_gather x1, blocking collectives, body(): lax.all_gather(key_bf, 'section', axis=0, tiled=True)  7.33 us
  transfers between devices with their start and end apart: 8, of which 7 were waited for; matrix products, arithmetic and copies ran while one was open for 10% of the time, Pallas kernels for 0%

commit v1 on v0

v1 whole, which is shorter than its diff:
```python
import functools
import math

import jax
import jax.numpy as jnp
from jax import lax
from jax.experimental import pallas as pl
from jax.experimental.pallas import tpu as pltpu
from jax.sharding import PartitionSpec as P

KEY = 64
VAL = 192
HALO = 32
EPSILON = 1e-06
SCALE = 3.0 / math.sqrt(KEY)
LOG2E = math.log2(math.e)

f32 = jnp.float32
bf16 = jnp.bfloat16
MIB = 1 << 20


def nn(left, right):
    return jnp.dot(left, right, preferred_element_type=f32)


def nt(left, right):
    return lax.dot_general(left, right, (((1,), (1,)), ((), ())), preferred_element_type=f32)


def call(kernel, outs, *args, scratch=(), flops=0, vmem=32):
    size = sum(math.prod(a.shape) * a.dtype.itemsize for a in args)
    return pl.pallas_call(
        kernel,
        out_shape=[jax.ShapeDtypeStruct(shape, kind) for shape, kind in outs],
        in_specs=[pl.BlockSpec(memory_space=pltpu.VMEM)] * len(args),
        out_specs=[pl.BlockSpec(memory_space=pltpu.VMEM)] * len(outs),
        scratch_shapes=list(scratch),
        compiler_params=pltpu.CompilerParams(vmem_limit_bytes=vmem * MIB),
        cost_estimate=pl.CostEstimate(flops=int(flops), bytes_accessed=int(size), transcendentals=0),
    )(*args)


def own_chip():
    section = lax.axis_index("section")
    return section >> 1, section & 1


def block_at(index, width):
    return pl.ds(pl.multiple_of(index * width, width), width)


def one_hot(marks):
    spread = (
        lax.broadcasted_iota(jnp.int32, (32, 128), 1) >> 2
        == lax.broadcasted_iota(jnp.int32, (32, 128), 0)
    )
    spread = jnp.where(spread, 1.0, 0.0).astype(bf16)
    wide = nn(marks.astype(f32).astype(bf16), spread)
    letter = ((lax.broadcasted_iota(jnp.int32, wide.shape, 1) & 3) + 1).astype(f32)
    return jnp.where(wide == letter, 1.0, 0.0).astype(bf16)


def gelu(x):
    return jax.nn.gelu(x, approximate=True)


def stem_kernel(marks_ref, weight_ref, act_ref):
    hot = one_hot(marks_ref[...])
    for j in range(0, weight_ref.shape[1], 256):
        act_ref[:, j : j + 256] = gelu(nn(hot, weight_ref[:, j : j + 256])).astype(bf16)


def conv_kernel(marks_ref, low_ref, high_ref, stem_ref, act_ref, weight_ref, hidden_ref, ext_ref):
    rows = act_ref.shape[0]
    width = weight_ref.shape[2]
    edge = jnp.concatenate([low_ref[...], high_ref[...]], axis=0)
    hot = one_hot(edge)
    edge_act = gelu(nn(hot, stem_ref[...])).astype(bf16)
    ext_ref[0:HALO] = edge_act[:HALO]
    ext_ref[HALO : HALO + rows] = act_ref[...]
    ext_ref[HALO + rows :] = edge_act[HALO:]
    own = stem_ref[:, block_at(lax.axis_index("tensor"), width)]
    total = nn(one_hot(marks_ref[...]), own)
    for k in range(3):
        total = total + nn(ext_ref[k * HALO : k * HALO + rows], weight_ref[k])
    hidden_ref[...] = total.astype(bf16)


def turn_kernel(q_ref, k_ref, v_ref, out_ref):
    out_ref[0:128] = q_ref[...].T
    out_ref[128:256] = k_ref[...].T
    out_ref[256:640] = v_ref[...].T


def taps_kernel(ext_ref, mine_ref, other_ref, turned):
    rows = turned.shape[1]
    _, core = own_chip()
    for k in range(3):
        turned[...] = ext_ref[k * HALO : k * HALO + rows].T
        for x in range(4):
            for z in range(4):
                to = ((x * 4 + z) * 3 + k) * 48
                base = z * 384 + x * 96
                mine_ref[to : to + 48] = turned[pl.ds(pl.multiple_of(base + core * 48, 16), 48)]
                other_ref[to : to + 48] = turned[
                    pl.ds(pl.multiple_of(base + (1 - core) * 48, 16), 48)
                ]


def project_kernel(h0, h1, h2, h3, w_ref, mine_ref, other_ref, unit_ref, factor_ref, values):
    y = lax.axis_index("tensor")
    chip, _ = own_chip()
    total = nt(w_ref[:, block_at(y, 384)], h0[...])
    for d, ref in ((1, h1), (2, h2), (3, h3)):
        total = total + nt(w_ref[:, block_at(y ^ d, 384)], ref[...])
    for g in range(4):
        raw = total[g * KEY : (g + 1) * KEY]
        factor = lax.rsqrt(jnp.mean(raw * raw, axis=0, keepdims=True) + EPSILON)
        unit_ref[g * KEY : (g + 1) * KEY] = raw * factor
        factor_ref[g : g + 1] = factor
    values[...] = total[256:].astype(bf16)
    for ref, head in ((mine_ref, chip), (other_ref, 1 - chip)):
        ref[0:64] = unit_ref[block_at(head, KEY)].astype(bf16)
        ref[64:128] = unit_ref[pl.ds(pl.multiple_of(128 + head * KEY, KEY), KEY)].astype(bf16)
        ref[128:320] = values[block_at(head, VAL)]


def grad_kernel(c0, c1, c2, c3, w_ref, mine_ref, other_ref):
    y = lax.axis_index("tensor")
    chip, _ = own_chip()
    for ref, head in ((mine_ref, chip), (other_ref, 1 - chip)):
        total = nt(w_ref[block_at(head, VAL), block_at(y, 384)], c0[...])
        for d, c in ((1, c1), (2, c2), (3, c3)):
            total = total + nt(w_ref[block_at(head, VAL), block_at(y ^ d, 384)], c[...])
        ref[...] = total.astype(bf16)


def attend_kernel(
    own, par, sib_own, sib_par, g_own, g_par,
    q_own_ref, q_par_ref, kv_mine_ref, kv_sib_ref,
    kv_t, kv_n, exps, score_grads, grads, queries,
):
    sections = (own, par, sib_own, sib_par)
    n = own.shape[1]
    for i, ref in enumerate(sections):
        kv = ref[64:320]
        kv_t[:, i * n : (i + 1) * n] = kv
        kv_n[i * n : (i + 1) * n] = kv.T
    width = 256
    zeros_q = jnp.zeros((VAL, width), bf16)
    zeros_g = jnp.zeros((KEY, width), bf16)
    for b in range(2 * n // width):
        src, g_src, dst = ((own, g_own, q_own_ref), (par, g_par, q_par_ref))[b * width // n]
        cols = slice((b * width) % n, (b * width) % n + width)
        lanes = slice(b * width, (b + 1) * width)
        query = src[0:64, cols]
        queries[:, lanes] = query
        right = jnp.concatenate([query, zeros_q], axis=0)
        total = jnp.zeros((1, width), f32)
        for i in range(4):
            e = jnp.exp2(nn(kv_n[i * n : (i + 1) * n], right) * (SCALE * LOG2E))
            total = total + jnp.sum(e, axis=0, keepdims=True)
            exps[i * n : (i + 1) * n, lanes] = e.astype(bf16)
        out = nn(kv_t[64:256], exps[:, lanes])
        inverse = 1.0 / total
        grad = (g_src[:, cols].astype(f32) * inverse).astype(bf16)
        grads[:, lanes] = grad
        inner = jnp.sum(grad.astype(f32) * out, axis=0, keepdims=True) * inverse
        right = jnp.concatenate([zeros_g, grad], axis=0)
        for i in range(4):
            prob = nn(kv_n[i * n : (i + 1) * n], right)
            e = exps[i * n : (i + 1) * n, lanes].astype(f32)
            score_grads[i * n : (i + 1) * n, lanes] = (e * (prob - inner)).astype(bf16)
        dst[:, cols] = (nn(kv_t[0:64], score_grads[:, lanes]) * SCALE).astype(bf16)
    for i, ref, at in ((2, kv_sib_ref, 0), (3, kv_sib_ref, n), (0, kv_mine_ref, 0), (1, kv_mine_ref, n)):
        key_grad = nt(queries[...], score_grads[i * n : (i + 1) * n]) * SCALE
        ref[0:64, at : at + n] = key_grad.astype(ref.dtype)
        value_grad = nt(grads[...], exps[i * n : (i + 1) * n])
        ref[64:256, at : at + n] = value_grad.astype(ref.dtype)


def join_kernel(q_own, q_par, kv_mine, kv_got, own_ref, par_ref):
    n = q_own.shape[1]
    par_ref[0:64] = q_par[...]
    par_ref[64:320] = (kv_mine[:, n:] + kv_got[:, n:].astype(f32)).astype(bf16)
    own_ref[0:64] = q_own[...]
    own_ref[64:320] = (kv_mine[:, :n] + kv_got[:, :n].astype(f32)).astype(bf16)


def back_kernel(own, other, unit_ref, factor_ref, wq, wk, wv, back, to1, to2, to3):
    y = lax.axis_index("tensor")
    chip, _ = own_chip()
    for ref, head in ((own, chip), (other, 1 - chip)):
        for kind in range(2):
            at = pl.ds(pl.multiple_of(kind * 128 + head * KEY, KEY), KEY)
            unit = unit_ref[at]
            factor = factor_ref[pl.ds(kind * 2 + head, 1)]
            g = ref[kind * 64 : kind * 64 + 64].astype(f32)
            mean = jnp.mean(g * unit, axis=0, keepdims=True)
            back[at] = (factor * (g - unit * mean)).astype(bf16)
        back[pl.ds(pl.multiple_of(256 + head * VAL, 64), VAL)] = ref[128:320]
    for d, ref in ((2, to2), (1, to1), (3, to3)):
        ref[...] = back_rows(back, wq, wk, wv, y ^ d).astype(bf16)


def back_rows(back, wq, wk, wv, index):
    at = block_at(index, 384)
    qk = jnp.concatenate([wq[at], wk[at]], axis=1)
    return nn(qk, back[0:256]) + nn(wv[at], back[256:640])


def back_own_kernel(back, wq, wk, wv, cot, out_ref):
    y = lax.axis_index("tensor")
    out_ref[...] = back_rows(back, wq, wk, wv, y) + cot[...].astype(f32).T


def hidden_grad_kernel(own, r1, r2, r3, out_ref):
    out_ref[...] = (
        own[...] + r1[...].astype(f32) + r2[...].astype(f32) + r3[...].astype(f32)
    ).astype(bf16)


def ring_place():
    x = (lax.axis_index("seq") & 1) * 2 + (lax.axis_index("section") >> 1)
    z = lax.axis_index("seq") >> 1
    return x, z


def tap_kernel(d, t_mine, t_sib, g_mine, g_sib, out_ref):
    x, _ = ring_place()
    at = block_at(x ^ d, 576)
    out_ref[...] = (nt(t_mine[at], g_mine[...]) + nt(t_sib[at], g_sib[...])).astype(out_ref.dtype)


def sum_x_kernel(own, r1, r2, r3, own_ref, to1, to2, to3):
    _, z = ring_place()
    for d, ref in ((2, to2), (1, to1), (3, to3), (0, own_ref)):
        at = block_at(z ^ d, 144)
        ref[...] = (
            own[at] + r1[at].astype(f32) + r2[at].astype(f32) + r3[at].astype(f32)
        ).astype(ref.dtype)


def sum_z_kernel(norm, own, r1, r2, r3, out_ref):
    out_ref[...] = (
        own[...] + r1[...].astype(f32) + r2[...].astype(f32) + r3[...].astype(f32)
    ) * norm


def body(bases, stem_w, conv_w, wq, wk, wv, out_w, cot):
    marks = bases[0] + 1
    cot = cot[0]
    rows = marks.shape[0]
    flat = ("seq", "section")

    low = lax.ppermute(marks[rows - HALO :], "section", [(i, i + 1) for i in range(3)])
    high = lax.ppermute(marks[:HALO], "section", [(i + 1, i) for i in range(3)])

    def over_y(value, d):
        return lax.ppermute(value, "tensor", [(i, i ^ d) for i in range(4)])

    def over_core(value):
        return lax.ppermute(value, "section", [(i, i ^ 1) for i in range(4)])

    def over_chip(value):
        return lax.ppermute(value, "section", [(i, i ^ 2) for i in range(4)])

    def over_x(value, d):
        return lax.ppermute(value, flat, [(i, i ^ (2 * d)) for i in range(32)])

    def over_z(value, d):
        return lax.ppermute(value, flat, [(i, i ^ (8 * d)) for i in range(32)])

    cots = [cot] + [over_y(cot, d) for d in (1, 2, 3)]

    (act,) = call(stem_kernel, [((rows, 1536), bf16)], marks, stem_w, flops=4e8)
    hidden, ext = call(
        conv_kernel,
        [((rows, 384), bf16), ((rows + 2 * HALO, 1536), bf16)],
        marks, low, high, stem_w, act, conv_w,
        flops=2e9,
    )
    hiddens = [hidden] + [over_y(hidden, d) for d in (1, 2, 3)]

    (w_t,) = call(turn_kernel, [((640, 1536), bf16)], wq, wk, wv, flops=1e9)
    taps_mine, taps_other = call(
        taps_kernel, [((2304, rows), bf16)] * 2, ext,
        scratch=[pltpu.VMEM((1536, rows), bf16)], flops=3e9,
    )
    taps_sib = over_core(taps_other)

    g_own, g_other = call(grad_kernel, [((VAL, rows), bf16)] * 2, *cots, out_w, flops=1e9)
    g_par = over_chip(g_other)

    own, other, unit, factor = call(
        project_kernel,
        [((320, rows), bf16)] * 2 + [((256, rows), f32), ((4, rows), f32)],
        *hiddens, w_t,
        scratch=[pltpu.VMEM((384, rows), bf16)], flops=1.5e9,
    )
    par = over_chip(other)
    sib_own = over_core(own)
    sib_par = over_core(par)
    q_own, q_par, kv_mine, kv_sib = call(
        attend_kernel,
        [((KEY, rows), bf16)] * 2 + [((256, 2 * rows), f32), ((256, 2 * rows), bf16)],
        own, par, sib_own, sib_par, g_own, g_par,
        scratch=[
            pltpu.VMEM((256, 4 * rows), bf16),
            pltpu.VMEM((4 * rows, 256), bf16),
            pltpu.VMEM((4 * rows, 2 * rows), bf16),
            pltpu.VMEM((4 * rows, 2 * rows), bf16),
            pltpu.VMEM((VAL, 2 * rows), bf16),
            pltpu.VMEM((KEY, 2 * rows), bf16),
        ],
        flops=8e9, vmem=48,
    )
    kv_got = over_core(kv_sib)
    back_own, back_par = call(join_kernel, [((320, rows), bf16)] * 2, q_own, q_par, kv_mine, kv_got)
    back_other = over_chip(back_par)
    back, to1, to2, to3 = call(
        back_kernel,
        [((640, rows), bf16)] + [((384, rows), bf16)] * 3,
        back_own, back_other, unit, factor, wq, wk, wv, flops=1e9,
    )
    got = [over_y(to2, 2), over_y(to1, 1), over_y(to3, 3)]
    (grad_own,) = call(back_own_kernel, [((384, rows), f32)], back, wq, wk, wv, cot, flops=1e9)
    (hg,) = call(hidden_grad_kernel, [((384, rows), bf16)], grad_own, *got)
    hg_sib = over_core(hg)

    parts = []
    for d in (2, 1, 3, 0):
        (part,) = call(
            functools.partial(tap_kernel, d),
            [((576, 384), bf16 if d else f32)],
            taps_mine, taps_sib, hg, hg_sib, flops=6e8,
        )
        parts.append(over_x(part, d) if d else part)
    own_z, z1, z2, z3 = call(
        sum_x_kernel,
        [((144, 384), f32)] + [((144, 384), bf16)] * 3,
        parts[3], parts[0], parts[1], parts[2],
    )
    got = [over_z(z2, 2), over_z(z1, 1), over_z(z3, 3)]
    norm = 1.0 / math.sqrt(rows * 32)
    (total,) = call(functools.partial(sum_z_kernel, norm), [((144, 384), f32)], own_z, *got)
    return total.reshape(3, 48, 384).transpose(1, 0, 2)


def solution(mesh):
    in_specs = (
        P("seq", "section", None),
        P(),
        P(None, None, "tensor"),
        P(None, "tensor"),
        P(None, "tensor"),
        P(None, "tensor"),
        P("tensor", None),
        P("seq", "section", "tensor"),
    )
    out_specs = P(("seq", "section"), None, "tensor")
    return jax.shard_map(body, mesh=mesh, in_specs=in_specs, out_specs=out_specs, check_vma=False)
```

time: 308 us -> 140 us (0.45)
  waiting for transfers between devices: 216 us -> 81.7 us
  matrix products: 52.6 us -> 0 us
  starting transfers between devices: 3.02 us -> 30.4 us
  Pallas kernels: 0 us -> 23.3 us
  between operations: 13.9 us -> 0.27 us
  other arithmetic: 10.7 us -> 0.04 us
  blocking collectives: 7.33 us -> 0 us
    reduce_scatter x3 -> x0, waiting for transfers between devices: 167 us -> none  [the longest x1 87.9 us: body(): lax.psum_scatter(jnp.stack(tap_parts, axis=1), ('seq', 'section'), scatte...]
    ppermute x2 -> x25, waiting for transfers between devices: 0.56 us -> 81.7 us  [the longest x9 34.6 us: over_y(): return lax.ppermute(value, 'tensor', [(i, i ^ d) for i in range(4)])]
    dot_general x26 -> x0, matrix products: 52.6 us -> none  [the longest x3 8.79 us: body(): jnp.dot(windows[offset], conv_weight[offset], preferred_element_type=jnp....]
    all_gather x3 -> x0, waiting for transfers between devices: 47.6 us -> none  [the longest x1 25 us: body(): lax.all_gather(hidden_own, 'tensor', axis=1, tiled=True)]
    ppermute x2 -> x25, starting transfers between devices: 2.59 us -> 30.4 us  [the longest x9 12.7 us: over_y(): return lax.ppermute(value, 'tensor', [(i, i ^ d) for i in range(4)])]
    pallas_call x0 -> x17, Pallas kernels: none -> 23.3 us  [call(): pl.pallas_call(kernel, out_shape=[jax.ShapeDtypeStruct(shape, kind) for s...]
    all_gather x1 -> x0, blocking collectives: 7.33 us -> none  [body(): lax.all_gather(key_bf, 'section', axis=0, tiled=True)]
    another operation x1 -> x0, other arithmetic: 3.34 us -> none  [body(): jnp.stack(tap_parts, axis=1)]
  transfers between devices with their start and end apart: 8 -> 25, of which waited for: 7 -> 17; matrix products, arithmetic and copies ran while one was open for 10% -> 0% of each run, Pallas kernels for 0% -> 13%
where the time goes in v1:
time: 140 us
  waiting for transfers between devices  81.7 us (58%)
  starting transfers between devices  30.4 us (22%)
  Pallas kernels  23.3 us (17%)
  local copies, waits for them, and re-layouts  4.13 us (3%)
    ppermute x9, waiting for transfers between devices, over_y(): return lax.ppermute(value, 'tensor', [(i, i ^ d) for i in range(4)])  34.6 us
    pallas_call x17, Pallas kernels, call(): pl.pallas_call(kernel, out_shape=[jax.ShapeDtypeStruct(shape, kind) for s...  23.3 us
    ppermute x3, waiting for transfers between devices, over_chip(): return lax.ppermute(value, 'section', [(i, i ^ 2) for i in range(4)])  20.9 us
    ppermute x3, waiting for transfers between devices, over_x(): return lax.ppermute(value, flat, [(i, i ^ 2 * d) for i in range(32)])  16.6 us
    ppermute x9, starting transfers between devices, over_y(): return lax.ppermute(value, 'tensor', [(i, i ^ d) for i in range(4)])  12.7 us
    ppermute x3, waiting for transfers between devices, over_z(): return lax.ppermute(value, flat, [(i, i ^ 8 * d) for i in range(32)])  5.95 us
    ppermute x3, starting transfers between devices, over_z(): return lax.ppermute(value, flat, [(i, i ^ 8 * d) for i in range(32)])  4.97 us
    ppermute x3, starting transfers between devices, over_x(): return lax.ppermute(value, flat, [(i, i ^ 2 * d) for i in range(32)])  4.32 us
  transfers between devices with their start and end apart: 25, of which 17 were waited for; matrix products, arithmetic and copies ran while one was open for 0% of the time, Pallas kernels for 13%

profile of v1, /device:TPU:0, one launch (start us, length us, event | category | flops | bytes accessed | tf_op | source)
XLA Modules:
  0.0 139.7 jit_solution(16403599550708126504)
XLA Ops:
  1.0 1.3 collective-permute-start.1
  2.3 3.0 %collective-permute-start = (s32[32,32]{1,0:T(8,128)S(1)}, s32[32,32]{1,0:T(8,128)S(1)}, u32[]{:S(2)}, u32[]{:S(2)}) collective-permute-start(s32[32,32]{1,0:T(8,128)S(1)} %get-tuple-element.54), channel_id=1, source_target_pairs={{0,1},{1,2},{2,3},{4,5},{5,6},{6,7},{8,9},{9,10},{10,11},{12,13},{... | collective-permute-start | bytes 12296 | tf_op jit(solution)/shard_map/ppermute | solution.py:257
  6.4 1.3 shard_map.82.act_ref
  7.7 2.1 %copy-done.5 = bf16[3,1536,384]{2,1,0:T(8,128)(2,1)S(1)} copy-done((bf16[3,1536,384]{2,1,0:T(8,128)(2,1)S(1)}, bf16[3,1536,384]{2,1,0:T(8,128)(2,1)}, u32[]{:S(2)}) %copy-start.5) | copy-done | bytes 3538968
  9.9 3.0 %shard_map.83 = (bf16[512,384]{1,0:T(8,128)(2,1)S(1)}, bf16[576,1536]{1,0:T(8,128)(2,1)S(1)}) custom-call(s32[512,32]{1,0:T(8,128)S(1)} %get-tuple-element.56.marks_ref, s32[32,32]{1,0:T(8,128)S(1)} %collective-permute-done.low_ref, s32[32,32]{1,0:T(8,128)S(1)} %collective-permute-done.1.high_ref, bf16[128,1536]{1,0:T(8,128)(2,1)S(1)} %copy-done.4, ...), custom_call_target="tpu_custom_call" | custom-call | flops 2000000000 | bytes 5578752 | tf_op jit(solution)/shard_map/pallas_call | solution.py:33
  12.9 3.2 %collective-permute-start.5 = (bf16[512,384]{1,0:T(8,128)(2,1)S(1)}, bf16[512,384]{1,0:T(8,128)(2,1)S(1)}, u32[]{:S(2)}, u32[]{:S(2)}) collective-permute-start(bf16[512,384]{1,0:T(8,128)(2,1)S(1)} %get-tuple-element.32.h0), channel_id=1, source_target_pairs={{0,12},{4,8},{8,4},{12,0},{1,13},{5,9},{9,5},{13,1},{2,14},{6,10},... | collective-permute-start | bytes 1179656 | tf_op jit(solution)/shard_map/ppermute | solution.py:261
  17.1 3.1 %collective-permute-start.11 = (bf16[512,384]{1,0:T(8,128)(2,1)S(1)}, bf16[512,384]{1,0:T(8,128)(2,1)S(1)}, u32[]{:S(2)}, u32[]{:S(2)}) collective-permute-start(bf16[512,384]{1,0:T(8,128)(2,1)S(1)} %bitcast.10), channel_id=1, source_target_pairs={{0,12},{4,8},{8,4},{12,0},{1,13},{5,9},{9,5},{13,1},{2,14},{6,10},... | collective-permute-start | bytes 1179656 | tf_op jit(solution)/shard_map/ppermute | solution.py:261
  21.4 12.9 %collective-permute-done.5.h3 = bf16[512,384]{1,0:T(8,128)(2,1)S(1)} collective-permute-done((bf16[512,384]{1,0:T(8,128)(2,1)S(1)}, bf16[512,384]{1,0:T(8,128)(2,1)S(1)}, u32[]{:S(2)}, u32[]{:S(2)}) %collective-permute-start.5) | collective-permute-done | bytes 393248 | tf_op jit(solution)/shard_map/ppermute | solution.py:261
  35.4 1.6 %shard_map.86 = (bf16[320,512]{1,0:T(8,128)(2,1)S(1)}, bf16[320,512]{1,0:T(8,128)(2,1)S(1)}, f32[256,512]{1,0:T(8,128)S(1)}, f32[4,512]{1,0:T(4,128)S(1)}) custom-call(bf16[512,384]{1,0:T(8,128)(2,1)S(1)} %get-tuple-element.32.h0, bf16[512,384]{1,0:T(8,128)(2,1)S(1)} %collective-permute-done.3.h1, bf16[512,384]{1,0:T(8,128)(2,1)S(1)} %collective-permute-done.4.h2, ...), custom_call_target="tpu_custom_call" | custom-call | flops 1500000000 | bytes 3538944 | tf_op jit(solution)/shard_map/pallas_call | solution.py:33
  37.0 3.0 %collective-permute-start.6 = (bf16[320,512]{1,0:T(8,128)(2,1)S(1)}, bf16[320,512]{1,0:T(8,128)(2,1)S(1)}, u32[]{:S(2)}, u32[]{:S(2)}) collective-permute-start(bf16[320,512]{1,0:T(8,128)(2,1)S(1)} %get-tuple-element.34), channel_id=1, source_target_pairs={{0,2},{1,3},{2,0},{3,1},{4,6},{5,7},{6,4},{7,5},{8,10},{9,11},{10,... | collective-permute-start | bytes 983048 | tf_op jit(solution)/shard_map/ppermute | solution.py:267
  40.0 7.0 %collective-permute-done.6.par = bf16[320,512]{1,0:T(8,128)(2,1)S(1)} collective-permute-done((bf16[320,512]{1,0:T(8,128)(2,1)S(1)}, bf16[320,512]{1,0:T(8,128)(2,1)S(1)}, u32[]{:S(2)}, u32[]{:S(2)}) %collective-permute-start.6) | collective-permute-done | bytes 327712 | tf_op jit(solution)/shard_map/ppermute | solution.py:267
  47.0 4.1 %collective-permute-done.11.c3 = bf16[512,384]{1,0:T(8,128)(2,1)S(1)} collective-permute-done((bf16[512,384]{1,0:T(8,128)(2,1)S(1)}, bf16[512,384]{1,0:T(8,128)(2,1)S(1)}, u32[]{:S(2)}, u32[]{:S(2)}) %collective-permute-start.11) | collective-permute-done | bytes 393248 | tf_op jit(solution)/shard_map/ppermute | solution.py:261
  51.2 1.1 collective-permute-done.9.c1
  52.3 1.2 shard_map.87
  53.6 2.1 %shard_map.84 = (bf16[2304,512]{1,0:T(8,128)(2,1)S(1)}, bf16[2304,512]{1,0:T(8,128)(2,1)S(1)}) custom-call(bf16[576,1536]{1,0:T(8,128)(2,1)S(1)} %get-tuple-element.29.ext_ref), custom_call_target="tpu_custom_call" | custom-call | flops 3000000000 | bytes 1769472 | tf_op jit(solution)/shard_map/pallas_call | solution.py:33
  56.1 4.5 %collective-permute-done.12.g_par = bf16[192,512]{1,0:T(8,128)(2,1)S(1)} collective-permute-done((bf16[192,512]{1,0:T(8,128)(2,1)S(1)}, bf16[192,512]{1,0:T(8,128)(2,1)S(1)}, u32[]{:S(2)}, u32[]{:S(2)}) %collective-permute-start.12) | collective-permute-done | bytes 196640 | tf_op jit(solution)/shard_map/ppermute | solution.py:267
  60.6 7.4 %shard_map.88 = (bf16[64,512]{1,0:T(8,128)(2,1)S(1)}, bf16[64,512]{1,0:T(8,128)(2,1)S(1)}, f32[256,1024]{1,0:T(8,128)S(1)}, bf16[256,1024]{1,0:T(8,128)(2,1)S(1)}) custom-call(bf16[320,512]{1,0:T(8,128)(2,1)S(1)} %get-tuple-element.33.own, bf16[320,512]{1,0:T(8,128)(2,1)S(1)} %collective-permute-done.6.par, ...), custom_call_target="tpu_custom_call" | custom-call | flops 8000000000 | bytes 1703936 | tf_op jit(solution)/shard_map/pallas_call | solution.py:33
  68.0 1.9 %collective-permute-done.13.kv_got = bf16[256,1024]{1,0:T(8,128)(2,1)S(1)} collective-permute-done((bf16[256,1024]{1,0:T(8,128)(2,1)S(1)}, bf16[256,1024]{1,0:T(8,128)(2,1)S(1)}, u32[]{:S(2)}, u32[]{:S(2)}) %collective-permute-start.13) | collective-permute-done | bytes 524320 | tf_op jit(solution)/shard_map/ppermute | solution.py:264
  70.4 9.5 %collective-permute-done.14.other = bf16[320,512]{1,0:T(8,128)(2,1)S(1)} collective-permute-done((bf16[320,512]{1,0:T(8,128)(2,1)S(1)}, bf16[320,512]{1,0:T(8,128)(2,1)S(1)}, u32[]{:S(2)}, u32[]{:S(2)}) %collective-permute-start.14) | collective-permute-done | bytes 327712 | tf_op jit(solution)/shard_map/ppermute | solution.py:267
  79.9 1.3 shard_map.90
  81.1 3.2 %collective-permute-start.15 = (bf16[384,512]{1,0:T(8,128)(2,1)S(1)}, bf16[384,512]{1,0:T(8,128)(2,1)S(1)}, u32[]{:S(2)}, u32[]{:S(2)}) collective-permute-start(bf16[384,512]{1,0:T(8,128)(2,1)S(1)} %get-tuple-element.46), channel_id=1, source_target_pairs={{0,8},{4,12},{8,0},{12,4},{1,9},{5,13},{9,1},{13,5},{2,10},{6,14},... | collective-permute-start | bytes 1179656 | tf_op jit(solution)/shard_map/ppermute | solution.py:261
  85.8 9.0 %collective-permute-done.15.r1 = bf16[384,512]{1,0:T(8,128)(2,1)S(1)} collective-permute-done((bf16[384,512]{1,0:T(8,128)(2,1)S(1)}, bf16[384,512]{1,0:T(8,128)(2,1)S(1)}, u32[]{:S(2)}, u32[]{:S(2)}) %collective-permute-start.15) | collective-permute-done | bytes 393248 | tf_op jit(solution)/shard_map/ppermute | solution.py:261
  94.8 7.0 %collective-permute-done.16.r2 = bf16[384,512]{1,0:T(8,128)(2,1)S(1)} collective-permute-done((bf16[384,512]{1,0:T(8,128)(2,1)S(1)}, bf16[384,512]{1,0:T(8,128)(2,1)S(1)}, u32[]{:S(2)}, u32[]{:S(2)}) %collective-permute-start.16) | collective-permute-done | bytes 393248 | tf_op jit(solution)/shard_map/ppermute | solution.py:261
  102.1 1.7 %collective-permute-done.18.g_sib = bf16[384,512]{1,0:T(8,128)(2,1)S(1)} collective-permute-done((bf16[384,512]{1,0:T(8,128)(2,1)S(1)}, bf16[384,512]{1,0:T(8,128)(2,1)S(1)}, u32[]{:S(2)}, u32[]{:S(2)}) %collective-permute-start.18) | collective-permute-done | bytes 393248 | tf_op jit(solution)/shard_map/ppermute | solution.py:264
  104.5 3.0 %collective-permute-start.19 = (bf16[576,384]{1,0:T(8,128)(2,1)S(1)}, bf16[576,384]{1,0:T(8,128)(2,1)S(1)}, u32[]{:S(2)}, u32[]{:S(2)}) collective-permute-start(bf16[576,384]{1,0:T(8,128)(2,1)S(1)} %shard_map.94), channel_id=1, source_target_pairs={{0,16},{1,17},{2,18},{3,19},{16,0},{17,1},{18,2},{19,3},{32,48},{3... | collective-permute-start | bytes 1327112 | tf_op jit(solution)/shard_map/ppermute | solution.py:270
  109.3 1.2 collective-permute-start.21
  111.3 7.9 %collective-permute-done.19.r1 = bf16[576,384]{1,0:T(8,128)(2,1)S(1)} collective-permute-done((bf16[576,384]{1,0:T(8,128)(2,1)S(1)}, bf16[576,384]{1,0:T(8,128)(2,1)S(1)}, u32[]{:S(2)}, u32[]{:S(2)}) %collective-permute-start.19) | collective-permute-done | bytes 442400 | tf_op jit(solution)/shard_map/ppermute | solution.py:270
  119.2 7.8 %collective-permute-done.20.r2 = bf16[576,384]{1,0:T(8,128)(2,1)S(1)} collective-permute-done((bf16[576,384]{1,0:T(8,128)(2,1)S(1)}, bf16[576,384]{1,0:T(8,128)(2,1)S(1)}, u32[]{:S(2)}, u32[]{:S(2)}) %collective-permute-start.20) | collective-permute-done | bytes 442400 | tf_op jit(solution)/shard_map/ppermute | solution.py:270
  128.0 4.0 %collective-permute-start.22 = (bf16[144,384]{1,0:T(8,128)(2,1)S(1)}, bf16[144,384]{1,0:T(8,128)(2,1)S(1)}, u32[]{:S(2)}, u32[]{:S(2)}) collective-permute-start(bf16[144,384]{1,0:T(8,128)(2,1)S(1)} %get-tuple-element.50), channel_id=1, source_target_pairs={{0,64},{1,65},{2,66},{3,67},{16,80},{17,81},{18,82},{19,83},{32,96... | collective-permute-start | bytes 331784 | tf_op jit(solution)/shard_map/ppermute | solution.py:273
  132.0 1.0 collective-permute-start.23
  133.0 2.8 %collective-permute-done.22.r1 = bf16[144,384]{1,0:T(8,128)(2,1)S(1)} collective-permute-done((bf16[144,384]{1,0:T(8,128)(2,1)S(1)}, bf16[144,384]{1,0:T(8,128)(2,1)S(1)}, u32[]{:S(2)}, u32[]{:S(2)}) %collective-permute-start.22) | collective-permute-done | bytes 110624 | tf_op jit(solution)/shard_map/ppermute | solution.py:273
  135.9 2.5 %collective-permute-done.23.r2 = bf16[144,384]{1,0:T(8,128)(2,1)S(1)} collective-permute-done((bf16[144,384]{1,0:T(8,128)(2,1)S(1)}, bf16[144,384]{1,0:T(8,128)(2,1)S(1)}, u32[]{:S(2)}, u32[]{:S(2)}) %collective-permute-start.23) | collective-permute-done | bytes 110624 | tf_op jit(solution)/shard_map/ppermute | solution.py:273
  (52 shorter events, 13.8 us)
Async XLA Ops:
  1.0 6.7 %collective-permute-start.1 = (s32[32,32]{1,0:T(8,128)S(1)}, s32[32,32]{1,0:T(8,128)S(1)}, u32[]{:S(2)}, u32[]{:S(2)}) collective-permute-start(s32[32,32]{1,0:T(8,128)S(1)} %get-tuple-element.53), channel_id=1, source_target_pairs={{1,0},{2,1},{3,2},{5,4},{6,5},{7,6},{9,8},{10,9},{11,10},{13,12},{... | collective-permute-start | bytes 12296 | tf_op jit(solution)/shard_map/ppermute | solution.py:258
  2.3 5.4 %collective-permute-start = (s32[32,32]{1,0:T(8,128)S(1)}, s32[32,32]{1,0:T(8,128)S(1)}, u32[]{:S(2)}, u32[]{:S(2)}) collective-permute-start(s32[32,32]{1,0:T(8,128)S(1)} %get-tuple-element.54), channel_id=1, source_target_pairs={{0,1},{1,2},{2,3},{4,5},{5,6},{6,7},{8,9},{9,10},{10,11},{12,13},{... | collective-permute-start | bytes 12296 | tf_op jit(solution)/shard_map/ppermute | solution.py:257
  5.4 1.0 copy-start.4
  7.6 9.4 %copy-start.3 = (bf16[1,512,384]{2,1,0:T(8,128)(2,1)S(1)}, bf16[1,512,384]{2,1,0:T(8,128)(2,1)}, u32[]{:S(2)}) copy-start(bf16[1,512,384]{2,1,0:T(8,128)(2,1)} %param.15) | copy-start | bytes 1179652
  7.6 13.2 %copy-start = (bf16[1536,384]{1,0:T(8,128)(2,1)S(1)}, bf16[1536,384]{1,0:T(8,128)(2,1)}, u32[]{:S(2)}) copy-start(bf16[1536,384]{1,0:T(8,128)(2,1)} %wv.3) | copy-start | bytes 3538948
  7.7 13.2 %copy-start.1 = (bf16[1536,128]{1,0:T(8,128)(2,1)S(1)}, bf16[1536,128]{1,0:T(8,128)(2,1)}, u32[]{:S(2)}) copy-start(bf16[1536,128]{1,0:T(8,128)(2,1)} %wq.3) | copy-start | bytes 1179652
  7.7 13.1 %copy-start.2 = (bf16[1536,128]{1,0:T(8,128)(2,1)S(1)}, bf16[1536,128]{1,0:T(8,128)(2,1)}, u32[]{:S(2)}) copy-start(bf16[1536,128]{1,0:T(8,128)(2,1)} %wk.3) | copy-start | bytes 1179652
  7.7 2.2 %copy-start.5 = (bf16[3,1536,384]{2,1,0:T(8,128)(2,1)S(1)}, bf16[3,1536,384]{2,1,0:T(8,128)(2,1)}, u32[]{:S(2)}) copy-start(bf16[3,1536,384]{2,1,0:T(8,128)(2,1)} %weight_ref.3) | copy-start | bytes 10616836
  12.9 21.4 %collective-permute-start.5 = (bf16[512,384]{1,0:T(8,128)(2,1)S(1)}, bf16[512,384]{1,0:T(8,128)(2,1)S(1)}, u32[]{:S(2)}, u32[]{:S(2)}) collective-permute-start(bf16[512,384]{1,0:T(8,128)(2,1)S(1)} %get-tuple-element.32.h0), channel_id=1, source_target_pairs={{0,12},{4,8},{8,4},{12,0},{1,13},{5,9},{9,5},{13,1},{2,14},{6,10},... | collective-permute-start | bytes 1179656 | tf_op jit(solution)/shard_map/ppermute | solution.py:261
  16.1 18.8 %collective-permute-start.4 = (bf16[512,384]{1,0:T(8,128)(2,1)S(1)}, bf16[512,384]{1,0:T(8,128)(2,1)S(1)}, u32[]{:S(2)}, u32[]{:S(2)}) collective-permute-start(bf16[512,384]{1,0:T(8,128)(2,1)S(1)} %get-tuple-element.32.h0), channel_id=1, source_target_pairs={{0,8},{4,12},{8,0},{12,4},{1,9},{5,13},{9,1},{13,5},{2,10},{6,14},... | collective-permute-start | bytes 1179656 | tf_op jit(solution)/shard_map/ppermute | solution.py:261
  16.7 18.7 %collective-permute-start.3 = (bf16[512,384]{1,0:T(8,128)(2,1)S(1)}, bf16[512,384]{1,0:T(8,128)(2,1)S(1)}, u32[]{:S(2)}, u32[]{:S(2)}) collective-permute-start(bf16[512,384]{1,0:T(8,128)(2,1)S(1)} %get-tuple-element.32.h0), channel_id=1, source_target_pairs={{0,4},{4,0},{8,12},{12,8},{1,5},{5,1},{9,13},{13,9},{2,6},{6,2},{1... | collective-permute-start | bytes 1179656 | tf_op jit(solution)/shard_map/ppermute | solution.py:261
  17.1 34.1 %collective-permute-start.11 = (bf16[512,384]{1,0:T(8,128)(2,1)S(1)}, bf16[512,384]{1,0:T(8,128)(2,1)S(1)}, u32[]{:S(2)}, u32[]{:S(2)}) collective-permute-start(bf16[512,384]{1,0:T(8,128)(2,1)S(1)} %bitcast.10), channel_id=1, source_target_pairs={{0,12},{4,8},{8,4},{12,0},{1,13},{5,9},{9,5},{13,1},{2,14},{6,10},... | collective-permute-start | bytes 1179656 | tf_op jit(solution)/shard_map/ppermute | solution.py:261
  20.2 31.0 %collective-permute-start.10 = (bf16[512,384]{1,0:T(8,128)(2,1)S(1)}, bf16[512,384]{1,0:T(8,128)(2,1)S(1)}, u32[]{:S(2)}, u32[]{:S(2)}) collective-permute-start(bf16[512,384]{1,0:T(8,128)(2,1)S(1)} %bitcast.11), channel_id=1, source_target_pairs={{0,8},{4,12},{8,0},{12,4},{1,9},{5,13},{9,1},{13,5},{2,10},{6,14},... | collective-permute-start | bytes 1179656 | tf_op jit(solution)/shard_map/ppermute | solution.py:261
  21.4 30.9 %copy-start.6 = (bf16[384,1536]{1,0:T(8,128)(2,1)S(1)}, bf16[384,1536]{1,0:T(8,128)(2,1)}, u32[]{:S(2)}) copy-start(bf16[384,1536]{1,0:T(8,128)(2,1)} %w_ref.1) | copy-start | bytes 3538948
  34.3 18.0 %collective-permute-start.9 = (bf16[512,384]{1,0:T(8,128)(2,1)S(1)}, bf16[512,384]{1,0:T(8,128)(2,1)S(1)}, u32[]{:S(2)}, u32[]{:S(2)}) collective-permute-start(bf16[512,384]{1,0:T(8,128)(2,1)S(1)} %bitcast.12), channel_id=1, source_target_pairs={{0,4},{4,0},{8,12},{12,8},{1,5},{5,1},{9,13},{13,9},{2,6},{6,2},{1... | collective-permute-start | bytes 1179656 | tf_op jit(solution)/shard_map/ppermute | solution.py:261
  37.0 10.0 %collective-permute-start.6 = (bf16[320,512]{1,0:T(8,128)(2,1)S(1)}, bf16[320,512]{1,0:T(8,128)(2,1)S(1)}, u32[]{:S(2)}, u32[]{:S(2)}) collective-permute-start(bf16[320,512]{1,0:T(8,128)(2,1)S(1)} %get-tuple-element.34), channel_id=1, source_target_pairs={{0,2},{1,3},{2,0},{3,1},{4,6},{5,7},{6,4},{7,5},{8,10},{9,11},{10,... | collective-permute-start | bytes 983048 | tf_op jit(solution)/shard_map/ppermute | solution.py:267
  40.0 20.6 %collective-permute-start.7 = (bf16[320,512]{1,0:T(8,128)(2,1)S(1)}, bf16[320,512]{1,0:T(8,128)(2,1)S(1)}, u32[]{:S(2)}, u32[]{:S(2)}) collective-permute-start(bf16[320,512]{1,0:T(8,128)(2,1)S(1)} %get-tuple-element.33.own), channel_id=1, source_target_pairs={{0,1},{1,0},{2,3},{3,2},{4,5},{5,4},{6,7},{7,6},{8,9},{9,8},{10,11... | collective-permute-start | bytes 983048 | tf_op jit(solution)/shard_map/ppermute | solution.py:264
  47.0 13.5 %collective-permute-start.8 = (bf16[320,512]{1,0:T(8,128)(2,1)S(1)}, bf16[320,512]{1,0:T(8,128)(2,1)S(1)}, u32[]{:S(2)}, u32[]{:S(2)}) collective-permute-start(bf16[320,512]{1,0:T(8,128)(2,1)S(1)} %collective-permute-done.6.par), channel_id=1, source_target_pairs={{0,1},{1,0},{2,3},{3,2},{4,5},{5,4},{6,7},{7,6},{8,9},{9,8},{10,11... | collective-permute-start | bytes 983048 | tf_op jit(solution)/shard_map/ppermute | solution.py:264
  53.6 7.0 %collective-permute-start.12 = (bf16[192,512]{1,0:T(8,128)(2,1)S(1)}, bf16[192,512]{1,0:T(8,128)(2,1)S(1)}, u32[]{:S(2)}, u32[]{:S(2)}) collective-permute-start(bf16[192,512]{1,0:T(8,128)(2,1)S(1)} %get-tuple-element.36), channel_id=1, source_target_pairs={{0,2},{1,3},{2,0},{3,1},{4,6},{5,7},{6,4},{7,5},{8,10},{9,11},{10,... | collective-permute-start | bytes 589832 | tf_op jit(solution)/shard_map/ppermute | solution.py:267
  55.7 46.3 %collective-permute-start.2 = (bf16[2304,512]{1,0:T(8,128)(2,1)S(1)}, bf16[2304,512]{1,0:T(8,128)(2,1)S(1)}, u32[]{:S(2)}, u32[]{:S(2)}) collective-permute-start(bf16[2304,512]{1,0:T(8,128)(2,1)S(1)} %get-tuple-element.31), channel_id=1, source_target_pairs={{0,1},{1,0},{2,3},{3,2},{4,5},{5,4},{6,7},{7,6},{8,9},{9,8},{10,11... | collective-permute-start | bytes 7077896 | tf_op jit(solution)/shard_map/ppermute | solution.py:264
  67.9 2.0 %collective-permute-start.13 = (bf16[256,1024]{1,0:T(8,128)(2,1)S(1)}, bf16[256,1024]{1,0:T(8,128)(2,1)S(1)}, u32[]{:S(2)}, u32[]{:S(2)}) collective-permute-start(bf16[256,1024]{1,0:T(8,128)(2,1)S(1)} %get-tuple-element.40), channel_id=1, source_target_pairs={{0,1},{1,0},{2,3},{3,2},{4,5},{5,4},{6,7},{7,6},{8,9},{9,8},{10,11... | collective-permute-start | bytes 1572872 | tf_op jit(solution)/shard_map/ppermute | solution.py:264
  70.0 9.8 %collective-permute-start.14 = (bf16[320,512]{1,0:T(8,128)(2,1)S(1)}, bf16[320,512]{1,0:T(8,128)(2,1)S(1)}, u32[]{:S(2)}, u32[]{:S(2)}) collective-permute-start(bf16[320,512]{1,0:T(8,128)(2,1)S(1)} %get-tuple-element.42), channel_id=1, source_target_pairs={{0,2},{1,3},{2,0},{3,1},{4,6},{5,7},{6,4},{7,5},{8,10},{9,11},{10,... | collective-permute-start | bytes 983048 | tf_op jit(solution)/shard_map/ppermute | solution.py:267
  81.1 13.7 %collective-permute-start.15 = (bf16[384,512]{1,0:T(8,128)(2,1)S(1)}, bf16[384,512]{1,0:T(8,128)(2,1)S(1)}, u32[]{:S(2)}, u32[]{:S(2)}) collective-permute-start(bf16[384,512]{1,0:T(8,128)(2,1)S(1)} %get-tuple-element.46), channel_id=1, source_target_pairs={{0,8},{4,12},{8,0},{12,4},{1,9},{5,13},{9,1},{13,5},{2,10},{6,14},... | collective-permute-start | bytes 1179656 | tf_op jit(solution)/shard_map/ppermute | solution.py:261
  84.3 17.5 %collective-permute-start.16 = (bf16[384,512]{1,0:T(8,128)(2,1)S(1)}, bf16[384,512]{1,0:T(8,128)(2,1)S(1)}, u32[]{:S(2)}, u32[]{:S(2)}) collective-permute-start(bf16[384,512]{1,0:T(8,128)(2,1)S(1)} %get-tuple-element.47), channel_id=1, source_target_pairs={{0,4},{4,0},{8,12},{12,8},{1,5},{5,1},{9,13},{13,9},{2,6},{6,2},{1... | collective-permute-start | bytes 1179656 | tf_op jit(solution)/shard_map/ppermute | solution.py:261
  85.0 16.8 %collective-permute-start.17 = (bf16[384,512]{1,0:T(8,128)(2,1)S(1)}, bf16[384,512]{1,0:T(8,128)(2,1)S(1)}, u32[]{:S(2)}, u32[]{:S(2)}) collective-permute-start(bf16[384,512]{1,0:T(8,128)(2,1)S(1)} %get-tuple-element.48), channel_id=1, source_target_pairs={{0,12},{4,8},{8,4},{12,0},{1,13},{5,9},{9,5},{13,1},{2,14},{6,10},... | collective-permute-start | bytes 1179656 | tf_op jit(solution)/shard_map/ppermute | solution.py:261
  102.0 1.8 %collective-permute-start.18 = (bf16[384,512]{1,0:T(8,128)(2,1)S(1)}, bf16[384,512]{1,0:T(8,128)(2,1)S(1)}, u32[]{:S(2)}, u32[]{:S(2)}) collective-permute-start(bf16[384,512]{1,0:T(8,128)(2,1)S(1)} %shard_map.92.g_mine), channel_id=1, source_target_pairs={{0,1},{1,0},{2,3},{3,2},{4,5},{5,4},{6,7},{7,6},{8,9},{9,8},{10,11... | collective-permute-start | bytes 1179656 | tf_op jit(solution)/shard_map/ppermute | solution.py:264
  104.5 14.6 %collective-permute-start.19 = (bf16[576,384]{1,0:T(8,128)(2,1)S(1)}, bf16[576,384]{1,0:T(8,128)(2,1)S(1)}, u32[]{:S(2)}, u32[]{:S(2)}) collective-permute-start(bf16[576,384]{1,0:T(8,128)(2,1)S(1)} %shard_map.94), channel_id=1, source_target_pairs={{0,16},{1,17},{2,18},{3,19},{16,0},{17,1},{18,2},{19,3},{32,48},{3... | collective-permute-start | bytes 1327112 | tf_op jit(solution)/shard_map/ppermute | solution.py:270
  108.4 18.6 %collective-permute-start.20 = (bf16[576,384]{1,0:T(8,128)(2,1)S(1)}, bf16[576,384]{1,0:T(8,128)(2,1)S(1)}, u32[]{:S(2)}, u32[]{:S(2)}) collective-permute-start(bf16[576,384]{1,0:T(8,128)(2,1)S(1)} %shard_map.95), channel_id=1, source_target_pairs={{0,2},{1,3},{2,0},{3,1},{16,18},{17,19},{18,16},{19,17},{32,34},{3... | collective-permute-start | bytes 1327112 | tf_op jit(solution)/shard_map/ppermute | solution.py:270
  109.3 18.6 %collective-permute-start.21 = (bf16[576,384]{1,0:T(8,128)(2,1)S(1)}, bf16[576,384]{1,0:T(8,128)(2,1)S(1)}, u32[]{:S(2)}, u32[]{:S(2)}) collective-permute-start(bf16[576,384]{1,0:T(8,128)(2,1)S(1)} %shard_map.96), channel_id=1, source_target_pairs={{0,18},{1,19},{2,16},{3,17},{16,2},{17,3},{18,0},{19,1},{32,50},{3... | collective-permute-start | bytes 1327112 | tf_op jit(solution)/shard_map/ppermute | solution.py:270
  128.0 7.8 %collective-permute-start.22 = (bf16[144,384]{1,0:T(8,128)(2,1)S(1)}, bf16[144,384]{1,0:T(8,128)(2,1)S(1)}, u32[]{:S(2)}, u32[]{:S(2)}) collective-permute-start(bf16[144,384]{1,0:T(8,128)(2,1)S(1)} %get-tuple-element.50), channel_id=1, source_target_pairs={{0,64},{1,65},{2,66},{3,67},{16,80},{17,81},{18,82},{19,83},{32,96... | collective-permute-start | bytes 331784 | tf_op jit(solution)/shard_map/ppermute | solution.py:273
  132.0 6.3 %collective-permute-start.23 = (bf16[144,384]{1,0:T(8,128)(2,1)S(1)}, bf16[144,384]{1,0:T(8,128)(2,1)S(1)}, u32[]{:S(2)}, u32[]{:S(2)}) collective-permute-start(bf16[144,384]{1,0:T(8,128)(2,1)S(1)} %get-tuple-element.51), channel_id=1, source_target_pairs={{0,32},{1,33},{2,34},{3,35},{16,48},{17,49},{18,50},{19,51},{32,0}... | collective-permute-start | bytes 331784 | tf_op jit(solution)/shard_map/ppermute | solution.py:273
  133.0 6.0 %collective-permute-start.24 = (bf16[144,384]{1,0:T(8,128)(2,1)S(1)}, bf16[144,384]{1,0:T(8,128)(2,1)S(1)}, u32[]{:S(2)}, u32[]{:S(2)}) collective-permute-start(bf16[144,384]{1,0:T(8,128)(2,1)S(1)} %get-tuple-element.52), channel_id=1, source_target_pairs={{0,96},{1,97},{2,98},{3,99},{16,112},{17,113},{18,114},{19,115},{3... | collective-permute-start | bytes 331784 | tf_op jit(solution)/shard_map/ppermute | solution.py:273

commit v2 on v1

--- a/solution.py
+++ b/solution.py
@@ -71,7 +71,7 @@
         act_ref[:, j : j + 256] = gelu(nn(hot, weight_ref[:, j : j + 256])).astype(bf16)
 
 
-def conv_kernel(marks_ref, low_ref, high_ref, stem_ref, act_ref, weight_ref, hidden_ref, ext_ref):
+def conv_kernel(marks_ref, low_ref, high_ref, stem_ref, act_ref, weight_ref, lo_ref, hi_ref, ext_ref):
     rows = act_ref.shape[0]
     width = weight_ref.shape[2]
     edge = jnp.concatenate([low_ref[...], high_ref[...]], axis=0)
@@ -84,7 +84,8 @@
     total = nn(one_hot(marks_ref[...]), own)
     for k in range(3):
         total = total + nn(ext_ref[k * HALO : k * HALO + rows], weight_ref[k])
-    hidden_ref[...] = total.astype(bf16)
+    lo_ref[...] = total[: rows // 2].astype(bf16)
+    hi_ref[...] = total[rows // 2 :].astype(bf16)
 
 
 def turn_kernel(q_ref, k_ref, v_ref, out_ref):
@@ -108,32 +109,45 @@
                 ]
 
 
-def project_kernel(h0, h1, h2, h3, w_ref, mine_ref, other_ref, unit_ref, factor_ref, values):
+def gathered(blocks):
+    lo, hi, lo1, hi1, lo3, hi3, lo2, hi2 = blocks
+    return ((0, lo), (1, lo1), (3, lo3), (2, lo2)), ((0, hi), (1, hi1), (3, hi3), (2, hi2))
+
+
+def project_kernel(*refs):
+    w_ref, mine_ref, other_ref, unit_ref, factor_ref, values = refs[8:]
     y = lax.axis_index("tensor")
     chip, _ = own_chip()
-    total = nt(w_ref[:, block_at(y, 384)], h0[...])
-    for d, ref in ((1, h1), (2, h2), (3, h3)):
-        total = total + nt(w_ref[:, block_at(y ^ d, 384)], ref[...])
-    for g in range(4):
-        raw = total[g * KEY : (g + 1) * KEY]
-        factor = lax.rsqrt(jnp.mean(raw * raw, axis=0, keepdims=True) + EPSILON)
-        unit_ref[g * KEY : (g + 1) * KEY] = raw * factor
-        factor_ref[g : g + 1] = factor
-    values[...] = total[256:].astype(bf16)
+    for half, blocks in enumerate(gathered(refs[:8])):
+        half_rows = blocks[0][1].shape[0]
+        at = slice(half * half_rows, (half + 1) * half_rows)
+        total = 0.0
+        for d, ref in blocks:
+            total = total + nt(w_ref[:, block_at(y ^ d, 384)], ref[...])
+        for g in range(4):
+            raw = total[g * KEY : (g + 1) * KEY]
+            factor = lax.rsqrt(jnp.mean(raw * raw, axis=0, keepdims=True) + EPSILON)
+            unit_ref[g * KEY : (g + 1) * KEY, at] = raw * factor
+            factor_ref[g : g + 1, at] = factor
+        values[:, at] = total[256:].astype(bf16)
     for ref, head in ((mine_ref, chip), (other_ref, 1 - chip)):
         ref[0:64] = unit_ref[block_at(head, KEY)].astype(bf16)
         ref[64:128] = unit_ref[pl.ds(pl.multiple_of(128 + head * KEY, KEY), KEY)].astype(bf16)
         ref[128:320] = values[block_at(head, VAL)]
 
 
-def grad_kernel(c0, c1, c2, c3, w_ref, mine_ref, other_ref):
+def grad_kernel(*refs):
+    w_ref, mine_ref, other_ref = refs[8:]
     y = lax.axis_index("tensor")
     chip, _ = own_chip()
-    for ref, head in ((mine_ref, chip), (other_ref, 1 - chip)):
-        total = nt(w_ref[block_at(head, VAL), block_at(y, 384)], c0[...])
-        for d, c in ((1, c1), (2, c2), (3, c3)):
-            total = total + nt(w_ref[block_at(head, VAL), block_at(y ^ d, 384)], c[...])
-        ref[...] = total.astype(bf16)
+    for half, blocks in enumerate(gathered(refs[:8])):
+        half_rows = blocks[0][1].shape[0]
+        at = slice(half * half_rows, (half + 1) * half_rows)
+        for ref, head in ((mine_ref, chip), (other_ref, 1 - chip)):
+            total = 0.0
+            for d, block in blocks:
+                total = total + nt(w_ref[block_at(head, VAL), block_at(y ^ d, 384)], block[...])
+            ref[:, at] = total.astype(bf16)
 
 
 def attend_kernel(
@@ -188,7 +202,7 @@
     own_ref[64:320] = (kv_mine[:, :n] + kv_got[:, :n].astype(f32)).astype(bf16)
 
 
-def back_kernel(own, other, unit_ref, factor_ref, wq, wk, wv, back, to1, to2, to3):
+def back_kernel(own, other, unit_ref, factor_ref, wq, wk, wv, back, to_a, to_b):
     y = lax.axis_index("tensor")
     chip, _ = own_chip()
     for ref, head in ((own, chip), (other, 1 - chip)):
@@ -200,25 +214,39 @@
             mean = jnp.mean(g * unit, axis=0, keepdims=True)
             back[at] = (factor * (g - unit * mean)).astype(bf16)
         back[pl.ds(pl.multiple_of(256 + head * VAL, 64), VAL)] = ref[128:320]
-    for d, ref in ((2, to2), (1, to1), (3, to3)):
-        ref[...] = back_rows(back, wq, wk, wv, y ^ d).astype(bf16)
-
-
-def back_rows(back, wq, wk, wv, index):
-    at = block_at(index, 384)
+    for half, ref in enumerate((to_a, to_b)):
+        ref[...] = back_rows(back, wq, wk, wv, (y ^ 2) * 2 + half, 192).astype(bf16)
+
+
+def back_rows(back, wq, wk, wv, index, width):
+    at = block_at(index, width)
     qk = jnp.concatenate([wq[at], wk[at]], axis=1)
     return nn(qk, back[0:256]) + nn(wv[at], back[256:640])
 
 
-def back_own_kernel(back, wq, wk, wv, cot, out_ref):
+def back_near_kernel(back, wq, wk, wv, near1_a, near1_b, near3_a, near3_b):
     y = lax.axis_index("tensor")
-    out_ref[...] = back_rows(back, wq, wk, wv, y) + cot[...].astype(f32).T
-
-
-def hidden_grad_kernel(own, r1, r2, r3, out_ref):
-    out_ref[...] = (
-        own[...] + r1[...].astype(f32) + r2[...].astype(f32) + r3[...].astype(f32)
-    ).astype(bf16)
+    for d, half, ref in ((1, 0, near1_a), (3, 1, near3_b), (3, 0, near3_a), (1, 1, near1_b)):
+        ref[...] = back_rows(back, wq, wk, wv, (y ^ d) * 2 + half, 192).astype(ref.dtype)
+
+
+def back_own_kernel(back, wq, wk, wv, cot_lo, cot_hi, out_ref):
+    y = lax.axis_index("tensor")
+    half = cot_lo.shape[0]
+    total = back_rows(back, wq, wk, wv, y, 384)
+    out_ref[:, :half] = total[:, :half] + cot_lo[...].astype(f32).T
+    out_ref[:, half:] = total[:, half:] + cot_hi[...].astype(f32).T
+
+
+def add_kernel(near3_a, got_a, near1_b, got_b, out_a, out_b):
+    out_a[...] = (near3_a[...] + got_a[...].astype(f32)).astype(bf16)
+    out_b[...] = (near1_b[...] + got_b[...].astype(f32)).astype(bf16)
+
+
+def hidden_grad_kernel(own, got1_a, got3_b, got3_a, got1_b, out_ref):
+    half = got1_a.shape[0]
+    for at, left, right in ((slice(0, half), got1_a, got3_a), (slice(half, 2 * half), got1_b, got3_b)):
+        out_ref[at] = (own[at] + left[...].astype(f32) + right[...].astype(f32)).astype(bf16)
 
 
 def ring_place():
@@ -227,19 +255,20 @@
     return x, z
 
 
-def tap_kernel(d, t_mine, t_sib, g_mine, g_sib, out_ref):
+def tap_kernel(pieces, t_mine, t_sib, g_mine, g_sib, *outs):
     x, _ = ring_place()
-    at = block_at(x ^ d, 576)
-    out_ref[...] = (nt(t_mine[at], g_mine[...]) + nt(t_sib[at], g_sib[...])).astype(out_ref.dtype)
-
-
-def sum_x_kernel(own, r1, r2, r3, own_ref, to1, to2, to3):
+    for (d, start, size), out_ref in zip(pieces, outs):
+        at = pl.ds(pl.multiple_of((x ^ d) * 576 + start, 288), size)
+        out_ref[...] = (nt(t_mine[at], g_mine[...]) + nt(t_sib[at], g_sib[...])).astype(out_ref.dtype)
+
+
+def sum_x_kernel(own, got1_a, got3_b, got3_a, got1_b, own_ref, to1, to2, to3, total):
     _, z = ring_place()
+    half = got1_a.shape[0]
+    for at, left, right in ((slice(0, half), got1_a, got3_a), (slice(half, 2 * half), got1_b, got3_b)):
+        total[at] = own[at] + left[...].astype(f32) + right[...].astype(f32)
     for d, ref in ((2, to2), (1, to1), (3, to3), (0, own_ref)):
-        at = block_at(z ^ d, 144)
-        ref[...] = (
-            own[at] + r1[at].astype(f32) + r2[at].astype(f32) + r3[at].astype(f32)
-        ).astype(ref.dtype)
+        ref[...] = total[block_at(z ^ d, 144)].astype(ref.dtype)
 
 
 def sum_z_kernel(norm, own, r1, r2, r3, out_ref):
@@ -272,26 +301,36 @@
     def over_z(value, d):
         return lax.ppermute(value, flat, [(i, i ^ (8 * d)) for i in range(32)])
 
-    cots = [cot] + [over_y(cot, d) for d in (1, 2, 3)]
+    def ring_gather(lo, hi, over):
+        lo1, hi3 = over(lo, 1), over(hi, 3)
+        hi1, lo3 = over(hi, 1), over(lo, 3)
+        hi2, lo2 = over(hi3, 1), over(lo1, 3)
+        return [lo, hi, lo1, hi1, lo3, hi3, lo2, hi2]
+
+    cots = ring_gather(cot[: rows // 2], cot[rows // 2 :], over_y)
 
     (act,) = call(stem_kernel, [((rows, 1536), bf16)], marks, stem_w, flops=4e8)
-    hidden, ext = call(
+    low, high, act, cots[2], cots[5] = lax.optimization_barrier((low, high, act, cots[2], cots[5]))
+    hidden_lo, hidden_hi, ext = call(
         conv_kernel,
-        [((rows, 384), bf16), ((rows + 2 * HALO, 1536), bf16)],
+        [((rows // 2, 384), bf16)] * 2 + [((rows + 2 * HALO, 1536), bf16)],
         marks, low, high, stem_w, act, conv_w,
         flops=2e9,
     )
-    hiddens = [hidden] + [over_y(hidden, d) for d in (1, 2, 3)]
+    hidden_lo, hidden_hi, cots = lax.optimization_barrier((hidden_lo, hidden_hi, cots))
+    hiddens = ring_gather(hidden_lo, hidden_hi, over_y)
 
     (w_t,) = call(turn_kernel, [((640, 1536), bf16)], wq, wk, wv, flops=1e9)
     taps_mine, taps_other = call(
         taps_kernel, [((2304, rows), bf16)] * 2, ext,
         scratch=[pltpu.VMEM((1536, rows), bf16)], flops=3e9,
     )
-    taps_sib = over_core(taps_other)
 
     g_own, g_other = call(grad_kernel, [((VAL, rows), bf16)] * 2, *cots, out_w, flops=1e9)
     g_par = over_chip(g_other)
+    hiddens, g_par, g_own, taps_mine, taps_other, w_t = lax.optimization_barrier(
+        (hiddens, g_par, g_own, taps_mine, taps_other, w_t)
+    )
 
     own, other, unit, factor = call(
         project_kernel,
@@ -302,6 +341,7 @@
     par = over_chip(other)
     sib_own = over_core(own)
     sib_par = over_core(par)
+    taps_sib = over_core(taps_other)
     q_own, q_par, kv_mine, kv_sib = call(
         attend_kernel,
         [((KEY, rows), bf16)] * 2 + [((256, 2 * rows), f32), ((256, 2 * rows), bf16)],
@@ -319,28 +359,44 @@
     kv_got = over_core(kv_sib)
     back_own, back_par = call(join_kernel, [((320, rows), bf16)] * 2, q_own, q_par, kv_mine, kv_got)
     back_other = over_chip(back_par)
-    back, to1, to2, to3 = call(
+    back, far_a, far_b = call(
         back_kernel,
-        [((640, rows), bf16)] + [((384, rows), bf16)] * 3,
-        back_own, back_other, unit, factor, wq, wk, wv, flops=1e9,
-    )
-    got = [over_y(to2, 2), over_y(to1, 1), over_y(to3, 3)]
-    (grad_own,) = call(back_own_kernel, [((384, rows), f32)], back, wq, wk, wv, cot, flops=1e9)
-    (hg,) = call(hidden_grad_kernel, [((384, rows), bf16)], grad_own, *got)
+        [((640, rows), bf16)] + [((192, rows), bf16)] * 2,
+        back_own, back_other, unit, factor, wq, wk, wv, flops=5e8,
+    )
+    got_a, got_b = over_y(far_a, 1), over_y(far_b, 3)
+    near1_a, near1_b, near3_a, near3_b = call(
+        back_near_kernel,
+        [((192, rows), kind) for kind in (bf16, f32, f32, bf16)],
+        back, wq, wk, wv, flops=8e8,
+    )
+    got1_a, got3_b = over_y(near1_a, 1), over_y(near3_b, 3)
+    (grad_own,) = call(back_own_kernel, [((384, rows), f32)], back, wq, wk, wv, cots[0], cots[1], flops=5e8)
+    sum_a, sum_b = call(add_kernel, [((192, rows), bf16)] * 2, near3_a, got_a, near1_b, got_b)
+    got3_a, got1_b = over_y(sum_a, 3), over_y(sum_b, 1)
+    (hg,) = call(hidden_grad_kernel, [((384, rows), bf16)], grad_own, got1_a, got3_b, got3_a, got1_b)
     hg_sib = over_core(hg)
 
-    parts = []
-    for d in (2, 1, 3, 0):
-        (part,) = call(
-            functools.partial(tap_kernel, d),
-            [((576, 384), bf16 if d else f32)],
+    def taps(*pieces):
+        return call(
+            functools.partial(tap_kernel, [p[:3] for p in pieces]),
+            [((p[2], 384), p[3]) for p in pieces],
             taps_mine, taps_sib, hg, hg_sib, flops=6e8,
         )
-        parts.append(over_x(part, d) if d else part)
+
+    far_a, far_b = taps((2, 0, 288, bf16), (2, 288, 288, bf16))
+    got_a, got_b = over_x(far_a, 1), over_x(far_b, 3)
+    near1_a, near3_b = taps((1, 0, 288, bf16), (3, 288, 288, bf16))
+    got1_a, got3_b = over_x(near1_a, 1), over_x(near3_b, 3)
+    near3_a, near1_b = taps((3, 0, 288, f32), (1, 288, 288, f32))
+    (part,) = taps((0, 0, 576, f32))
+    sum_a, sum_b = call(add_kernel, [((288, 384), bf16)] * 2, near3_a, got_a, near1_b, got_b)
+    got3_a, got1_b = over_x(sum_a, 3), over_x(sum_b, 1)
     own_z, z1, z2, z3 = call(
         sum_x_kernel,
         [((144, 384), f32)] + [((144, 384), bf16)] * 3,
-        parts[3], parts[0], parts[1], parts[2],
+        part, got1_a, got3_b, got3_a, got1_b,
+        scratch=[pltpu.VMEM((576, 384), f32)],
     )
     got = [over_z(z2, 2), over_z(z1, 1), over_z(z3, 3)]
     norm = 1.0 / math.sqrt(rows * 32)

time: 140 us -> 122 us (0.87)
  waiting for transfers between devices: 81.7 us -> 49.1 us
  starting transfers between devices: 30.4 us -> 44.7 us
    ppermute x9 -> x18, waiting for transfers between devices: 34.6 us -> 12.5 us  [over_y(): return lax.ppermute(value, 'tensor', [(i, i ^ d) for i in range(4)])]
    ppermute x9 -> x18, starting transfers between devices: 12.7 us -> 21.7 us  [over_y(): return lax.ppermute(value, 'tensor', [(i, i ^ d) for i in range(4)])]
    ppermute x3 -> x6, waiting for transfers between devices: 16.6 us -> 9.85 us  [over_x(): return lax.ppermute(value, flat, [(i, i ^ 2 * d) for i in range(32)])]
    ppermute x3, waiting for transfers between devices: 20.9 us -> 16.2 us  [over_chip(): return lax.ppermute(value, 'section', [(i, i ^ 2) for i in range(4)])]
    ppermute x3 -> x6, starting transfers between devices: 4.32 us -> 7.99 us  [over_x(): return lax.ppermute(value, flat, [(i, i ^ 2 * d) for i in range(32)])]
    ppermute x3, starting transfers between devices: 3.44 us -> 6.68 us  [over_chip(): return lax.ppermute(value, 'section', [(i, i ^ 2) for i in range(4)])]
    ppermute x1, starting transfers between devices: 3.03 us -> 1.29 us  [body(): lax.ppermute(marks[rows - HALO:], 'section', [(i, i + 1) for i in range(3)])]
    unnamed x15 -> x13, local copies, waits for them, and re-layouts: 4.13 us -> 3.12 us
  transfers between devices with their start and end apart: 25 -> 37, of which waited for: 17 -> 18; matrix products, arithmetic and copies ran while one was open for 0% -> 1% of each run, Pallas kernels for 13% -> 16%
where the time goes in v2:
time: 122 us
  waiting for transfers between devices  49.1 us (40%)
  starting transfers between devices  44.7 us (37%)
  Pallas kernels  23.5 us (19%)
  local copies, waits for them, and re-layouts  4.23 us (3%)
    pallas_call x20, Pallas kernels, call(): pl.pallas_call(kernel, out_shape=[jax.ShapeDtypeStruct(shape, kind) for s...  23.5 us
    ppermute x18, starting transfers between devices, over_y(): return lax.ppermute(value, 'tensor', [(i, i ^ d) for i in range(4)])  21.7 us
    ppermute x3, waiting for transfers between devices, over_chip(): return lax.ppermute(value, 'section', [(i, i ^ 2) for i in range(4)])  16.2 us
    ppermute x18, waiting for transfers between devices, over_y(): return lax.ppermute(value, 'tensor', [(i, i ^ d) for i in range(4)])  12.5 us
    ppermute x6, waiting for transfers between devices, over_x(): return lax.ppermute(value, flat, [(i, i ^ 2 * d) for i in range(32)])  9.85 us
    ppermute x6, starting transfers between devices, over_x(): return lax.ppermute(value, flat, [(i, i ^ 2 * d) for i in range(32)])  7.99 us
    ppermute x3, starting transfers between devices, over_chip(): return lax.ppermute(value, 'section', [(i, i ^ 2) for i in range(4)])  6.68 us
    ppermute x3, waiting for transfers between devices, over_z(): return lax.ppermute(value, flat, [(i, i ^ 8 * d) for i in range(32)])  5.95 us
  transfers between devices with their start and end apart: 37, of which 18 were waited for; matrix products, arithmetic and copies ran while one was open for 1% of the time, Pallas kernels for 16%

profile of v2, /device:TPU:0, one launch (start us, length us, event | category | flops | bytes accessed | tf_op | source)
XLA Modules:
  0.0 121.9 jit_solution(1668393211601450886)
XLA Ops:
  1.1 1.7 %collective-permute-start.2 = (bf16[256,384]{1,0:T(8,128)(2,1)S(1)}, bf16[256,384]{1,0:T(8,128)(2,1)S(1)}, u32[]{:S(2)}, u32[]{:S(2)}) collective-permute-start(bf16[256,384]{1,0:T(8,128)(2,1)S(1)} %get-tuple-element.80.refs_0_.cot_lo), channel_id=1, source_target_pairs={{0,4},{4,0},{8,12},{12,8},{1,5},{5,1},{9,13},{13,9},{2,6},{6,2},{1... | collective-permute-start | bytes 589832 | tf_op jit(solution)/shard_map/ppermute | solution.py:290
  2.9 2.2 %collective-permute-start.3 = (bf16[256,384]{1,0:T(8,128)(2,1)S(1)}, bf16[256,384]{1,0:T(8,128)(2,1)S(1)}, u32[]{:S(2)}, u32[]{:S(2)}) collective-permute-start(bf16[256,384]{1,0:T(8,128)(2,1)S(1)} %get-tuple-element.81.refs_1_.cot_hi), channel_id=1, source_target_pairs={{0,12},{4,8},{8,4},{12,0},{1,13},{5,9},{9,5},{13,1},{2,14},{6,10},... | collective-permute-start | bytes 589832 | tf_op jit(solution)/shard_map/ppermute | solution.py:290
  10.2 2.5 %collective-permute-start.6 = (bf16[256,384]{1,0:T(8,128)(2,1)S(1)}, bf16[256,384]{1,0:T(8,128)(2,1)S(1)}, u32[]{:S(2)}, u32[]{:S(2)}) collective-permute-start(bf16[256,384]{1,0:T(8,128)(2,1)S(1)} %collective-permute-done.2.refs_2_), channel_id=1, source_target_pairs={{0,12},{4,8},{8,4},{12,0},{1,13},{5,9},{9,5},{13,1},{2,14},{6,10},... | collective-permute-start | bytes 589832 | tf_op jit(solution)/shard_map/ppermute | solution.py:290
  14.2 2.1 %copy-done.4 = bf16[3,1536,384]{2,1,0:T(8,128)(2,1)S(1)} copy-done((bf16[3,1536,384]{2,1,0:T(8,128)(2,1)S(1)}, bf16[3,1536,384]{2,1,0:T(8,128)(2,1)}, u32[]{:S(2)}) %copy-start.4) | copy-done | bytes 3538968
  16.3 3.0 %shard_map.83 = (bf16[256,384]{1,0:T(8,128)(2,1)S(1)}, bf16[256,384]{1,0:T(8,128)(2,1)S(1)}, bf16[576,1536]{1,0:T(8,128)(2,1)S(1)}) custom-call(s32[512,32]{1,0:T(8,128)S(1)} %get-tuple-element.142.marks_ref, s32[32,32]{1,0:T(8,128)S(1)} %collective-permute-done.low_ref, s32[32,32]{1,0:T(8,128)S(1)} %collective-permute-done.1.high_ref, ...), custom_call_target="tpu_custom_call" | custom-call | flops 2000000000 | bytes 5578752 | tf_op jit(solution)/shard_map/pallas_call | solution.py:33
  22.8 2.5 %collective-permute-start.10 = (bf16[256,384]{1,0:T(8,128)(2,1)S(1)}, bf16[256,384]{1,0:T(8,128)(2,1)S(1)}, u32[]{:S(2)}, u32[]{:S(2)}) collective-permute-start(bf16[256,384]{1,0:T(8,128)(2,1)S(1)} %get-tuple-element.95.refs_0_), channel_id=1, source_target_pairs={{0,12},{4,8},{8,4},{12,0},{1,13},{5,9},{9,5},{13,1},{2,14},{6,10},... | collective-permute-start | bytes 589832 | tf_op jit(solution)/shard_map/ppermute | solution.py:290
  26.5 4.0 %collective-permute-start.14 = (bf16[192,512]{1,0:T(8,128)(2,1)S(1)}, bf16[192,512]{1,0:T(8,128)(2,1)S(1)}, u32[]{:S(2)}, u32[]{:S(2)}) collective-permute-start(bf16[192,512]{1,0:T(8,128)(2,1)S(1)} %get-tuple-element.88), channel_id=1, source_target_pairs={{0,2},{1,3},{2,0},{3,1},{4,6},{5,7},{6,4},{7,5},{8,10},{9,11},{10,... | collective-permute-start | bytes 589832 | tf_op jit(solution)/shard_map/ppermute | solution.py:296
  31.7 1.5 %collective-permute-start.13 = (bf16[256,384]{1,0:T(8,128)(2,1)S(1)}, bf16[256,384]{1,0:T(8,128)(2,1)S(1)}, u32[]{:S(2)}, u32[]{:S(2)}) collective-permute-start(bf16[256,384]{1,0:T(8,128)(2,1)S(1)} %collective-permute-done.11.refs_5_), channel_id=1, source_target_pairs={{0,4},{4,0},{8,12},{12,8},{1,5},{5,1},{9,13},{13,9},{2,6},{6,2},{1... | collective-permute-start | bytes 589832 | tf_op jit(solution)/shard_map/ppermute | solution.py:290
  33.2 2.1 %shard_map.85 = (bf16[2304,512]{1,0:T(8,128)(2,1)S(1)}, bf16[2304,512]{1,0:T(8,128)(2,1)S(1)}) custom-call(bf16[576,1536]{1,0:T(8,128)(2,1)S(1)} %get-tuple-element.90.ext_ref), custom_call_target="tpu_custom_call" | custom-call | flops 3000000000 | bytes 1769472 | tf_op jit(solution)/shard_map/pallas_call | solution.py:33
  35.3 3.5 %collective-permute-done.12.refs_6_ = bf16[256,384]{1,0:T(8,128)(2,1)S(1)} collective-permute-done((bf16[256,384]{1,0:T(8,128)(2,1)S(1)}, bf16[256,384]{1,0:T(8,128)(2,1)S(1)}, u32[]{:S(2)}, u32[]{:S(2)}) %collective-permute-start.12) | collective-permute-done | bytes 196640 | tf_op jit(solution)/shard_map/ppermute | solution.py:290
  38.8 1.6 %shard_map.87 = (bf16[320,512]{1,0:T(8,128)(2,1)S(1)}, bf16[320,512]{1,0:T(8,128)(2,1)S(1)}, f32[256,512]{1,0:T(8,128)S(1)}, f32[4,512]{1,0:T(4,128)S(1)}) custom-call(bf16[256,384]{1,0:T(8,128)(2,1)S(1)} %get-tuple-element.95.refs_0_, bf16[256,384]{1,0:T(8,128)(2,1)S(1)} %get-tuple-element.96.refs_1_, bf16[256,384]{1,0:T(8,128)(2,1)S(1)} %collective-permute-done.8.refs_2_, ...), custom_call_target="tpu_custom_call" | custom-call | flops 1500000000 | bytes 3538944 | tf_op jit(solution)/shard_map/pallas_call | solution.py:33
  40.4 1.9 %collective-permute-start.16 = (bf16[320,512]{1,0:T(8,128)(2,1)S(1)}, bf16[320,512]{1,0:T(8,128)(2,1)S(1)}, u32[]{:S(2)}, u32[]{:S(2)}) collective-permute-start(bf16[320,512]{1,0:T(8,128)(2,1)S(1)} %get-tuple-element.105), channel_id=1, source_target_pairs={{0,2},{1,3},{2,0},{3,1},{4,6},{5,7},{6,4},{7,5},{8,10},{9,11},{10,... | collective-permute-start | bytes 983048 | tf_op jit(solution)/shard_map/ppermute | solution.py:296
  42.3 7.2 %collective-permute-done.16.par = bf16[320,512]{1,0:T(8,128)(2,1)S(1)} collective-permute-done((bf16[320,512]{1,0:T(8,128)(2,1)S(1)}, bf16[320,512]{1,0:T(8,128)(2,1)S(1)}, u32[]{:S(2)}, u32[]{:S(2)}) %collective-permute-start.16) | collective-permute-done | bytes 327712 | tf_op jit(solution)/shard_map/ppermute | solution.py:296
  51.1 7.4 %shard_map.88 = (bf16[64,512]{1,0:T(8,128)(2,1)S(1)}, bf16[64,512]{1,0:T(8,128)(2,1)S(1)}, f32[256,1024]{1,0:T(8,128)S(1)}, bf16[256,1024]{1,0:T(8,128)(2,1)S(1)}) custom-call(bf16[320,512]{1,0:T(8,128)(2,1)S(1)} %get-tuple-element.104.own, bf16[320,512]{1,0:T(8,128)(2,1)S(1)} %collective-permute-done.16.par, ...), custom_call_target="tpu_custom_call" | custom-call | flops 8000000000 | bytes 1703936 | tf_op jit(solution)/shard_map/pallas_call | solution.py:33
  58.7 1.8 %collective-permute-done.19.kv_got = bf16[256,1024]{1,0:T(8,128)(2,1)S(1)} collective-permute-done((bf16[256,1024]{1,0:T(8,128)(2,1)S(1)}, bf16[256,1024]{1,0:T(8,128)(2,1)S(1)}, u32[]{:S(2)}, u32[]{:S(2)}) %collective-permute-start.19) | collective-permute-done | bytes 524320 | tf_op jit(solution)/shard_map/ppermute | solution.py:293
  61.4 9.0 %collective-permute-done.20.other = bf16[320,512]{1,0:T(8,128)(2,1)S(1)} collective-permute-done((bf16[320,512]{1,0:T(8,128)(2,1)S(1)}, bf16[320,512]{1,0:T(8,128)(2,1)S(1)}, u32[]{:S(2)}, u32[]{:S(2)}) %collective-permute-start.20) | collective-permute-done | bytes 327712 | tf_op jit(solution)/shard_map/ppermute | solution.py:296
  71.2 1.5 %collective-permute-start.24 = (bf16[192,512]{1,0:T(8,128)(2,1)S(1)}, bf16[192,512]{1,0:T(8,128)(2,1)S(1)}, u32[]{:S(2)}, u32[]{:S(2)}) collective-permute-start(bf16[192,512]{1,0:T(8,128)(2,1)S(1)} %get-tuple-element.122), channel_id=1, source_target_pairs={{0,12},{4,8},{8,4},{12,0},{1,13},{5,9},{9,5},{13,1},{2,14},{6,10},... | collective-permute-start | bytes 589832 | tf_op jit(solution)/shard_map/ppermute | solution.py:290
  73.5 1.4 %collective-permute-start.21 = (bf16[192,512]{1,0:T(8,128)(2,1)S(1)}, bf16[192,512]{1,0:T(8,128)(2,1)S(1)}, u32[]{:S(2)}, u32[]{:S(2)}) collective-permute-start(bf16[192,512]{1,0:T(8,128)(2,1)S(1)} %get-tuple-element.117), channel_id=1, source_target_pairs={{0,4},{4,0},{8,12},{12,8},{1,5},{5,1},{9,13},{13,9},{2,6},{6,2},{1... | collective-permute-start | bytes 589832 | tf_op jit(solution)/shard_map/ppermute | solution.py:290
  74.9 1.8 %collective-permute-start.22 = (bf16[192,512]{1,0:T(8,128)(2,1)S(1)}, bf16[192,512]{1,0:T(8,128)(2,1)S(1)}, u32[]{:S(2)}, u32[]{:S(2)}) collective-permute-start(bf16[192,512]{1,0:T(8,128)(2,1)S(1)} %get-tuple-element.118), channel_id=1, source_target_pairs={{0,12},{4,8},{8,4},{12,0},{1,13},{5,9},{9,5},{13,1},{2,14},{6,10},... | collective-permute-start | bytes 589832 | tf_op jit(solution)/shard_map/ppermute | solution.py:290
  76.7 2.3 %collective-permute-done.23.got_a = bf16[192,512]{1,0:T(8,128)(2,1)S(1)} collective-permute-done((bf16[192,512]{1,0:T(8,128)(2,1)S(1)}, bf16[192,512]{1,0:T(8,128)(2,1)S(1)}, u32[]{:S(2)}, u32[]{:S(2)}) %collective-permute-start.23) | collective-permute-done | bytes 196640 | tf_op jit(solution)/shard_map/ppermute | solution.py:290
  82.3 1.9 %collective-permute-done.22.got3_b = bf16[192,512]{1,0:T(8,128)(2,1)S(1)} collective-permute-done((bf16[192,512]{1,0:T(8,128)(2,1)S(1)}, bf16[192,512]{1,0:T(8,128)(2,1)S(1)}, u32[]{:S(2)}, u32[]{:S(2)}) %collective-permute-start.22) | collective-permute-done | bytes 196640 | tf_op jit(solution)/shard_map/ppermute | solution.py:290
  84.2 2.8 %collective-permute-done.25.got3_a = bf16[192,512]{1,0:T(8,128)(2,1)S(1)} collective-permute-done((bf16[192,512]{1,0:T(8,128)(2,1)S(1)}, bf16[192,512]{1,0:T(8,128)(2,1)S(1)}, u32[]{:S(2)}, u32[]{:S(2)}) %collective-permute-start.25) | collective-permute-done | bytes 196640 | tf_op jit(solution)/shard_map/ppermute | solution.py:290
  87.2 1.7 %collective-permute-done.27.g_sib = bf16[384,512]{1,0:T(8,128)(2,1)S(1)} collective-permute-done((bf16[384,512]{1,0:T(8,128)(2,1)S(1)}, bf16[384,512]{1,0:T(8,128)(2,1)S(1)}, u32[]{:S(2)}, u32[]{:S(2)}) %collective-permute-start.27) | collective-permute-done | bytes 393248 | tf_op jit(solution)/shard_map/ppermute | solution.py:293
  89.7 2.4 %collective-permute-start.30 = (bf16[288,384]{1,0:T(8,128)(2,1)S(1)}, bf16[288,384]{1,0:T(8,128)(2,1)S(1)}, u32[]{:S(2)}, u32[]{:S(2)}) collective-permute-start(bf16[288,384]{1,0:T(8,128)(2,1)S(1)} %get-tuple-element.128), channel_id=1, source_target_pairs={{0,2},{1,3},{2,0},{3,1},{16,18},{17,19},{18,16},{19,17},{32,34},{3... | collective-permute-start | bytes 663560 | tf_op jit(solution)/shard_map/ppermute | solution.py:299
  92.1 1.9 %collective-permute-start.31 = (bf16[288,384]{1,0:T(8,128)(2,1)S(1)}, bf16[288,384]{1,0:T(8,128)(2,1)S(1)}, u32[]{:S(2)}, u32[]{:S(2)}) collective-permute-start(bf16[288,384]{1,0:T(8,128)(2,1)S(1)} %get-tuple-element.130), channel_id=1, source_target_pairs={{0,18},{1,19},{2,16},{3,17},{16,2},{17,3},{18,0},{19,1},{32,50},{3... | collective-permute-start | bytes 663560 | tf_op jit(solution)/shard_map/ppermute | solution.py:299
  98.4 3.3 %collective-permute-done.31.got_b = bf16[288,384]{1,0:T(8,128)(2,1)S(1)} collective-permute-done((bf16[288,384]{1,0:T(8,128)(2,1)S(1)}, bf16[288,384]{1,0:T(8,128)(2,1)S(1)}, u32[]{:S(2)}, u32[]{:S(2)}) %collective-permute-start.31) | collective-permute-done | bytes 221216 | tf_op jit(solution)/shard_map/ppermute | solution.py:299
  101.7 2.0 %collective-permute-start.32 = (bf16[288,384]{1,0:T(8,128)(2,1)S(1)}, bf16[288,384]{1,0:T(8,128)(2,1)S(1)}, u32[]{:S(2)}, u32[]{:S(2)}) collective-permute-start(bf16[288,384]{1,0:T(8,128)(2,1)S(1)} %get-tuple-element.131), channel_id=1, source_target_pairs={{0,18},{1,19},{2,16},{3,17},{16,2},{17,3},{18,0},{19,1},{32,50},{3... | collective-permute-start | bytes 663560 | tf_op jit(solution)/shard_map/ppermute | solution.py:299
  104.5 1.9 %collective-permute-done.29.got3_b = bf16[288,384]{1,0:T(8,128)(2,1)S(1)} collective-permute-done((bf16[288,384]{1,0:T(8,128)(2,1)S(1)}, bf16[288,384]{1,0:T(8,128)(2,1)S(1)}, u32[]{:S(2)}, u32[]{:S(2)}) %collective-permute-start.29) | collective-permute-done | bytes 221216 | tf_op jit(solution)/shard_map/ppermute | solution.py:299
  106.4 3.6 %collective-permute-done.32.got3_a = bf16[288,384]{1,0:T(8,128)(2,1)S(1)} collective-permute-done((bf16[288,384]{1,0:T(8,128)(2,1)S(1)}, bf16[288,384]{1,0:T(8,128)(2,1)S(1)}, u32[]{:S(2)}, u32[]{:S(2)}) %collective-permute-start.32) | collective-permute-done | bytes 221216 | tf_op jit(solution)/shard_map/ppermute | solution.py:299
  110.3 4.0 %collective-permute-start.34 = (bf16[144,384]{1,0:T(8,128)(2,1)S(1)}, bf16[144,384]{1,0:T(8,128)(2,1)S(1)}, u32[]{:S(2)}, u32[]{:S(2)}) collective-permute-start(bf16[144,384]{1,0:T(8,128)(2,1)S(1)} %get-tuple-element.134), channel_id=1, source_target_pairs={{0,64},{1,65},{2,66},{3,67},{16,80},{17,81},{18,82},{19,83},{32,96... | collective-permute-start | bytes 331784 | tf_op jit(solution)/shard_map/ppermute | solution.py:302
  115.2 2.6 %collective-permute-done.34.r1 = bf16[144,384]{1,0:T(8,128)(2,1)S(1)} collective-permute-done((bf16[144,384]{1,0:T(8,128)(2,1)S(1)}, bf16[144,384]{1,0:T(8,128)(2,1)S(1)}, u32[]{:S(2)}, u32[]{:S(2)}) %collective-permute-start.34) | collective-permute-done | bytes 110624 | tf_op jit(solution)/shard_map/ppermute | solution.py:302
  119.3 1.9 %collective-permute-done.36.r3 = bf16[144,384]{1,0:T(8,128)(2,1)S(1)} collective-permute-done((bf16[144,384]{1,0:T(8,128)(2,1)S(1)}, bf16[144,384]{1,0:T(8,128)(2,1)S(1)}, u32[]{:S(2)}, u32[]{:S(2)}) %collective-permute-start.36) | collective-permute-done | bytes 110624 | tf_op jit(solution)/shard_map/ppermute | solution.py:302
  (78 shorter events, 30.5 us)
Async XLA Ops:
  1.1 9.1 %collective-permute-start.2 = (bf16[256,384]{1,0:T(8,128)(2,1)S(1)}, bf16[256,384]{1,0:T(8,128)(2,1)S(1)}, u32[]{:S(2)}, u32[]{:S(2)}) collective-permute-start(bf16[256,384]{1,0:T(8,128)(2,1)S(1)} %get-tuple-element.80.refs_0_.cot_lo), channel_id=1, source_target_pairs={{0,4},{4,0},{8,12},{12,8},{1,5},{5,1},{9,13},{13,9},{2,6},{6,2},{1... | collective-permute-start | bytes 589832 | tf_op jit(solution)/shard_map/ppermute | solution.py:290
  2.9 9.9 %collective-permute-start.3 = (bf16[256,384]{1,0:T(8,128)(2,1)S(1)}, bf16[256,384]{1,0:T(8,128)(2,1)S(1)}, u32[]{:S(2)}, u32[]{:S(2)}) collective-permute-start(bf16[256,384]{1,0:T(8,128)(2,1)S(1)} %get-tuple-element.81.refs_1_.cot_hi), channel_id=1, source_target_pairs={{0,12},{4,8},{8,4},{12,0},{1,13},{5,9},{9,5},{13,1},{2,14},{6,10},... | collective-permute-start | bytes 589832 | tf_op jit(solution)/shard_map/ppermute | solution.py:290
  7.4 12.0 %collective-permute-start.4 = (bf16[256,384]{1,0:T(8,128)(2,1)S(1)}, bf16[256,384]{1,0:T(8,128)(2,1)S(1)}, u32[]{:S(2)}, u32[]{:S(2)}) collective-permute-start(bf16[256,384]{1,0:T(8,128)(2,1)S(1)} %get-tuple-element.81.refs_1_.cot_hi), channel_id=1, source_target_pairs={{0,4},{4,0},{8,12},{12,8},{1,5},{5,1},{9,13},{13,9},{2,6},{6,2},{1... | collective-permute-start | bytes 589832 | tf_op jit(solution)/shard_map/ppermute | solution.py:290
  8.1 11.3 %collective-permute-start.5 = (bf16[256,384]{1,0:T(8,128)(2,1)S(1)}, bf16[256,384]{1,0:T(8,128)(2,1)S(1)}, u32[]{:S(2)}, u32[]{:S(2)}) collective-permute-start(bf16[256,384]{1,0:T(8,128)(2,1)S(1)} %get-tuple-element.80.refs_0_.cot_lo), channel_id=1, source_target_pairs={{0,12},{4,8},{8,4},{12,0},{1,13},{5,9},{9,5},{13,1},{2,14},{6,10},... | collective-permute-start | bytes 589832 | tf_op jit(solution)/shard_map/ppermute | solution.py:290
  8.9 5.3 %collective-permute-start.1 = (s32[32,32]{1,0:T(8,128)S(1)}, s32[32,32]{1,0:T(8,128)S(1)}, u32[]{:S(2)}, u32[]{:S(2)}) collective-permute-start(s32[32,32]{1,0:T(8,128)S(1)} %get-tuple-element.139), channel_id=1, source_target_pairs={{1,0},{2,1},{3,2},{5,4},{6,5},{7,6},{9,8},{10,9},{11,10},{13,12},{... | collective-permute-start | bytes 12296 | tf_op jit(solution)/shard_map/ppermute | solution.py:287
  10.2 10.1 %collective-permute-start.6 = (bf16[256,384]{1,0:T(8,128)(2,1)S(1)}, bf16[256,384]{1,0:T(8,128)(2,1)S(1)}, u32[]{:S(2)}, u32[]{:S(2)}) collective-permute-start(bf16[256,384]{1,0:T(8,128)(2,1)S(1)} %collective-permute-done.2.refs_2_), channel_id=1, source_target_pairs={{0,12},{4,8},{8,4},{12,0},{1,13},{5,9},{9,5},{13,1},{2,14},{6,10},... | collective-permute-start | bytes 589832 | tf_op jit(solution)/shard_map/ppermute | solution.py:290
  12.7 7.6 %collective-permute-start.7 = (bf16[256,384]{1,0:T(8,128)(2,1)S(1)}, bf16[256,384]{1,0:T(8,128)(2,1)S(1)}, u32[]{:S(2)}, u32[]{:S(2)}) collective-permute-start(bf16[256,384]{1,0:T(8,128)(2,1)S(1)} %collective-permute-done.3.refs_5_), channel_id=1, source_target_pairs={{0,4},{4,0},{8,12},{12,8},{1,5},{5,1},{9,13},{13,9},{2,6},{6,2},{1... | collective-permute-start | bytes 589832 | tf_op jit(solution)/shard_map/ppermute | solution.py:290
  20.4 10.2 %collective-permute-start.8 = (bf16[256,384]{1,0:T(8,128)(2,1)S(1)}, bf16[256,384]{1,0:T(8,128)(2,1)S(1)}, u32[]{:S(2)}, u32[]{:S(2)}) collective-permute-start(bf16[256,384]{1,0:T(8,128)(2,1)S(1)} %get-tuple-element.95.refs_0_), channel_id=1, source_target_pairs={{0,4},{4,0},{8,12},{12,8},{1,5},{5,1},{9,13},{13,9},{2,6},{6,2},{1... | collective-permute-start | bytes 589832 | tf_op jit(solution)/shard_map/ppermute | solution.py:290
  21.4 10.3 %collective-permute-start.11 = (bf16[256,384]{1,0:T(8,128)(2,1)S(1)}, bf16[256,384]{1,0:T(8,128)(2,1)S(1)}, u32[]{:S(2)}, u32[]{:S(2)}) collective-permute-start(bf16[256,384]{1,0:T(8,128)(2,1)S(1)} %get-tuple-element.96.refs_1_), channel_id=1, source_target_pairs={{0,12},{4,8},{8,4},{12,0},{1,13},{5,9},{9,5},{13,1},{2,14},{6,10},... | collective-permute-start | bytes 589832 | tf_op jit(solution)/shard_map/ppermute | solution.py:290
  22.8 12.5 %collective-permute-start.10 = (bf16[256,384]{1,0:T(8,128)(2,1)S(1)}, bf16[256,384]{1,0:T(8,128)(2,1)S(1)}, u32[]{:S(2)}, u32[]{:S(2)}) collective-permute-start(bf16[256,384]{1,0:T(8,128)(2,1)S(1)} %get-tuple-element.95.refs_0_), channel_id=1, source_target_pairs={{0,12},{4,8},{8,4},{12,0},{1,13},{5,9},{9,5},{13,1},{2,14},{6,10},... | collective-permute-start | bytes 589832 | tf_op jit(solution)/shard_map/ppermute | solution.py:290
  25.3 10.0 %collective-permute-start.9 = (bf16[256,384]{1,0:T(8,128)(2,1)S(1)}, bf16[256,384]{1,0:T(8,128)(2,1)S(1)}, u32[]{:S(2)}, u32[]{:S(2)}) collective-permute-start(bf16[256,384]{1,0:T(8,128)(2,1)S(1)} %get-tuple-element.96.refs_1_), channel_id=1, source_target_pairs={{0,4},{4,0},{8,12},{12,8},{1,5},{5,1},{9,13},{13,9},{2,6},{6,2},{1... | collective-permute-start | bytes 589832 | tf_op jit(solution)/shard_map/ppermute | solution.py:290
  26.5 8.7 %collective-permute-start.14 = (bf16[192,512]{1,0:T(8,128)(2,1)S(1)}, bf16[192,512]{1,0:T(8,128)(2,1)S(1)}, u32[]{:S(2)}, u32[]{:S(2)}) collective-permute-start(bf16[192,512]{1,0:T(8,128)(2,1)S(1)} %get-tuple-element.88), channel_id=1, source_target_pairs={{0,2},{1,3},{2,0},{3,1},{4,6},{5,7},{6,4},{7,5},{8,10},{9,11},{10,... | collective-permute-start | bytes 589832 | tf_op jit(solution)/shard_map/ppermute | solution.py:296
  30.5 8.3 %collective-permute-start.12 = (bf16[256,384]{1,0:T(8,128)(2,1)S(1)}, bf16[256,384]{1,0:T(8,128)(2,1)S(1)}, u32[]{:S(2)}, u32[]{:S(2)}) collective-permute-start(bf16[256,384]{1,0:T(8,128)(2,1)S(1)} %collective-permute-done.8.refs_2_), channel_id=1, source_target_pairs={{0,12},{4,8},{8,4},{12,0},{1,13},{5,9},{9,5},{13,1},{2,14},{6,10},... | collective-permute-start | bytes 589832 | tf_op jit(solution)/shard_map/ppermute | solution.py:290
  31.7 7.1 %collective-permute-start.13 = (bf16[256,384]{1,0:T(8,128)(2,1)S(1)}, bf16[256,384]{1,0:T(8,128)(2,1)S(1)}, u32[]{:S(2)}, u32[]{:S(2)}) collective-permute-start(bf16[256,384]{1,0:T(8,128)(2,1)S(1)} %collective-permute-done.11.refs_5_), channel_id=1, source_target_pairs={{0,4},{4,0},{8,12},{12,8},{1,5},{5,1},{9,13},{13,9},{2,6},{6,2},{1... | collective-permute-start | bytes 589832 | tf_op jit(solution)/shard_map/ppermute | solution.py:290
  40.4 9.1 %collective-permute-start.16 = (bf16[320,512]{1,0:T(8,128)(2,1)S(1)}, bf16[320,512]{1,0:T(8,128)(2,1)S(1)}, u32[]{:S(2)}, u32[]{:S(2)}) collective-permute-start(bf16[320,512]{1,0:T(8,128)(2,1)S(1)} %get-tuple-element.105), channel_id=1, source_target_pairs={{0,2},{1,3},{2,0},{3,1},{4,6},{5,7},{6,4},{7,5},{8,10},{9,11},{10,... | collective-permute-start | bytes 983048 | tf_op jit(solution)/shard_map/ppermute | solution.py:296
  42.3 7.7 %collective-permute-start.17 = (bf16[320,512]{1,0:T(8,128)(2,1)S(1)}, bf16[320,512]{1,0:T(8,128)(2,1)S(1)}, u32[]{:S(2)}, u32[]{:S(2)}) collective-permute-start(bf16[320,512]{1,0:T(8,128)(2,1)S(1)} %get-tuple-element.104.own), channel_id=1, source_target_pairs={{0,1},{1,0},{2,3},{3,2},{4,5},{5,4},{6,7},{7,6},{8,9},{9,8},{10,11... | collective-permute-start | bytes 983048 | tf_op jit(solution)/shard_map/ppermute | solution.py:293
  49.5 39.5 %collective-permute-start.15 = (bf16[2304,512]{1,0:T(8,128)(2,1)S(1)}, bf16[2304,512]{1,0:T(8,128)(2,1)S(1)}, u32[]{:S(2)}, u32[]{:S(2)}) collective-permute-start(bf16[2304,512]{1,0:T(8,128)(2,1)S(1)} %get-tuple-element.94), channel_id=1, source_target_pairs={{0,1},{1,0},{2,3},{3,2},{4,5},{5,4},{6,7},{7,6},{8,9},{9,8},{10,11... | collective-permute-start | bytes 7077896 | tf_op jit(solution)/shard_map/ppermute | solution.py:293
  60.6 9.8 %collective-permute-start.20 = (bf16[320,512]{1,0:T(8,128)(2,1)S(1)}, bf16[320,512]{1,0:T(8,128)(2,1)S(1)}, u32[]{:S(2)}, u32[]{:S(2)}) collective-permute-start(bf16[320,512]{1,0:T(8,128)(2,1)S(1)} %get-tuple-element.113), channel_id=1, source_target_pairs={{0,2},{1,3},{2,0},{3,1},{4,6},{5,7},{6,4},{7,5},{8,10},{9,11},{10,... | collective-permute-start | bytes 983048 | tf_op jit(solution)/shard_map/ppermute | solution.py:296
  71.1 7.9 %collective-permute-start.23 = (bf16[192,512]{1,0:T(8,128)(2,1)S(1)}, bf16[192,512]{1,0:T(8,128)(2,1)S(1)}, u32[]{:S(2)}, u32[]{:S(2)}) collective-permute-start(bf16[192,512]{1,0:T(8,128)(2,1)S(1)} %get-tuple-element.120), channel_id=1, source_target_pairs={{0,4},{4,0},{8,12},{12,8},{1,5},{5,1},{9,13},{13,9},{2,6},{6,2},{1... | collective-permute-start | bytes 589832 | tf_op jit(solution)/shard_map/ppermute | solution.py:290
  71.2 8.8 %collective-permute-start.24 = (bf16[192,512]{1,0:T(8,128)(2,1)S(1)}, bf16[192,512]{1,0:T(8,128)(2,1)S(1)}, u32[]{:S(2)}, u32[]{:S(2)}) collective-permute-start(bf16[192,512]{1,0:T(8,128)(2,1)S(1)} %get-tuple-element.122), channel_id=1, source_target_pairs={{0,12},{4,8},{8,4},{12,0},{1,13},{5,9},{9,5},{13,1},{2,14},{6,10},... | collective-permute-start | bytes 589832 | tf_op jit(solution)/shard_map/ppermute | solution.py:290
  73.5 8.8 %collective-permute-start.21 = (bf16[192,512]{1,0:T(8,128)(2,1)S(1)}, bf16[192,512]{1,0:T(8,128)(2,1)S(1)}, u32[]{:S(2)}, u32[]{:S(2)}) collective-permute-start(bf16[192,512]{1,0:T(8,128)(2,1)S(1)} %get-tuple-element.117), channel_id=1, source_target_pairs={{0,4},{4,0},{8,12},{12,8},{1,5},{5,1},{9,13},{13,9},{2,6},{6,2},{1... | collective-permute-start | bytes 589832 | tf_op jit(solution)/shard_map/ppermute | solution.py:290
  74.9 9.3 %collective-permute-start.22 = (bf16[192,512]{1,0:T(8,128)(2,1)S(1)}, bf16[192,512]{1,0:T(8,128)(2,1)S(1)}, u32[]{:S(2)}, u32[]{:S(2)}) collective-permute-start(bf16[192,512]{1,0:T(8,128)(2,1)S(1)} %get-tuple-element.118), channel_id=1, source_target_pairs={{0,12},{4,8},{8,4},{12,0},{1,13},{5,9},{9,5},{13,1},{2,14},{6,10},... | collective-permute-start | bytes 589832 | tf_op jit(solution)/shard_map/ppermute | solution.py:290
  80.0 7.0 %collective-permute-start.25 = (bf16[192,512]{1,0:T(8,128)(2,1)S(1)}, bf16[192,512]{1,0:T(8,128)(2,1)S(1)}, u32[]{:S(2)}, u32[]{:S(2)}) collective-permute-start(bf16[192,512]{1,0:T(8,128)(2,1)S(1)} %get-tuple-element.123), channel_id=1, source_target_pairs={{0,12},{4,8},{8,4},{12,0},{1,13},{5,9},{9,5},{13,1},{2,14},{6,10},... | collective-permute-start | bytes 589832 | tf_op jit(solution)/shard_map/ppermute | solution.py:290
  81.2 5.8 %collective-permute-start.26 = (bf16[192,512]{1,0:T(8,128)(2,1)S(1)}, bf16[192,512]{1,0:T(8,128)(2,1)S(1)}, u32[]{:S(2)}, u32[]{:S(2)}) collective-permute-start(bf16[192,512]{1,0:T(8,128)(2,1)S(1)} %get-tuple-element.124), channel_id=1, source_target_pairs={{0,4},{4,0},{8,12},{12,8},{1,5},{5,1},{9,13},{13,9},{2,6},{6,2},{1... | collective-permute-start | bytes 589832 | tf_op jit(solution)/shard_map/ppermute | solution.py:290
  89.7 8.6 %collective-permute-start.30 = (bf16[288,384]{1,0:T(8,128)(2,1)S(1)}, bf16[288,384]{1,0:T(8,128)(2,1)S(1)}, u32[]{:S(2)}, u32[]{:S(2)}) collective-permute-start(bf16[288,384]{1,0:T(8,128)(2,1)S(1)} %get-tuple-element.128), channel_id=1, source_target_pairs={{0,2},{1,3},{2,0},{3,1},{16,18},{17,19},{18,16},{19,17},{32,34},{3... | collective-permute-start | bytes 663560 | tf_op jit(solution)/shard_map/ppermute | solution.py:299
  92.1 9.5 %collective-permute-start.31 = (bf16[288,384]{1,0:T(8,128)(2,1)S(1)}, bf16[288,384]{1,0:T(8,128)(2,1)S(1)}, u32[]{:S(2)}, u32[]{:S(2)}) collective-permute-start(bf16[288,384]{1,0:T(8,128)(2,1)S(1)} %get-tuple-element.130), channel_id=1, source_target_pairs={{0,18},{1,19},{2,16},{3,17},{16,2},{17,3},{18,0},{19,1},{32,50},{3... | collective-permute-start | bytes 663560 | tf_op jit(solution)/shard_map/ppermute | solution.py:299
  94.8 9.7 %collective-permute-start.28 = (bf16[288,384]{1,0:T(8,128)(2,1)S(1)}, bf16[288,384]{1,0:T(8,128)(2,1)S(1)}, u32[]{:S(2)}, u32[]{:S(2)}) collective-permute-start(bf16[288,384]{1,0:T(8,128)(2,1)S(1)} %get-tuple-element.125), channel_id=1, source_target_pairs={{0,2},{1,3},{2,0},{3,1},{16,18},{17,19},{18,16},{19,17},{32,34},{3... | collective-permute-start | bytes 663560 | tf_op jit(solution)/shard_map/ppermute | solution.py:299
  95.9 10.5 %collective-permute-start.29 = (bf16[288,384]{1,0:T(8,128)(2,1)S(1)}, bf16[288,384]{1,0:T(8,128)(2,1)S(1)}, u32[]{:S(2)}, u32[]{:S(2)}) collective-permute-start(bf16[288,384]{1,0:T(8,128)(2,1)S(1)} %get-tuple-element.126), channel_id=1, source_target_pairs={{0,18},{1,19},{2,16},{3,17},{16,2},{17,3},{18,0},{19,1},{32,50},{3... | collective-permute-start | bytes 663560 | tf_op jit(solution)/shard_map/ppermute | solution.py:299
  101.7 8.3 %collective-permute-start.32 = (bf16[288,384]{1,0:T(8,128)(2,1)S(1)}, bf16[288,384]{1,0:T(8,128)(2,1)S(1)}, u32[]{:S(2)}, u32[]{:S(2)}) collective-permute-start(bf16[288,384]{1,0:T(8,128)(2,1)S(1)} %get-tuple-element.131), channel_id=1, source_target_pairs={{0,18},{1,19},{2,16},{3,17},{16,2},{17,3},{18,0},{19,1},{32,50},{3... | collective-permute-start | bytes 663560 | tf_op jit(solution)/shard_map/ppermute | solution.py:299
  103.7 6.3 %collective-permute-start.33 = (bf16[288,384]{1,0:T(8,128)(2,1)S(1)}, bf16[288,384]{1,0:T(8,128)(2,1)S(1)}, u32[]{:S(2)}, u32[]{:S(2)}) collective-permute-start(bf16[288,384]{1,0:T(8,128)(2,1)S(1)} %get-tuple-element.132), channel_id=1, source_target_pairs={{0,2},{1,3},{2,0},{3,1},{16,18},{17,19},{18,16},{19,17},{32,34},{3... | collective-permute-start | bytes 663560 | tf_op jit(solution)/shard_map/ppermute | solution.py:299
  110.3 7.6 %collective-permute-start.34 = (bf16[144,384]{1,0:T(8,128)(2,1)S(1)}, bf16[144,384]{1,0:T(8,128)(2,1)S(1)}, u32[]{:S(2)}, u32[]{:S(2)}) collective-permute-start(bf16[144,384]{1,0:T(8,128)(2,1)S(1)} %get-tuple-element.134), channel_id=1, source_target_pairs={{0,64},{1,65},{2,66},{3,67},{16,80},{17,81},{18,82},{19,83},{32,96... | collective-permute-start | bytes 331784 | tf_op jit(solution)/shard_map/ppermute | solution.py:302
  115.2 6.0 %collective-permute-start.36 = (bf16[144,384]{1,0:T(8,128)(2,1)S(1)}, bf16[144,384]{1,0:T(8,128)(2,1)S(1)}, u32[]{:S(2)}, u32[]{:S(2)}) collective-permute-start(bf16[144,384]{1,0:T(8,128)(2,1)S(1)} %get-tuple-element.136), channel_id=1, source_target_pairs={{0,96},{1,97},{2,98},{3,99},{16,112},{17,113},{18,114},{19,115},{3... | collective-permute-start | bytes 331784 | tf_op jit(solution)/shard_map/ppermute | solution.py:302
  (11 other events, 57.3 us)

commit v3 on v1

--- a/solution.py
+++ b/solution.py
@@ -28,12 +28,14 @@
     return lax.dot_general(left, right, (((1,), (1,)), ((), ())), preferred_element_type=f32)
 
 
-def call(kernel, outs, *args, scratch=(), flops=0, vmem=32):
+def call(kernel, outs, *args, scratch=(), flops=0, vmem=32, hbm=()):
     size = sum(math.prod(a.shape) * a.dtype.itemsize for a in args)
     return pl.pallas_call(
         kernel,
         out_shape=[jax.ShapeDtypeStruct(shape, kind) for shape, kind in outs],
-        in_specs=[pl.BlockSpec(memory_space=pltpu.VMEM)] * len(args),
+        in_specs=[
+            pl.BlockSpec(memory_space=pl.ANY if i in hbm else pltpu.VMEM) for i in range(len(args))
+        ],
         out_specs=[pl.BlockSpec(memory_space=pltpu.VMEM)] * len(outs),
         scratch_shapes=list(scratch),
         compiler_params=pltpu.CompilerParams(vmem_limit_bytes=vmem * MIB),
@@ -51,37 +53,36 @@
 
 
 def one_hot(marks):
-    spread = (
-        lax.broadcasted_iota(jnp.int32, (32, 128), 1) >> 2
-        == lax.broadcasted_iota(jnp.int32, (32, 128), 0)
-    )
+    shape = (128, 32)
+    spread = lax.broadcasted_iota(jnp.int32, shape, 0) >> 2 == lax.broadcasted_iota(jnp.int32, shape, 1)
     spread = jnp.where(spread, 1.0, 0.0).astype(bf16)
-    wide = nn(marks.astype(f32).astype(bf16), spread)
-    letter = ((lax.broadcasted_iota(jnp.int32, wide.shape, 1) & 3) + 1).astype(f32)
-    return jnp.where(wide == letter, 1.0, 0.0).astype(bf16)
+    wide = nn(spread, marks.astype(f32).astype(bf16))
+    letter = (lax.broadcasted_iota(jnp.int32, wide.shape, 0) & 3).astype(f32)
+    return jnp.where(wide == letter, 1.0, 0.0).T.astype(bf16)
 
 
 def gelu(x):
     return jax.nn.gelu(x, approximate=True)
 
 
-def stem_kernel(marks_ref, weight_ref, act_ref):
+def stem_kernel(marks_ref, stem_ref, weight_hbm, act_ref, weight_ref, arrived):
+    copy = pltpu.make_async_copy(weight_hbm, weight_ref, arrived)
+    copy.start()
     hot = one_hot(marks_ref[...])
-    for j in range(0, weight_ref.shape[1], 256):
-        act_ref[:, j : j + 256] = gelu(nn(hot, weight_ref[:, j : j + 256])).astype(bf16)
+    for j in range(0, stem_ref.shape[1], 256):
+        act_ref[:, j : j + 256] = gelu(nn(hot, stem_ref[:, j : j + 256])).astype(bf16)
+    copy.wait()
 
 
 def conv_kernel(marks_ref, low_ref, high_ref, stem_ref, act_ref, weight_ref, hidden_ref, ext_ref):
     rows = act_ref.shape[0]
-    width = weight_ref.shape[2]
-    edge = jnp.concatenate([low_ref[...], high_ref[...]], axis=0)
-    hot = one_hot(edge)
-    edge_act = gelu(nn(hot, stem_ref[...])).astype(bf16)
-    ext_ref[0:HALO] = edge_act[:HALO]
+    section = lax.axis_index("section")
+    edge = one_hot(jnp.concatenate([low_ref[:, rows - HALO :], high_ref[:, :HALO]], axis=1))
+    edge_act = gelu(nn(edge, stem_ref[...])).astype(bf16)
+    ext_ref[0:HALO] = jnp.where(section > 0, edge_act[:HALO], 0)
     ext_ref[HALO : HALO + rows] = act_ref[...]
-    ext_ref[HALO + rows :] = edge_act[HALO:]
-    own = stem_ref[:, block_at(lax.axis_index("tensor"), width)]
-    total = nn(one_hot(marks_ref[...]), own)
+    ext_ref[HALO + rows :] = jnp.where(section < 3, edge_act[HALO:], 0)
+    total = nn(one_hot(marks_ref[...]), stem_ref[:, block_at(lax.axis_index("tensor"), 384)])
     for k in range(3):
         total = total + nn(ext_ref[k * HALO : k * HALO + rows], weight_ref[k])
     hidden_ref[...] = total.astype(bf16)
@@ -108,11 +109,22 @@
                 ]
 
 
+def distances():
+    core = lax.axis_index("section") & 1
+    return 1 + 2 * core, 3 - 2 * core
+
+
+def gathered(blocks):
+    own, first, second, far = blocks
+    one, two = distances()
+    return (0, own), (one, first), (two, second), (2, far)
+
+
 def project_kernel(h0, h1, h2, h3, w_ref, mine_ref, other_ref, unit_ref, factor_ref, values):
     y = lax.axis_index("tensor")
     chip, _ = own_chip()
-    total = nt(w_ref[:, block_at(y, 384)], h0[...])
-    for d, ref in ((1, h1), (2, h2), (3, h3)):
+    total = 0.0
+    for d, ref in gathered((h0, h1, h2, h3)):
         total = total + nt(w_ref[:, block_at(y ^ d, 384)], ref[...])
     for g in range(4):
         raw = total[g * KEY : (g + 1) * KEY]
@@ -130,9 +142,9 @@
     y = lax.axis_index("tensor")
     chip, _ = own_chip()
     for ref, head in ((mine_ref, chip), (other_ref, 1 - chip)):
-        total = nt(w_ref[block_at(head, VAL), block_at(y, 384)], c0[...])
-        for d, c in ((1, c1), (2, c2), (3, c3)):
-            total = total + nt(w_ref[block_at(head, VAL), block_at(y ^ d, 384)], c[...])
+        total = 0.0
+        for d, block in gathered((c0, c1, c2, c3)):
+            total = total + nt(w_ref[block_at(head, VAL), block_at(y ^ d, 384)], block[...])
         ref[...] = total.astype(bf16)
 
 
@@ -188,7 +200,7 @@
     own_ref[64:320] = (kv_mine[:, :n] + kv_got[:, :n].astype(f32)).astype(bf16)
 
 
-def back_kernel(own, other, unit_ref, factor_ref, wq, wk, wv, back, to1, to2, to3):
+def back_kernel(own, other, unit_ref, factor_ref, wq, wk, wv, back, far_ref):
     y = lax.axis_index("tensor")
     chip, _ = own_chip()
     for ref, head in ((own, chip), (other, 1 - chip)):
@@ -200,8 +212,7 @@
             mean = jnp.mean(g * unit, axis=0, keepdims=True)
             back[at] = (factor * (g - unit * mean)).astype(bf16)
         back[pl.ds(pl.multiple_of(256 + head * VAL, 64), VAL)] = ref[128:320]
-    for d, ref in ((2, to2), (1, to1), (3, to3)):
-        ref[...] = back_rows(back, wq, wk, wv, y ^ d).astype(bf16)
+    far_ref[...] = back_rows(back, wq, wk, wv, y ^ 2).astype(bf16)
 
 
 def back_rows(back, wq, wk, wv, index):
@@ -210,15 +221,24 @@
     return nn(qk, back[0:256]) + nn(wv[at], back[256:640])
 
 
+def back_near_kernel(back, wq, wk, wv, alone_ref, joined_ref):
+    y = lax.axis_index("tensor")
+    one, two = distances()
+    alone_ref[...] = back_rows(back, wq, wk, wv, y ^ one).astype(bf16)
+    joined_ref[...] = back_rows(back, wq, wk, wv, y ^ two)
+
+
 def back_own_kernel(back, wq, wk, wv, cot, out_ref):
     y = lax.axis_index("tensor")
     out_ref[...] = back_rows(back, wq, wk, wv, y) + cot[...].astype(f32).T
 
 
-def hidden_grad_kernel(own, r1, r2, r3, out_ref):
-    out_ref[...] = (
-        own[...] + r1[...].astype(f32) + r2[...].astype(f32) + r3[...].astype(f32)
-    ).astype(bf16)
+def add_kernel(joined, got, out_ref):
+    out_ref[...] = (joined[...] + got[...].astype(f32)).astype(bf16)
+
+
+def hidden_grad_kernel(own, alone, joined, out_ref):
+    out_ref[...] = (own[...] + alone[...].astype(f32) + joined[...].astype(f32)).astype(bf16)
 
 
 def ring_place():
@@ -227,19 +247,18 @@
     return x, z
 
 
-def tap_kernel(d, t_mine, t_sib, g_mine, g_sib, out_ref):
+def tap_kernel(which, t_mine, t_sib, g_mine, g_sib, out_ref):
     x, _ = ring_place()
+    d = (0, *distances(), 2)[which]
     at = block_at(x ^ d, 576)
     out_ref[...] = (nt(t_mine[at], g_mine[...]) + nt(t_sib[at], g_sib[...])).astype(out_ref.dtype)
 
 
-def sum_x_kernel(own, r1, r2, r3, own_ref, to1, to2, to3):
+def sum_x_kernel(own, alone, joined, own_ref, to1, to2, to3):
     _, z = ring_place()
     for d, ref in ((2, to2), (1, to1), (3, to3), (0, own_ref)):
         at = block_at(z ^ d, 144)
-        ref[...] = (
-            own[at] + r1[at].astype(f32) + r2[at].astype(f32) + r3[at].astype(f32)
-        ).astype(ref.dtype)
+        ref[...] = (own[at] + alone[at].astype(f32) + joined[at].astype(f32)).astype(ref.dtype)
 
 
 def sum_z_kernel(norm, own, r1, r2, r3, out_ref):
@@ -249,16 +268,23 @@
 
 
 def body(bases, stem_w, conv_w, wq, wk, wv, out_w, cot):
-    marks = bases[0] + 1
+    marks = bases[0].T
     cot = cot[0]
-    rows = marks.shape[0]
+    rows = marks.shape[1]
     flat = ("seq", "section")
 
-    low = lax.ppermute(marks[rows - HALO :], "section", [(i, i + 1) for i in range(3)])
-    high = lax.ppermute(marks[:HALO], "section", [(i + 1, i) for i in range(3)])
-
-    def over_y(value, d):
-        return lax.ppermute(value, "tensor", [(i, i ^ d) for i in range(4)])
+    low = lax.ppermute(marks, "section", [(i, (i + 1) % 4) for i in range(4)])
+    high = lax.ppermute(marks, "section", [((i + 1) % 4, i) for i in range(4)])
+
+    def y_way(value, way):
+        pairs = []
+        for t in range(4):
+            for i in range(4):
+                pairs.append((t * 4 + i, (t ^ (1, 3)[(i + way) % 2]) * 4 + i))
+        return lax.ppermute(value, ("tensor", "section"), pairs)
+
+    def x_way(value, way):
+        return lax.ppermute(value, flat, [(i, i ^ (2 * (1, 3)[(i + way) % 2])) for i in range(32)])
 
     def over_core(value):
         return lax.ppermute(value, "section", [(i, i ^ 1) for i in range(4)])
@@ -266,42 +292,47 @@
     def over_chip(value):
         return lax.ppermute(value, "section", [(i, i ^ 2) for i in range(4)])
 
-    def over_x(value, d):
-        return lax.ppermute(value, flat, [(i, i ^ (2 * d)) for i in range(32)])
-
     def over_z(value, d):
         return lax.ppermute(value, flat, [(i, i ^ (8 * d)) for i in range(32)])
 
-    cots = [cot] + [over_y(cot, d) for d in (1, 2, 3)]
-
-    (act,) = call(stem_kernel, [((rows, 1536), bf16)], marks, stem_w, flops=4e8)
+    second = y_way(cot, 1)
+    act, conv_here = call(
+        stem_kernel, [((rows, 1536), bf16), (conv_w.shape, bf16)], marks, stem_w, conv_w,
+        scratch=[pltpu.SemaphoreType.DMA(())], flops=4e8, vmem=16, hbm=(2,),
+    )
+    first = y_way(cot, 0)
     hidden, ext = call(
         conv_kernel,
         [((rows, 384), bf16), ((rows + 2 * HALO, 1536), bf16)],
-        marks, low, high, stem_w, act, conv_w,
+        marks, low, high, stem_w, act, conv_here,
         flops=2e9,
     )
-    hiddens = [hidden] + [over_y(hidden, d) for d in (1, 2, 3)]
-
-    (w_t,) = call(turn_kernel, [((640, 1536), bf16)], wq, wk, wv, flops=1e9)
+    far = y_way(second, 0)
+    cots = (cot, first, second, far)
+
+    second = y_way(hidden, 1)
     taps_mine, taps_other = call(
         taps_kernel, [((2304, rows), bf16)] * 2, ext,
         scratch=[pltpu.VMEM((1536, rows), bf16)], flops=3e9,
     )
-    taps_sib = over_core(taps_other)
-
+    (w_t,) = call(turn_kernel, [((640, 1536), bf16)], wq, wk, wv, flops=1e9)
+    first = y_way(lax.optimization_barrier((hidden, taps_mine, w_t))[0], 0)
+    second, cots = lax.optimization_barrier((second, cots))
+    far = y_way(second, 0)
     g_own, g_other = call(grad_kernel, [((VAL, rows), bf16)] * 2, *cots, out_w, flops=1e9)
     g_par = over_chip(g_other)
+    first, second, far, g_par, g_own = lax.optimization_barrier((first, second, far, g_par, g_own))
 
     own, other, unit, factor = call(
         project_kernel,
         [((320, rows), bf16)] * 2 + [((256, rows), f32), ((4, rows), f32)],
-        *hiddens, w_t,
+        hidden, first, second, far, w_t,
         scratch=[pltpu.VMEM((384, rows), bf16)], flops=1.5e9,
     )
     par = over_chip(other)
     sib_own = over_core(own)
     sib_par = over_core(par)
+    taps_sib = over_core(taps_other)
     q_own, q_par, kv_mine, kv_sib = call(
         attend_kernel,
         [((KEY, rows), bf16)] * 2 + [((256, 2 * rows), f32), ((256, 2 * rows), bf16)],
@@ -319,28 +350,37 @@
     kv_got = over_core(kv_sib)
     back_own, back_par = call(join_kernel, [((320, rows), bf16)] * 2, q_own, q_par, kv_mine, kv_got)
     back_other = over_chip(back_par)
-    back, to1, to2, to3 = call(
+    back, far = call(
         back_kernel,
-        [((640, rows), bf16)] + [((384, rows), bf16)] * 3,
-        back_own, back_other, unit, factor, wq, wk, wv, flops=1e9,
-    )
-    got = [over_y(to2, 2), over_y(to1, 1), over_y(to3, 3)]
-    (grad_own,) = call(back_own_kernel, [((384, rows), f32)], back, wq, wk, wv, cot, flops=1e9)
-    (hg,) = call(hidden_grad_kernel, [((384, rows), bf16)], grad_own, *got)
+        [((640, rows), bf16), ((384, rows), bf16)],
+        back_own, back_other, unit, factor, wq, wk, wv, flops=5e8,
+    )
+    got = y_way(far, 0)
+    alone, joined = call(
+        back_near_kernel, [((384, rows), bf16), ((384, rows), f32)], back, wq, wk, wv, flops=8e8
+    )
+    alone = y_way(alone, 0)
+    (grad_own,) = call(back_own_kernel, [((384, rows), f32)], back, wq, wk, wv, cot, flops=5e8)
+    (joined,) = call(add_kernel, [((384, rows), bf16)], joined, got)
+    joined = y_way(joined, 1)
+    (hg,) = call(hidden_grad_kernel, [((384, rows), bf16)], grad_own, alone, joined)
     hg_sib = over_core(hg)
 
-    parts = []
-    for d in (2, 1, 3, 0):
-        (part,) = call(
-            functools.partial(tap_kernel, d),
-            [((576, 384), bf16 if d else f32)],
+    def product(which, kind):
+        return call(
+            functools.partial(tap_kernel, which),
+            [((576, 384), kind)],
             taps_mine, taps_sib, hg, hg_sib, flops=6e8,
-        )
-        parts.append(over_x(part, d) if d else part)
+        )[0]
+
+    got = x_way(product(3, bf16), 0)
+    alone = x_way(product(1, bf16), 0)
+    joined = product(2, f32)
+    part = product(0, f32)
+    (joined,) = call(add_kernel, [((576, 384), bf16)], joined, got)
+    joined = x_way(joined, 1)
     own_z, z1, z2, z3 = call(
-        sum_x_kernel,
-        [((144, 384), f32)] + [((144, 384), bf16)] * 3,
-        parts[3], parts[0], parts[1], parts[2],
+        sum_x_kernel, [((144, 384), f32)] + [((144, 384), bf16)] * 3, part, alone, joined
     )
     got = [over_z(z2, 2), over_z(z1, 1), over_z(z3, 3)]
     norm = 1.0 / math.sqrt(rows * 32)

time: 140 us -> 118 us (0.84)
  waiting for transfers between devices: 81.7 us -> 61.5 us
  starting transfers between devices: 30.4 us -> 28.2 us
    ppermute x14, waiting for transfers between devices: 51.2 us -> 29.9 us  [the longest x9 19.3 us: y_way(): return lax.ppermute(value, ('tensor', 'section'), pairs)]
    ppermute x14, starting transfers between devices: 21.4 us -> 17.9 us  [the longest x9 10.8 us: y_way(): return lax.ppermute(value, ('tensor', 'section'), pairs)]
    pallas_call x17 -> x20, Pallas kernels: 23.3 us -> 24.1 us  [call(): pl.pallas_call(kernel, out_shape=[jax.ShapeDtypeStruct(shape, kind) for s...]
    unnamed x15 -> x20, local copies, waits for them, and re-layouts: 4.13 us -> 3.87 us
  transfers between devices with their start and end apart: 25 -> 25, of which waited for: 17 -> 16; matrix products, arithmetic and copies ran while one was open for 0% -> 0% of each run, Pallas kernels for 13% -> 18%
where the time goes in v3:
time: 118 us
  waiting for transfers between devices  61.5 us (52%)
  starting transfers between devices  28.2 us (24%)
  Pallas kernels  24.1 us (20%)
  local copies, waits for them, and re-layouts  3.87 us (3%)
    pallas_call x20, Pallas kernels, call(): pl.pallas_call(kernel, out_shape=[jax.ShapeDtypeStruct(shape, kind) for s...  24.1 us
    ppermute x3, waiting for transfers between devices, over_chip(): return lax.ppermute(value, 'section', [(i, i ^ 2) for i in range(4)])  21 us
    ppermute x9, waiting for transfers between devices, y_way(): return lax.ppermute(value, ('tensor', 'section'), pairs)  19.3 us
    ppermute x9, starting transfers between devices, y_way(): return lax.ppermute(value, ('tensor', 'section'), pairs)  10.8 us
    ppermute x3, waiting for transfers between devices, x_way(): lax.ppermute(value, flat, [(i, i ^ 2 * (1, 3)[(i + way) % 2]) for i in ra...  10.5 us
    ppermute x3, waiting for transfers between devices, over_z(): return lax.ppermute(value, flat, [(i, i ^ 8 * d) for i in range(32)])  5.95 us
    ppermute x3, starting transfers between devices, x_way(): lax.ppermute(value, flat, [(i, i ^ 2 * (1, 3)[(i + way) % 2]) for i in ra...  5.35 us
    ppermute x3, starting transfers between devices, over_z(): return lax.ppermute(value, flat, [(i, i ^ 8 * d) for i in range(32)])  5 us
  transfers between devices with their start and end apart: 25, of which 16 were waited for; matrix products, arithmetic and copies ran while one was open for 0% of the time, Pallas kernels for 18%

profile of v3, /device:TPU:0, one launch (start us, length us, event | category | flops | bytes accessed | tf_op | source)
XLA Modules:
  0.0 117.8 jit_solution(10835625933742957658)
XLA Ops:
  0.0 3.1 %collective-permute-start.6 = (bf16[512,384]{1,0:T(8,128)(2,1)}, bf16[512,384]{1,0:T(8,128)(2,1)S(1)}, u32[]{:S(2)}, u32[]{:S(2)}) collective-permute-start(bf16[512,384]{1,0:T(8,128)(2,1)} %bitcast.7), channel_id=1, source_target_pairs={{0,12},{1,5},{2,14},{3,7},{4,8},{5,1},{6,10},{7,3},{8,4},{9,13},{1... | collective-permute-start | bytes 1179656 | tf_op jit(solution)/shard_map/ppermute | solution.py:284
  3.1 1.7 %collective-permute-start.1 = (s32[32,512]{1,0:T(8,128)}, s32[32,512]{1,0:T(8,128)S(1)}, u32[]{:S(2)}, u32[]{:S(2)}) collective-permute-start(s32[32,512]{1,0:T(8,128)} %bitcast.12), channel_id=1, source_target_pairs={{1,0},{2,1},{3,2},{0,3},{5,4},{6,5},{7,6},{4,7},{9,8},{10,9},{11,1... | collective-permute-start | bytes 196616 | tf_op jit(solution)/shard_map/ppermute | solution.py:277
  5.0 2.0 %copy-done.1 = bf16[3,1536,384]{2,1,0:T(8,128)(2,1)S(1)} copy-done((bf16[3,1536,384]{2,1,0:T(8,128)(2,1)S(1)}, bf16[3,1536,384]{2,1,0:T(8,128)(2,1)}, u32[]{:S(2)}) %copy-start.1) | copy-done | bytes 3538968
  8.8 1.8 %shard_map.82 = (bf16[512,1536]{1,0:T(8,128)(2,1)S(1)}, bf16[3,1536,384]{2,1,0:T(8,128)(2,1)S(1)}) custom-call(s32[32,512]{1,0:T(8,128)S(1)} %bitcast.13, bf16[128,1536]{1,0:T(8,128)(2,1)S(1)} %copy-done.5, bf16[3,1536,384]{2,1,0:T(8,128)(2,1)S(1)} %copy-done.1), custom_call_target="tpu_custom_call" | custom-call | flops 400000000 | bytes 3997696 | tf_op jit(solution)/shard_map/pallas_call | solution.py:33
  10.7 3.2 %shard_map.83 = (bf16[512,384]{1,0:T(8,128)(2,1)S(1)}, bf16[576,1536]{1,0:T(8,128)(2,1)S(1)}) custom-call(s32[32,512]{1,0:T(8,128)S(1)} %bitcast.14, s32[32,512]{1,0:T(8,128)S(1)} %collective-permute-done.low_ref, s32[32,512]{1,0:T(8,128)S(1)} %collective-permute-done.1.high_ref, bf16[128,1536]{1,0:T(8,128)(2,1)S(1)} %copy-done.6, ...), custom_call_target="tpu_custom_call" | custom-call | flops 2000000000 | bytes 5701632 | tf_op jit(solution)/shard_map/pallas_call | solution.py:33
  16.5 2.1 %shard_map.84 = (bf16[2304,512]{1,0:T(8,128)(2,1)S(1)}, bf16[2304,512]{1,0:T(8,128)(2,1)S(1)}) custom-call(bf16[576,1536]{1,0:T(8,128)(2,1)S(1)} %get-tuple-element.44.ext_ref), custom_call_target="tpu_custom_call" | custom-call | flops 3000000000 | bytes 1769472 | tf_op jit(solution)/shard_map/pallas_call | solution.py:33
  18.6 1.2 collective-permute-start.3
  19.8 7.4 %collective-permute-done.4.h2 = bf16[512,384]{1,0:T(8,128)(2,1)S(1)} collective-permute-done((bf16[512,384]{1,0:T(8,128)(2,1)S(1)}, bf16[512,384]{1,0:T(8,128)(2,1)S(1)}, u32[]{:S(2)}, u32[]{:S(2)}) %collective-permute-start.4) | collective-permute-done | bytes 393248 | tf_op jit(solution)/shard_map/ppermute | solution.py:284
  27.8 1.2 %shard_map.86 = (bf16[192,512]{1,0:T(8,128)(2,1)S(1)}, bf16[192,512]{1,0:T(8,128)(2,1)S(1)}) custom-call(bf16[512,384]{1,0:T(8,128)(2,1)S(1)} %bitcast.9, bf16[512,384]{1,0:T(8,128)(2,1)S(1)} %collective-permute-done.5.c1, bf16[512,384]{1,0:T(8,128)(2,1)S(1)} %collective-permute-done.6.c2, bf16[512,384]{1,0:T(8,128)(2,1)S(1)} %collective-permute-done.7.c3, ...), custom_call_target="tpu_custom_call" | custom-call | flops 1000000000 | bytes 2752512 | tf_op jit(solution)/shard_map/pallas_call | solution.py:33
  29.0 1.7 %collective-permute-start.9 = (bf16[192,512]{1,0:T(8,128)(2,1)S(1)}, bf16[192,512]{1,0:T(8,128)(2,1)S(1)}, u32[]{:S(2)}, u32[]{:S(2)}) collective-permute-start(bf16[192,512]{1,0:T(8,128)(2,1)S(1)} %get-tuple-element.54), channel_id=1, source_target_pairs={{0,2},{1,3},{2,0},{3,1},{4,6},{5,7},{6,4},{7,5},{8,10},{9,11},{10,... | collective-permute-start | bytes 589832 | tf_op jit(solution)/shard_map/ppermute | solution.py:293
  30.7 5.2 %collective-permute-done.9.g_par = bf16[192,512]{1,0:T(8,128)(2,1)S(1)} collective-permute-done((bf16[192,512]{1,0:T(8,128)(2,1)S(1)}, bf16[192,512]{1,0:T(8,128)(2,1)S(1)}, u32[]{:S(2)}, u32[]{:S(2)}) %collective-permute-start.9) | collective-permute-done | bytes 196640 | tf_op jit(solution)/shard_map/ppermute | solution.py:293
  35.9 1.6 %shard_map.87 = (bf16[320,512]{1,0:T(8,128)(2,1)S(1)}, bf16[320,512]{1,0:T(8,128)(2,1)S(1)}, f32[256,512]{1,0:T(8,128)S(1)}, f32[4,512]{1,0:T(4,128)S(1)}) custom-call(bf16[512,384]{1,0:T(8,128)(2,1)S(1)} %get-tuple-element.48.h0, bf16[512,384]{1,0:T(8,128)(2,1)S(1)} %collective-permute-done.3.h1, bf16[512,384]{1,0:T(8,128)(2,1)S(1)} %collective-permute-done.4.h2, ...), custom_call_target="tpu_custom_call" | custom-call | flops 1500000000 | bytes 3538944 | tf_op jit(solution)/shard_map/pallas_call | solution.py:33
  37.5 1.5 %collective-permute-start.10 = (bf16[320,512]{1,0:T(8,128)(2,1)S(1)}, bf16[320,512]{1,0:T(8,128)(2,1)S(1)}, u32[]{:S(2)}, u32[]{:S(2)}) collective-permute-start(bf16[320,512]{1,0:T(8,128)(2,1)S(1)} %get-tuple-element.60), channel_id=1, source_target_pairs={{0,2},{1,3},{2,0},{3,1},{4,6},{5,7},{6,4},{7,5},{8,10},{9,11},{10,... | collective-permute-start | bytes 983048 | tf_op jit(solution)/shard_map/ppermute | solution.py:293
  39.0 7.3 %collective-permute-done.10.par = bf16[320,512]{1,0:T(8,128)(2,1)S(1)} collective-permute-done((bf16[320,512]{1,0:T(8,128)(2,1)S(1)}, bf16[320,512]{1,0:T(8,128)(2,1)S(1)}, u32[]{:S(2)}, u32[]{:S(2)}) %collective-permute-start.10) | collective-permute-done | bytes 327712 | tf_op jit(solution)/shard_map/ppermute | solution.py:293
  47.9 7.4 %shard_map.88 = (bf16[64,512]{1,0:T(8,128)(2,1)S(1)}, bf16[64,512]{1,0:T(8,128)(2,1)S(1)}, f32[256,1024]{1,0:T(8,128)S(1)}, bf16[256,1024]{1,0:T(8,128)(2,1)S(1)}) custom-call(bf16[320,512]{1,0:T(8,128)(2,1)S(1)} %get-tuple-element.59.own, bf16[320,512]{1,0:T(8,128)(2,1)S(1)} %collective-permute-done.10.par, ...), custom_call_target="tpu_custom_call" | custom-call | flops 8000000000 | bytes 1703936 | tf_op jit(solution)/shard_map/pallas_call | solution.py:33
  55.5 1.8 %collective-permute-done.13.kv_got = bf16[256,1024]{1,0:T(8,128)(2,1)S(1)} collective-permute-done((bf16[256,1024]{1,0:T(8,128)(2,1)S(1)}, bf16[256,1024]{1,0:T(8,128)(2,1)S(1)}, u32[]{:S(2)}, u32[]{:S(2)}) %collective-permute-start.13) | collective-permute-done | bytes 524320 | tf_op jit(solution)/shard_map/ppermute | solution.py:290
  57.4 1.3 %collective-permute-start.14 = (bf16[320,512]{1,0:T(8,128)(2,1)S(1)}, bf16[320,512]{1,0:T(8,128)(2,1)S(1)}, u32[]{:S(2)}, u32[]{:S(2)}) collective-permute-start(bf16[320,512]{1,0:T(8,128)(2,1)S(1)} %get-tuple-element.68), channel_id=1, source_target_pairs={{0,2},{1,3},{2,0},{3,1},{4,6},{5,7},{6,4},{7,5},{8,10},{9,11},{10,... | collective-permute-start | bytes 983048 | tf_op jit(solution)/shard_map/ppermute | solution.py:293
  58.6 8.6 %collective-permute-done.14.other = bf16[320,512]{1,0:T(8,128)(2,1)S(1)} collective-permute-done((bf16[320,512]{1,0:T(8,128)(2,1)S(1)}, bf16[320,512]{1,0:T(8,128)(2,1)S(1)}, u32[]{:S(2)}, u32[]{:S(2)}) %collective-permute-start.14) | collective-permute-done | bytes 327712 | tf_op jit(solution)/shard_map/ppermute | solution.py:293
  69.3 1.5 %collective-permute-start.15 = (bf16[384,512]{1,0:T(8,128)(2,1)S(1)}, bf16[384,512]{1,0:T(8,128)(2,1)S(1)}, u32[]{:S(2)}, u32[]{:S(2)}) collective-permute-start(bf16[384,512]{1,0:T(8,128)(2,1)S(1)} %get-tuple-element.72), channel_id=1, source_target_pairs={{0,4},{1,13},{2,6},{3,15},{4,0},{5,9},{6,2},{7,11},{8,12},{9,5},{1... | collective-permute-start | bytes 1179656 | tf_op jit(solution)/shard_map/ppermute | solution.py:284
  70.8 4.9 %collective-permute-done.16.got = bf16[384,512]{1,0:T(8,128)(2,1)S(1)} collective-permute-done((bf16[384,512]{1,0:T(8,128)(2,1)S(1)}, bf16[384,512]{1,0:T(8,128)(2,1)S(1)}, u32[]{:S(2)}, u32[]{:S(2)}) %collective-permute-start.16) | collective-permute-done | bytes 393248 | tf_op jit(solution)/shard_map/ppermute | solution.py:284
  75.8 1.5 %collective-permute-start.17 = (bf16[384,512]{1,0:T(8,128)(2,1)S(1)}, bf16[384,512]{1,0:T(8,128)(2,1)S(1)}, u32[]{:S(2)}, u32[]{:S(2)}) collective-permute-start(bf16[384,512]{1,0:T(8,128)(2,1)S(1)} %shard_map.93), channel_id=1, source_target_pairs={{0,12},{1,5},{2,14},{3,7},{4,8},{5,1},{6,10},{7,3},{8,4},{9,13},{1... | collective-permute-start | bytes 1179656 | tf_op jit(solution)/shard_map/ppermute | solution.py:284
  77.8 4.2 %collective-permute-done.15.alone = bf16[384,512]{1,0:T(8,128)(2,1)S(1)} collective-permute-done((bf16[384,512]{1,0:T(8,128)(2,1)S(1)}, bf16[384,512]{1,0:T(8,128)(2,1)S(1)}, u32[]{:S(2)}, u32[]{:S(2)}) %collective-permute-start.15) | collective-permute-done | bytes 393248 | tf_op jit(solution)/shard_map/ppermute | solution.py:284
  82.0 2.9 %collective-permute-done.17.joined = bf16[384,512]{1,0:T(8,128)(2,1)S(1)} collective-permute-done((bf16[384,512]{1,0:T(8,128)(2,1)S(1)}, bf16[384,512]{1,0:T(8,128)(2,1)S(1)}, u32[]{:S(2)}, u32[]{:S(2)}) %collective-permute-start.17) | collective-permute-done | bytes 393248 | tf_op jit(solution)/shard_map/ppermute | solution.py:284
  85.1 1.7 %collective-permute-done.18.g_sib = bf16[384,512]{1,0:T(8,128)(2,1)S(1)} collective-permute-done((bf16[384,512]{1,0:T(8,128)(2,1)S(1)}, bf16[384,512]{1,0:T(8,128)(2,1)S(1)}, u32[]{:S(2)}, u32[]{:S(2)}) %collective-permute-start.18) | collective-permute-done | bytes 393248 | tf_op jit(solution)/shard_map/ppermute | solution.py:290
  87.6 1.3 %collective-permute-start.20 = (bf16[576,384]{1,0:T(8,128)(2,1)S(1)}, bf16[576,384]{1,0:T(8,128)(2,1)S(1)}, u32[]{:S(2)}, u32[]{:S(2)}) collective-permute-start(bf16[576,384]{1,0:T(8,128)(2,1)S(1)} %shard_map.98), channel_id=1, source_target_pairs={{0,2},{1,19},{2,0},{3,17},{16,18},{17,3},{18,16},{19,1},{32,34},{3... | collective-permute-start | bytes 1327112 | tf_op jit(solution)/shard_map/ppermute | solution.py:287
  91.4 4.6 %collective-permute-done.20.got = bf16[576,384]{1,0:T(8,128)(2,1)S(1)} collective-permute-done((bf16[576,384]{1,0:T(8,128)(2,1)S(1)}, bf16[576,384]{1,0:T(8,128)(2,1)S(1)}, u32[]{:S(2)}, u32[]{:S(2)}) %collective-permute-start.20) | collective-permute-done | bytes 442400 | tf_op jit(solution)/shard_map/ppermute | solution.py:287
  96.0 3.2 %collective-permute-start.21 = (bf16[576,384]{1,0:T(8,128)(2,1)S(1)}, bf16[576,384]{1,0:T(8,128)(2,1)S(1)}, u32[]{:S(2)}, u32[]{:S(2)}) collective-permute-start(bf16[576,384]{1,0:T(8,128)(2,1)S(1)} %shard_map.99), channel_id=1, source_target_pairs={{0,18},{1,3},{2,16},{3,1},{16,2},{17,19},{18,0},{19,17},{32,50},{3... | collective-permute-start | bytes 1327112 | tf_op jit(solution)/shard_map/ppermute | solution.py:287
  100.0 2.3 %collective-permute-done.19.alone = bf16[576,384]{1,0:T(8,128)(2,1)S(1)} collective-permute-done((bf16[576,384]{1,0:T(8,128)(2,1)S(1)}, bf16[576,384]{1,0:T(8,128)(2,1)S(1)}, u32[]{:S(2)}, u32[]{:S(2)}) %collective-permute-start.19) | collective-permute-done | bytes 442400 | tf_op jit(solution)/shard_map/ppermute | solution.py:287
  102.3 3.7 %collective-permute-done.21.joined = bf16[576,384]{1,0:T(8,128)(2,1)S(1)} collective-permute-done((bf16[576,384]{1,0:T(8,128)(2,1)S(1)}, bf16[576,384]{1,0:T(8,128)(2,1)S(1)}, u32[]{:S(2)}, u32[]{:S(2)}) %collective-permute-start.21) | collective-permute-done | bytes 442400 | tf_op jit(solution)/shard_map/ppermute | solution.py:287
  106.1 4.0 %collective-permute-start.22 = (bf16[144,384]{1,0:T(8,128)(2,1)S(1)}, bf16[144,384]{1,0:T(8,128)(2,1)S(1)}, u32[]{:S(2)}, u32[]{:S(2)}) collective-permute-start(bf16[144,384]{1,0:T(8,128)(2,1)S(1)} %get-tuple-element.76), channel_id=1, source_target_pairs={{0,64},{1,65},{2,66},{3,67},{16,80},{17,81},{18,82},{19,83},{32,96... | collective-permute-start | bytes 331784 | tf_op jit(solution)/shard_map/ppermute | solution.py:296
  111.1 2.6 %collective-permute-done.22.r1 = bf16[144,384]{1,0:T(8,128)(2,1)S(1)} collective-permute-done((bf16[144,384]{1,0:T(8,128)(2,1)S(1)}, bf16[144,384]{1,0:T(8,128)(2,1)S(1)}, u32[]{:S(2)}, u32[]{:S(2)}) %collective-permute-start.22) | collective-permute-done | bytes 110624 | tf_op jit(solution)/shard_map/ppermute | solution.py:296
  113.7 2.3 %collective-permute-done.23.r2 = bf16[144,384]{1,0:T(8,128)(2,1)S(1)} collective-permute-done((bf16[144,384]{1,0:T(8,128)(2,1)S(1)}, bf16[144,384]{1,0:T(8,128)(2,1)S(1)}, u32[]{:S(2)}, u32[]{:S(2)}) %collective-permute-start.23) | collective-permute-done | bytes 110624 | tf_op jit(solution)/shard_map/ppermute | solution.py:296
  (58 shorter events, 17.2 us)
Async XLA Ops:
  0.0 15.0 %collective-permute-start.6 = (bf16[512,384]{1,0:T(8,128)(2,1)}, bf16[512,384]{1,0:T(8,128)(2,1)S(1)}, u32[]{:S(2)}, u32[]{:S(2)}) collective-permute-start(bf16[512,384]{1,0:T(8,128)(2,1)} %bitcast.7), channel_id=1, source_target_pairs={{0,12},{1,5},{2,14},{3,7},{4,8},{5,1},{6,10},{7,3},{8,4},{9,13},{1... | collective-permute-start | bytes 1179656 | tf_op jit(solution)/shard_map/ppermute | solution.py:284
  3.1 7.5 %collective-permute-start = (s32[32,512]{1,0:T(8,128)}, s32[32,512]{1,0:T(8,128)S(1)}, u32[]{:S(2)}, u32[]{:S(2)}) collective-permute-start(s32[32,512]{1,0:T(8,128)} %bitcast.11), channel_id=1, source_target_pairs={{0,1},{1,2},{2,3},{3,0},{4,5},{5,6},{6,7},{7,4},{8,9},{9,10},{10,1... | collective-permute-start | bytes 196616 | tf_op jit(solution)/shard_map/ppermute | solution.py:276
  3.1 7.5 %collective-permute-start.1 = (s32[32,512]{1,0:T(8,128)}, s32[32,512]{1,0:T(8,128)S(1)}, u32[]{:S(2)}, u32[]{:S(2)}) collective-permute-start(s32[32,512]{1,0:T(8,128)} %bitcast.12), channel_id=1, source_target_pairs={{1,0},{2,1},{3,2},{0,3},{5,4},{6,5},{7,6},{4,7},{9,8},{10,9},{11,1... | collective-permute-start | bytes 196616 | tf_op jit(solution)/shard_map/ppermute | solution.py:277
  4.8 14.9 %collective-permute-start.5 = (bf16[512,384]{1,0:T(8,128)(2,1)}, bf16[512,384]{1,0:T(8,128)(2,1)S(1)}, u32[]{:S(2)}, u32[]{:S(2)}) collective-permute-start(bf16[512,384]{1,0:T(8,128)(2,1)} %bitcast.8), channel_id=1, source_target_pairs={{0,4},{1,13},{2,6},{3,15},{4,0},{5,9},{6,2},{7,11},{8,12},{9,5},{1... | collective-permute-start | bytes 1179656 | tf_op jit(solution)/shard_map/ppermute | solution.py:284
  5.0 2.0 %copy-start.1 = (bf16[3,1536,384]{2,1,0:T(8,128)(2,1)S(1)}, bf16[3,1536,384]{2,1,0:T(8,128)(2,1)}, u32[]{:S(2)}) copy-start(bf16[3,1536,384]{2,1,0:T(8,128)(2,1)} %weight_hbm.1) | copy-start | bytes 10616836
  8.8 1.8 %copy-start.8 = (s32[1,512,32]{1,2,0:T(8,128)S(1)}, s32[1,512,32]{1,2,0:T(8,128)}, u32[]{:S(2)}) copy-start(s32[1,512,32]{1,2,0:T(8,128)} %param.8) | copy-start | bytes 196612
  10.6 5.3 %copy-start = (bf16[1536,384]{1,0:T(8,128)(2,1)S(1)}, bf16[1536,384]{1,0:T(8,128)(2,1)}, u32[]{:S(2)}) copy-start(bf16[1536,384]{1,0:T(8,128)(2,1)} %wv.5) | copy-start | bytes 3538948
  10.6 5.3 %copy-start.2 = (bf16[1536,128]{1,0:T(8,128)(2,1)S(1)}, bf16[1536,128]{1,0:T(8,128)(2,1)}, u32[]{:S(2)}) copy-start(bf16[1536,128]{1,0:T(8,128)(2,1)} %wq.5) | copy-start | bytes 1179652
  10.7 5.3 %copy-start.3 = (bf16[1536,128]{1,0:T(8,128)(2,1)S(1)}, bf16[1536,128]{1,0:T(8,128)(2,1)}, u32[]{:S(2)}) copy-start(bf16[1536,128]{1,0:T(8,128)(2,1)} %wk.5) | copy-start | bytes 1179652
  13.9 13.3 %collective-permute-start.4 = (bf16[512,384]{1,0:T(8,128)(2,1)S(1)}, bf16[512,384]{1,0:T(8,128)(2,1)S(1)}, u32[]{:S(2)}, u32[]{:S(2)}) collective-permute-start(bf16[512,384]{1,0:T(8,128)(2,1)S(1)} %get-tuple-element.48.h0), channel_id=1, source_target_pairs={{0,12},{1,5},{2,14},{3,7},{4,8},{5,1},{6,10},{7,3},{8,4},{9,13},{1... | collective-permute-start | bytes 1179656 | tf_op jit(solution)/shard_map/ppermute | solution.py:284
  15.0 12.2 %collective-permute-start.7 = (bf16[512,384]{1,0:T(8,128)(2,1)S(1)}, bf16[512,384]{1,0:T(8,128)(2,1)S(1)}, u32[]{:S(2)}, u32[]{:S(2)}) collective-permute-start(bf16[512,384]{1,0:T(8,128)(2,1)S(1)} %collective-permute-done.6.c2), channel_id=1, source_target_pairs={{0,4},{1,13},{2,6},{3,15},{4,0},{5,9},{6,2},{7,11},{8,12},{9,5},{1... | collective-permute-start | bytes 1179656 | tf_op jit(solution)/shard_map/ppermute | solution.py:284
  16.5 11.3 %copy-start.4 = (bf16[1,512,384]{2,1,0:T(8,128)(2,1)S(1)}, bf16[1,512,384]{2,1,0:T(8,128)(2,1)}, u32[]{:S(2)}) copy-start(bf16[1,512,384]{2,1,0:T(8,128)(2,1)} %param.15) | copy-start | bytes 1179652
  16.5 11.3 %copy-start.9 = (bf16[384,1536]{1,0:T(8,128)(2,1)S(1)}, bf16[384,1536]{1,0:T(8,128)(2,1)}, u32[]{:S(2)}) copy-start(bf16[384,1536]{1,0:T(8,128)(2,1)} %w_ref.1) | copy-start | bytes 3538948
  18.6 12.1 %collective-permute-start.3 = (bf16[512,384]{1,0:T(8,128)(2,1)S(1)}, bf16[512,384]{1,0:T(8,128)(2,1)S(1)}, u32[]{:S(2)}, u32[]{:S(2)}) collective-permute-start(bf16[512,384]{1,0:T(8,128)(2,1)S(1)} %get-tuple-element.48.h0), channel_id=1, source_target_pairs={{0,4},{1,13},{2,6},{3,15},{4,0},{5,9},{6,2},{7,11},{8,12},{9,5},{1... | collective-permute-start | bytes 1179656 | tf_op jit(solution)/shard_map/ppermute | solution.py:284
  27.2 8.7 %collective-permute-start.8 = (bf16[512,384]{1,0:T(8,128)(2,1)S(1)}, bf16[512,384]{1,0:T(8,128)(2,1)S(1)}, u32[]{:S(2)}, u32[]{:S(2)}) collective-permute-start(bf16[512,384]{1,0:T(8,128)(2,1)S(1)} %collective-permute-done.4.h2), channel_id=1, source_target_pairs={{0,4},{1,13},{2,6},{3,15},{4,0},{5,9},{6,2},{7,11},{8,12},{9,5},{1... | collective-permute-start | bytes 1179656 | tf_op jit(solution)/shard_map/ppermute | solution.py:284
  29.0 6.8 %collective-permute-start.9 = (bf16[192,512]{1,0:T(8,128)(2,1)S(1)}, bf16[192,512]{1,0:T(8,128)(2,1)S(1)}, u32[]{:S(2)}, u32[]{:S(2)}) collective-permute-start(bf16[192,512]{1,0:T(8,128)(2,1)S(1)} %get-tuple-element.54), channel_id=1, source_target_pairs={{0,2},{1,3},{2,0},{3,1},{4,6},{5,7},{6,4},{7,5},{8,10},{9,11},{10,... | collective-permute-start | bytes 589832 | tf_op jit(solution)/shard_map/ppermute | solution.py:293
  37.5 8.8 %collective-permute-start.10 = (bf16[320,512]{1,0:T(8,128)(2,1)S(1)}, bf16[320,512]{1,0:T(8,128)(2,1)S(1)}, u32[]{:S(2)}, u32[]{:S(2)}) collective-permute-start(bf16[320,512]{1,0:T(8,128)(2,1)S(1)} %get-tuple-element.60), channel_id=1, source_target_pairs={{0,2},{1,3},{2,0},{3,1},{4,6},{5,7},{6,4},{7,5},{8,10},{9,11},{10,... | collective-permute-start | bytes 983048 | tf_op jit(solution)/shard_map/ppermute | solution.py:293
  39.0 7.8 %collective-permute-start.11 = (bf16[320,512]{1,0:T(8,128)(2,1)S(1)}, bf16[320,512]{1,0:T(8,128)(2,1)S(1)}, u32[]{:S(2)}, u32[]{:S(2)}) collective-permute-start(bf16[320,512]{1,0:T(8,128)(2,1)S(1)} %get-tuple-element.59.own), channel_id=1, source_target_pairs={{0,1},{1,0},{2,3},{3,2},{4,5},{5,4},{6,7},{7,6},{8,9},{9,8},{10,11... | collective-permute-start | bytes 983048 | tf_op jit(solution)/shard_map/ppermute | solution.py:290
  46.3 1.6 %collective-permute-start.12 = (bf16[320,512]{1,0:T(8,128)(2,1)S(1)}, bf16[320,512]{1,0:T(8,128)(2,1)S(1)}, u32[]{:S(2)}, u32[]{:S(2)}) collective-permute-start(bf16[320,512]{1,0:T(8,128)(2,1)S(1)} %collective-permute-done.10.par), channel_id=1, source_target_pairs={{0,1},{1,0},{2,3},{3,2},{4,5},{5,4},{6,7},{7,6},{8,9},{9,8},{10,11... | collective-permute-start | bytes 983048 | tf_op jit(solution)/shard_map/ppermute | solution.py:290
  46.3 38.8 %collective-permute-start.2 = (bf16[2304,512]{1,0:T(8,128)(2,1)S(1)}, bf16[2304,512]{1,0:T(8,128)(2,1)S(1)}, u32[]{:S(2)}, u32[]{:S(2)}) collective-permute-start(bf16[2304,512]{1,0:T(8,128)(2,1)S(1)} %get-tuple-element.46), channel_id=1, source_target_pairs={{0,1},{1,0},{2,3},{3,2},{4,5},{5,4},{6,7},{7,6},{8,9},{9,8},{10,11... | collective-permute-start | bytes 7077896 | tf_op jit(solution)/shard_map/ppermute | solution.py:290
  55.3 2.0 %collective-permute-start.13 = (bf16[256,1024]{1,0:T(8,128)(2,1)S(1)}, bf16[256,1024]{1,0:T(8,128)(2,1)S(1)}, u32[]{:S(2)}, u32[]{:S(2)}) collective-permute-start(bf16[256,1024]{1,0:T(8,128)(2,1)S(1)} %get-tuple-element.66), channel_id=1, source_target_pairs={{0,1},{1,0},{2,3},{3,2},{4,5},{5,4},{6,7},{7,6},{8,9},{9,8},{10,11... | collective-permute-start | bytes 1572872 | tf_op jit(solution)/shard_map/ppermute | solution.py:290
  57.4 9.8 %collective-permute-start.14 = (bf16[320,512]{1,0:T(8,128)(2,1)S(1)}, bf16[320,512]{1,0:T(8,128)(2,1)S(1)}, u32[]{:S(2)}, u32[]{:S(2)}) collective-permute-start(bf16[320,512]{1,0:T(8,128)(2,1)S(1)} %get-tuple-element.68), channel_id=1, source_target_pairs={{0,2},{1,3},{2,0},{3,1},{4,6},{5,7},{6,4},{7,5},{8,10},{9,11},{10,... | collective-permute-start | bytes 983048 | tf_op jit(solution)/shard_map/ppermute | solution.py:293
  67.9 7.9 %collective-permute-start.16 = (bf16[384,512]{1,0:T(8,128)(2,1)S(1)}, bf16[384,512]{1,0:T(8,128)(2,1)S(1)}, u32[]{:S(2)}, u32[]{:S(2)}) collective-permute-start(bf16[384,512]{1,0:T(8,128)(2,1)S(1)} %get-tuple-element.74), channel_id=1, source_target_pairs={{0,4},{1,13},{2,6},{3,15},{4,0},{5,9},{6,2},{7,11},{8,12},{9,5},{1... | collective-permute-start | bytes 1179656 | tf_op jit(solution)/shard_map/ppermute | solution.py:284
  69.3 12.6 %collective-permute-start.15 = (bf16[384,512]{1,0:T(8,128)(2,1)S(1)}, bf16[384,512]{1,0:T(8,128)(2,1)S(1)}, u32[]{:S(2)}, u32[]{:S(2)}) collective-permute-start(bf16[384,512]{1,0:T(8,128)(2,1)S(1)} %get-tuple-element.72), channel_id=1, source_target_pairs={{0,4},{1,13},{2,6},{3,15},{4,0},{5,9},{6,2},{7,11},{8,12},{9,5},{1... | collective-permute-start | bytes 1179656 | tf_op jit(solution)/shard_map/ppermute | solution.py:284
  75.8 9.1 %collective-permute-start.17 = (bf16[384,512]{1,0:T(8,128)(2,1)S(1)}, bf16[384,512]{1,0:T(8,128)(2,1)S(1)}, u32[]{:S(2)}, u32[]{:S(2)}) collective-permute-start(bf16[384,512]{1,0:T(8,128)(2,1)S(1)} %shard_map.93), channel_id=1, source_target_pairs={{0,12},{1,5},{2,14},{3,7},{4,8},{5,1},{6,10},{7,3},{8,4},{9,13},{1... | collective-permute-start | bytes 1179656 | tf_op jit(solution)/shard_map/ppermute | solution.py:284
  85.0 1.8 %collective-permute-start.18 = (bf16[384,512]{1,0:T(8,128)(2,1)S(1)}, bf16[384,512]{1,0:T(8,128)(2,1)S(1)}, u32[]{:S(2)}, u32[]{:S(2)}) collective-permute-start(bf16[384,512]{1,0:T(8,128)(2,1)S(1)} %shard_map.94.g_mine), channel_id=1, source_target_pairs={{0,1},{1,0},{2,3},{3,2},{4,5},{5,4},{6,7},{7,6},{8,9},{9,8},{10,11... | collective-permute-start | bytes 1179656 | tf_op jit(solution)/shard_map/ppermute | solution.py:290
  87.6 8.4 %collective-permute-start.20 = (bf16[576,384]{1,0:T(8,128)(2,1)S(1)}, bf16[576,384]{1,0:T(8,128)(2,1)S(1)}, u32[]{:S(2)}, u32[]{:S(2)}) collective-permute-start(bf16[576,384]{1,0:T(8,128)(2,1)S(1)} %shard_map.98), channel_id=1, source_target_pairs={{0,2},{1,19},{2,0},{3,17},{16,18},{17,3},{18,16},{19,1},{32,34},{3... | collective-permute-start | bytes 1327112 | tf_op jit(solution)/shard_map/ppermute | solution.py:287
  89.6 12.6 %collective-permute-start.19 = (bf16[576,384]{1,0:T(8,128)(2,1)S(1)}, bf16[576,384]{1,0:T(8,128)(2,1)S(1)}, u32[]{:S(2)}, u32[]{:S(2)}) collective-permute-start(bf16[576,384]{1,0:T(8,128)(2,1)S(1)} %shard_map.96), channel_id=1, source_target_pairs={{0,2},{1,19},{2,0},{3,17},{16,18},{17,3},{18,16},{19,1},{32,34},{3... | collective-permute-start | bytes 1327112 | tf_op jit(solution)/shard_map/ppermute | solution.py:287
  96.0 9.9 %collective-permute-start.21 = (bf16[576,384]{1,0:T(8,128)(2,1)S(1)}, bf16[576,384]{1,0:T(8,128)(2,1)S(1)}, u32[]{:S(2)}, u32[]{:S(2)}) collective-permute-start(bf16[576,384]{1,0:T(8,128)(2,1)S(1)} %shard_map.99), channel_id=1, source_target_pairs={{0,18},{1,3},{2,16},{3,1},{16,2},{17,19},{18,0},{19,17},{32,50},{3... | collective-permute-start | bytes 1327112 | tf_op jit(solution)/shard_map/ppermute | solution.py:287
  106.1 7.6 %collective-permute-start.22 = (bf16[144,384]{1,0:T(8,128)(2,1)S(1)}, bf16[144,384]{1,0:T(8,128)(2,1)S(1)}, u32[]{:S(2)}, u32[]{:S(2)}) collective-permute-start(bf16[144,384]{1,0:T(8,128)(2,1)S(1)} %get-tuple-element.76), channel_id=1, source_target_pairs={{0,64},{1,65},{2,66},{3,67},{16,80},{17,81},{18,82},{19,83},{32,96... | collective-permute-start | bytes 331784 | tf_op jit(solution)/shard_map/ppermute | solution.py:296
  110.1 5.9 %collective-permute-start.23 = (bf16[144,384]{1,0:T(8,128)(2,1)S(1)}, bf16[144,384]{1,0:T(8,128)(2,1)S(1)}, u32[]{:S(2)}, u32[]{:S(2)}) collective-permute-start(bf16[144,384]{1,0:T(8,128)(2,1)S(1)} %get-tuple-element.77), channel_id=1, source_target_pairs={{0,32},{1,33},{2,34},{3,35},{16,48},{17,49},{18,50},{19,51},{32,0}... | collective-permute-start | bytes 331784 | tf_op jit(solution)/shard_map/ppermute | solution.py:296
  111.1 6.0 %collective-permute-start.24 = (bf16[144,384]{1,0:T(8,128)(2,1)S(1)}, bf16[144,384]{1,0:T(8,128)(2,1)S(1)}, u32[]{:S(2)}, u32[]{:S(2)}) collective-permute-start(bf16[144,384]{1,0:T(8,128)(2,1)S(1)} %get-tuple-element.78), channel_id=1, source_target_pairs={{0,96},{1,97},{2,98},{3,99},{16,112},{17,113},{18,114},{19,115},{3... | collective-permute-start | bytes 331784 | tf_op jit(solution)/shard_map/ppermute | solution.py:296
  (3 other events, 3.6 us)

commit v4 on v3

--- a/solution.py
+++ b/solution.py
@@ -120,11 +120,20 @@
     return (0, own), (one, first), (two, second), (2, far)
 
 
-def project_kernel(h0, h1, h2, h3, w_ref, mine_ref, other_ref, unit_ref, factor_ref, values):
+def project_part_kernel(own, second, w_ref, out_ref):
+    y = lax.axis_index("tensor")
+    _, two = distances()
+    out_ref[...] = nt(w_ref[:, block_at(y, 384)], own[...]) + nt(
+        w_ref[:, block_at(y ^ two, 384)], second[...]
+    )
+
+
+def project_kernel(part, first, far, w_ref, mine_ref, other_ref, unit_ref, factor_ref, values):
     y = lax.axis_index("tensor")
     chip, _ = own_chip()
-    total = 0.0
-    for d, ref in gathered((h0, h1, h2, h3)):
+    one, _ = distances()
+    total = part[...]
+    for d, ref in ((one, first), (2, far)):
         total = total + nt(w_ref[:, block_at(y ^ d, 384)], ref[...])
     for g in range(4):
         raw = total[g * KEY : (g + 1) * KEY]
@@ -247,6 +256,18 @@
     return x, z
 
 
+def tap_own_kernel(taps, grad, out_ref):
+    x, _ = ring_place()
+    for i, d in enumerate((2, distances()[0])):
+        out_ref[i] = nt(taps[block_at(x ^ d, 576)], grad[...])
+
+
+def tap_add_kernel(index, own, taps, grad, out_ref):
+    x, _ = ring_place()
+    d = (2, distances()[0])[index]
+    out_ref[...] = (own[index] + nt(taps[block_at(x ^ d, 576)], grad[...])).astype(bf16)
+
+
 def tap_kernel(which, t_mine, t_sib, g_mine, g_sib, out_ref):
     x, _ = ring_place()
     d = (0, *distances(), 2)[which]
@@ -321,14 +342,16 @@
     far = y_way(second, 0)
     g_own, g_other = call(grad_kernel, [((VAL, rows), bf16)] * 2, *cots, out_w, flops=1e9)
     g_par = over_chip(g_other)
-    first, second, far, g_par, g_own = lax.optimization_barrier((first, second, far, g_par, g_own))
+    (part,) = call(project_part_kernel, [((640, rows), f32)], hidden, second, w_t, flops=7e8)
+    first, far, part = lax.optimization_barrier((first, far, part))
 
     own, other, unit, factor = call(
         project_kernel,
         [((320, rows), bf16)] * 2 + [((256, rows), f32), ((4, rows), f32)],
-        hidden, first, second, far, w_t,
+        part, first, far, w_t,
         scratch=[pltpu.VMEM((384, rows), bf16)], flops=1.5e9,
     )
+    other, g_par, g_own = lax.optimization_barrier((other, g_par, g_own))
     par = over_chip(other)
     sib_own = over_core(own)
     sib_par = over_core(par)
@@ -373,8 +396,16 @@
             taps_mine, taps_sib, hg, hg_sib, flops=6e8,
         )[0]
 
-    got = x_way(product(3, bf16), 0)
-    alone = x_way(product(1, bf16), 0)
+    (parts,) = call(tap_own_kernel, [((2, 576, 384), f32)], taps_mine, hg, flops=6e8)
+    hg_sib, parts = lax.optimization_barrier((hg_sib, parts))
+    far, near = [
+        call(
+            functools.partial(tap_add_kernel, i), [((576, 384), bf16)], parts, taps_sib, hg_sib, flops=3e8
+        )[0]
+        for i in range(2)
+    ]
+    got = x_way(far, 0)
+    alone = x_way(near, 0)
     joined = product(2, f32)
     part = product(0, f32)
     (joined,) = call(add_kernel, [((576, 384), bf16)], joined, got)

time: 118 us -> 116 us (0.983)
  waiting for transfers between devices: 61.5 us -> 58.5 us
    ppermute x3, waiting for transfers between devices: 21 us -> 17.4 us  [over_chip(): return lax.ppermute(value, 'section', [(i, i ^ 2) for i in range(4)])]
    ppermute x1, starting transfers between devices: 1.74 us -> 0.01 us  [body(): high = lax.ppermute(marks, 'section', [((i + 1) % 4, i) for i in range(4)])]
    ppermute x9, starting transfers between devices: 10.8 us -> 12.5 us  [y_way(): return lax.ppermute(value, ('tensor', 'section'), pairs)]
    pallas_call x20 -> x22, Pallas kernels: 24.1 us -> 24.5 us  [call(): pl.pallas_call(kernel, out_shape=[jax.ShapeDtypeStruct(shape, kind) for s...]
  transfers between devices with their start and end apart: 25 -> 25, of which waited for: 16 -> 17; matrix products, arithmetic and copies ran while one was open for 0% -> 0% of each run, Pallas kernels for 18% -> 20%
where the time goes in v4:
time: 116 us
  waiting for transfers between devices  58.5 us (50%)
  starting transfers between devices  28.8 us (25%)
  Pallas kernels  24.5 us (21%)
  local copies, waits for them, and re-layouts  3.87 us (3%)
    pallas_call x22, Pallas kernels, call(): pl.pallas_call(kernel, out_shape=[jax.ShapeDtypeStruct(shape, kind) for s...  24.5 us
    ppermute x9, waiting for transfers between devices, y_way(): return lax.ppermute(value, ('tensor', 'section'), pairs)  20.3 us
    ppermute x3, waiting for transfers between devices, over_chip(): return lax.ppermute(value, 'section', [(i, i ^ 2) for i in range(4)])  17.4 us
    ppermute x9, starting transfers between devices, y_way(): return lax.ppermute(value, ('tensor', 'section'), pairs)  12.5 us
    ppermute x3, waiting for transfers between devices, x_way(): lax.ppermute(value, flat, [(i, i ^ 2 * (1, 3)[(i + way) % 2]) for i in ra...  11.1 us
    ppermute x3, waiting for transfers between devices, over_z(): return lax.ppermute(value, flat, [(i, i ^ 8 * d) for i in range(32)])  5.95 us
    ppermute x3, starting transfers between devices, x_way(): lax.ppermute(value, flat, [(i, i ^ 2 * (1, 3)[(i + way) % 2]) for i in ra...  5.03 us
    ppermute x3, starting transfers between devices, over_z(): return lax.ppermute(value, flat, [(i, i ^ 8 * d) for i in range(32)])  4.99 us
  transfers between devices with their start and end apart: 25, of which 17 were waited for; matrix products, arithmetic and copies ran while one was open for 0% of the time, Pallas kernels for 20%

profile of v4, /device:TPU:0, one launch (start us, length us, event | category | flops | bytes accessed | tf_op | source)
XLA Modules:
  0.0 115.9 jit_solution(5402756825245231034)
XLA Ops:
  0.0 3.1 %collective-permute-start.6 = (bf16[512,384]{1,0:T(8,128)(2,1)}, bf16[512,384]{1,0:T(8,128)(2,1)S(1)}, u32[]{:S(2)}, u32[]{:S(2)}) collective-permute-start(bf16[512,384]{1,0:T(8,128)(2,1)} %bitcast.7), channel_id=1, source_target_pairs={{0,12},{1,5},{2,14},{3,7},{4,8},{5,1},{6,10},{7,3},{8,4},{9,13},{1... | collective-permute-start | bytes 1179656 | tf_op jit(solution)/shard_map/ppermute | solution.py:305
  3.8 2.0 %copy-done.1 = bf16[3,1536,384]{2,1,0:T(8,128)(2,1)S(1)} copy-done((bf16[3,1536,384]{2,1,0:T(8,128)(2,1)S(1)}, bf16[3,1536,384]{2,1,0:T(8,128)(2,1)}, u32[]{:S(2)}) %copy-start.1) | copy-done | bytes 3538968
  7.6 1.8 %shard_map.82 = (bf16[512,1536]{1,0:T(8,128)(2,1)S(1)}, bf16[3,1536,384]{2,1,0:T(8,128)(2,1)S(1)}) custom-call(s32[32,512]{1,0:T(8,128)S(1)} %bitcast.13, bf16[128,1536]{1,0:T(8,128)(2,1)S(1)} %copy-done.5, bf16[3,1536,384]{2,1,0:T(8,128)(2,1)S(1)} %copy-done.1), custom_call_target="tpu_custom_call" | custom-call | flops 400000000 | bytes 3997696 | tf_op jit(solution)/shard_map/pallas_call | solution.py:33
  9.4 3.2 %shard_map.83 = (bf16[512,384]{1,0:T(8,128)(2,1)S(1)}, bf16[576,1536]{1,0:T(8,128)(2,1)S(1)}) custom-call(s32[32,512]{1,0:T(8,128)S(1)} %bitcast.14, s32[32,512]{1,0:T(8,128)S(1)} %collective-permute-done.low_ref, s32[32,512]{1,0:T(8,128)S(1)} %collective-permute-done.1.high_ref, bf16[128,1536]{1,0:T(8,128)(2,1)S(1)} %copy-done.6, ...), custom_call_target="tpu_custom_call" | custom-call | flops 2000000000 | bytes 5701632 | tf_op jit(solution)/shard_map/pallas_call | solution.py:33
  12.6 2.1 %collective-permute-start.4 = (bf16[512,384]{1,0:T(8,128)(2,1)S(1)}, bf16[512,384]{1,0:T(8,128)(2,1)S(1)}, u32[]{:S(2)}, u32[]{:S(2)}) collective-permute-start(bf16[512,384]{1,0:T(8,128)(2,1)S(1)} %get-tuple-element.51.own), channel_id=1, source_target_pairs={{0,12},{1,5},{2,14},{3,7},{4,8},{5,1},{6,10},{7,3},{8,4},{9,13},{1... | collective-permute-start | bytes 1179656 | tf_op jit(solution)/shard_map/ppermute | solution.py:305
  15.5 2.1 %shard_map.84 = (bf16[2304,512]{1,0:T(8,128)(2,1)S(1)}, bf16[2304,512]{1,0:T(8,128)(2,1)S(1)}) custom-call(bf16[576,1536]{1,0:T(8,128)(2,1)S(1)} %get-tuple-element.47.ext_ref), custom_call_target="tpu_custom_call" | custom-call | flops 3000000000 | bytes 1769472 | tf_op jit(solution)/shard_map/pallas_call | solution.py:33
  17.6 2.0 %collective-permute-start.3 = (bf16[512,384]{1,0:T(8,128)(2,1)S(1)}, bf16[512,384]{1,0:T(8,128)(2,1)S(1)}, u32[]{:S(2)}, u32[]{:S(2)}) collective-permute-start(bf16[512,384]{1,0:T(8,128)(2,1)S(1)} %get-tuple-element.51.own), channel_id=1, source_target_pairs={{0,4},{1,13},{2,6},{3,15},{4,0},{5,9},{6,2},{7,11},{8,12},{9,5},{1... | collective-permute-start | bytes 1179656 | tf_op jit(solution)/shard_map/ppermute | solution.py:305
  19.5 5.9 %collective-permute-done.4.second = bf16[512,384]{1,0:T(8,128)(2,1)S(1)} collective-permute-done((bf16[512,384]{1,0:T(8,128)(2,1)S(1)}, bf16[512,384]{1,0:T(8,128)(2,1)S(1)}, u32[]{:S(2)}, u32[]{:S(2)}) %collective-permute-start.4) | collective-permute-done | bytes 393248 | tf_op jit(solution)/shard_map/ppermute | solution.py:305
  26.2 1.2 %shard_map.88 = (bf16[192,512]{1,0:T(8,128)(2,1)S(1)}, bf16[192,512]{1,0:T(8,128)(2,1)S(1)}) custom-call(bf16[512,384]{1,0:T(8,128)(2,1)S(1)} %bitcast.9, bf16[512,384]{1,0:T(8,128)(2,1)S(1)} %collective-permute-done.5.c1, bf16[512,384]{1,0:T(8,128)(2,1)S(1)} %collective-permute-done.6.c2, bf16[512,384]{1,0:T(8,128)(2,1)S(1)} %collective-permute-done.7.c3, ...), custom_call_target="tpu_custom_call" | custom-call | flops 1000000000 | bytes 2752512 | tf_op jit(solution)/shard_map/pallas_call | solution.py:33
  27.5 1.9 %collective-permute-start.9 = (bf16[192,512]{1,0:T(8,128)(2,1)S(1)}, bf16[192,512]{1,0:T(8,128)(2,1)S(1)}, u32[]{:S(2)}, u32[]{:S(2)}) collective-permute-start(bf16[192,512]{1,0:T(8,128)(2,1)S(1)} %get-tuple-element.62), channel_id=1, source_target_pairs={{0,2},{1,3},{2,0},{3,1},{4,6},{5,7},{6,4},{7,5},{8,10},{9,11},{10,... | collective-permute-start | bytes 589832 | tf_op jit(solution)/shard_map/ppermute | solution.py:314
  30.3 3.0 %collective-permute-done.8.far = bf16[512,384]{1,0:T(8,128)(2,1)S(1)} collective-permute-done((bf16[512,384]{1,0:T(8,128)(2,1)S(1)}, bf16[512,384]{1,0:T(8,128)(2,1)S(1)}, u32[]{:S(2)}, u32[]{:S(2)}) %collective-permute-start.8) | collective-permute-done | bytes 393248 | tf_op jit(solution)/shard_map/ppermute | solution.py:305
  35.0 1.1 collective-permute-start.10
  36.4 8.4 %collective-permute-done.10.par = bf16[320,512]{1,0:T(8,128)(2,1)S(1)} collective-permute-done((bf16[320,512]{1,0:T(8,128)(2,1)S(1)}, bf16[320,512]{1,0:T(8,128)(2,1)S(1)}, u32[]{:S(2)}, u32[]{:S(2)}) %collective-permute-start.10) | collective-permute-done | bytes 327712 | tf_op jit(solution)/shard_map/ppermute | solution.py:314
  45.4 1.1 collective-permute-done.12.sib_par
  46.5 7.4 %shard_map.89 = (bf16[64,512]{1,0:T(8,128)(2,1)S(1)}, bf16[64,512]{1,0:T(8,128)(2,1)S(1)}, f32[256,1024]{1,0:T(8,128)S(1)}, bf16[256,1024]{1,0:T(8,128)(2,1)S(1)}) custom-call(bf16[320,512]{1,0:T(8,128)(2,1)S(1)} %get-tuple-element.56.own, bf16[320,512]{1,0:T(8,128)(2,1)S(1)} %collective-permute-done.10.par, ...), custom_call_target="tpu_custom_call" | custom-call | flops 8000000000 | bytes 1703936 | tf_op jit(solution)/shard_map/pallas_call | solution.py:33
  54.1 1.8 %collective-permute-done.13.kv_got = bf16[256,1024]{1,0:T(8,128)(2,1)S(1)} collective-permute-done((bf16[256,1024]{1,0:T(8,128)(2,1)S(1)}, bf16[256,1024]{1,0:T(8,128)(2,1)S(1)}, u32[]{:S(2)}, u32[]{:S(2)}) %collective-permute-start.13) | collective-permute-done | bytes 524320 | tf_op jit(solution)/shard_map/ppermute | solution.py:311
  55.9 1.6 %collective-permute-start.14 = (bf16[320,512]{1,0:T(8,128)(2,1)S(1)}, bf16[320,512]{1,0:T(8,128)(2,1)S(1)}, u32[]{:S(2)}, u32[]{:S(2)}) collective-permute-start(bf16[320,512]{1,0:T(8,128)(2,1)S(1)} %get-tuple-element.72), channel_id=1, source_target_pairs={{0,2},{1,3},{2,0},{3,1},{4,6},{5,7},{6,4},{7,5},{8,10},{9,11},{10,... | collective-permute-start | bytes 983048 | tf_op jit(solution)/shard_map/ppermute | solution.py:314
  57.5 8.3 %collective-permute-done.14.other = bf16[320,512]{1,0:T(8,128)(2,1)S(1)} collective-permute-done((bf16[320,512]{1,0:T(8,128)(2,1)S(1)}, bf16[320,512]{1,0:T(8,128)(2,1)S(1)}, u32[]{:S(2)}, u32[]{:S(2)}) %collective-permute-start.14) | collective-permute-done | bytes 327712 | tf_op jit(solution)/shard_map/ppermute | solution.py:314
  68.0 1.3 %collective-permute-start.15 = (bf16[384,512]{1,0:T(8,128)(2,1)S(1)}, bf16[384,512]{1,0:T(8,128)(2,1)S(1)}, u32[]{:S(2)}, u32[]{:S(2)}) collective-permute-start(bf16[384,512]{1,0:T(8,128)(2,1)S(1)} %get-tuple-element.76), channel_id=1, source_target_pairs={{0,4},{1,13},{2,6},{3,15},{4,0},{5,9},{6,2},{7,11},{8,12},{9,5},{1... | collective-permute-start | bytes 1179656 | tf_op jit(solution)/shard_map/ppermute | solution.py:305
  69.4 4.9 %collective-permute-done.16.got = bf16[384,512]{1,0:T(8,128)(2,1)S(1)} collective-permute-done((bf16[384,512]{1,0:T(8,128)(2,1)S(1)}, bf16[384,512]{1,0:T(8,128)(2,1)S(1)}, u32[]{:S(2)}, u32[]{:S(2)}) %collective-permute-start.16) | collective-permute-done | bytes 393248 | tf_op jit(solution)/shard_map/ppermute | solution.py:305
  74.3 2.1 %collective-permute-start.17 = (bf16[384,512]{1,0:T(8,128)(2,1)S(1)}, bf16[384,512]{1,0:T(8,128)(2,1)S(1)}, u32[]{:S(2)}, u32[]{:S(2)}) collective-permute-start(bf16[384,512]{1,0:T(8,128)(2,1)S(1)} %shard_map.94), channel_id=1, source_target_pairs={{0,12},{1,5},{2,14},{3,7},{4,8},{5,1},{6,10},{7,3},{8,4},{9,13},{1... | collective-permute-start | bytes 1179656 | tf_op jit(solution)/shard_map/ppermute | solution.py:305
  76.9 3.6 %collective-permute-done.15.alone = bf16[384,512]{1,0:T(8,128)(2,1)S(1)} collective-permute-done((bf16[384,512]{1,0:T(8,128)(2,1)S(1)}, bf16[384,512]{1,0:T(8,128)(2,1)S(1)}, u32[]{:S(2)}, u32[]{:S(2)}) %collective-permute-start.15) | collective-permute-done | bytes 393248 | tf_op jit(solution)/shard_map/ppermute | solution.py:305
  80.5 2.9 %collective-permute-done.17.joined = bf16[384,512]{1,0:T(8,128)(2,1)S(1)} collective-permute-done((bf16[384,512]{1,0:T(8,128)(2,1)S(1)}, bf16[384,512]{1,0:T(8,128)(2,1)S(1)}, u32[]{:S(2)}, u32[]{:S(2)}) %collective-permute-start.17) | collective-permute-done | bytes 393248 | tf_op jit(solution)/shard_map/ppermute | solution.py:305
  85.9 1.6 %collective-permute-start.20 = (bf16[576,384]{1,0:T(8,128)(2,1)S(1)}, bf16[576,384]{1,0:T(8,128)(2,1)S(1)}, u32[]{:S(2)}, u32[]{:S(2)}) collective-permute-start(bf16[576,384]{1,0:T(8,128)(2,1)S(1)} %shard_map.100), channel_id=1, source_target_pairs={{0,2},{1,19},{2,0},{3,17},{16,18},{17,3},{18,16},{19,1},{32,34},{3... | collective-permute-start | bytes 1327112 | tf_op jit(solution)/shard_map/ppermute | solution.py:308
  89.3 4.9 %collective-permute-done.20.got = bf16[576,384]{1,0:T(8,128)(2,1)S(1)} collective-permute-done((bf16[576,384]{1,0:T(8,128)(2,1)S(1)}, bf16[576,384]{1,0:T(8,128)(2,1)S(1)}, u32[]{:S(2)}, u32[]{:S(2)}) %collective-permute-start.20) | collective-permute-done | bytes 442400 | tf_op jit(solution)/shard_map/ppermute | solution.py:308
  94.3 2.8 %collective-permute-start.21 = (bf16[576,384]{1,0:T(8,128)(2,1)S(1)}, bf16[576,384]{1,0:T(8,128)(2,1)S(1)}, u32[]{:S(2)}, u32[]{:S(2)}) collective-permute-start(bf16[576,384]{1,0:T(8,128)(2,1)S(1)} %shard_map.101), channel_id=1, source_target_pairs={{0,18},{1,3},{2,16},{3,1},{16,2},{17,19},{18,0},{19,17},{32,50},{3... | collective-permute-start | bytes 1327112 | tf_op jit(solution)/shard_map/ppermute | solution.py:308
  98.0 2.7 %collective-permute-done.19.alone = bf16[576,384]{1,0:T(8,128)(2,1)S(1)} collective-permute-done((bf16[576,384]{1,0:T(8,128)(2,1)S(1)}, bf16[576,384]{1,0:T(8,128)(2,1)S(1)}, u32[]{:S(2)}, u32[]{:S(2)}) %collective-permute-start.19) | collective-permute-done | bytes 442400 | tf_op jit(solution)/shard_map/ppermute | solution.py:308
  100.7 3.4 %collective-permute-done.21.joined = bf16[576,384]{1,0:T(8,128)(2,1)S(1)} collective-permute-done((bf16[576,384]{1,0:T(8,128)(2,1)S(1)}, bf16[576,384]{1,0:T(8,128)(2,1)S(1)}, u32[]{:S(2)}, u32[]{:S(2)}) %collective-permute-start.21) | collective-permute-done | bytes 442400 | tf_op jit(solution)/shard_map/ppermute | solution.py:308
  104.2 4.0 %collective-permute-start.22 = (bf16[144,384]{1,0:T(8,128)(2,1)S(1)}, bf16[144,384]{1,0:T(8,128)(2,1)S(1)}, u32[]{:S(2)}, u32[]{:S(2)}) collective-permute-start(bf16[144,384]{1,0:T(8,128)(2,1)S(1)} %get-tuple-element.82), channel_id=1, source_target_pairs={{0,64},{1,65},{2,66},{3,67},{16,80},{17,81},{18,82},{19,83},{32,96... | collective-permute-start | bytes 331784 | tf_op jit(solution)/shard_map/ppermute | solution.py:317
  108.2 1.0 collective-permute-start.23
  109.2 2.7 %collective-permute-done.22.r1 = bf16[144,384]{1,0:T(8,128)(2,1)S(1)} collective-permute-done((bf16[144,384]{1,0:T(8,128)(2,1)S(1)}, bf16[144,384]{1,0:T(8,128)(2,1)S(1)}, u32[]{:S(2)}, u32[]{:S(2)}) %collective-permute-start.22) | collective-permute-done | bytes 110624 | tf_op jit(solution)/shard_map/ppermute | solution.py:317
  112.0 2.3 %collective-permute-done.23.r2 = bf16[144,384]{1,0:T(8,128)(2,1)S(1)} collective-permute-done((bf16[144,384]{1,0:T(8,128)(2,1)S(1)}, bf16[144,384]{1,0:T(8,128)(2,1)S(1)}, u32[]{:S(2)}, u32[]{:S(2)}) %collective-permute-start.23) | collective-permute-done | bytes 110624 | tf_op jit(solution)/shard_map/ppermute | solution.py:317
  (60 shorter events, 17.5 us)
Async XLA Ops:
  0.0 14.7 %collective-permute-start.6 = (bf16[512,384]{1,0:T(8,128)(2,1)}, bf16[512,384]{1,0:T(8,128)(2,1)S(1)}, u32[]{:S(2)}, u32[]{:S(2)}) collective-permute-start(bf16[512,384]{1,0:T(8,128)(2,1)} %bitcast.7), channel_id=1, source_target_pairs={{0,12},{1,5},{2,14},{3,7},{4,8},{5,1},{6,10},{7,3},{8,4},{9,13},{1... | collective-permute-start | bytes 1179656 | tf_op jit(solution)/shard_map/ppermute | solution.py:305
  3.1 6.3 %collective-permute-start.1 = (s32[32,512]{1,0:T(8,128)}, s32[32,512]{1,0:T(8,128)S(1)}, u32[]{:S(2)}, u32[]{:S(2)}) collective-permute-start(s32[32,512]{1,0:T(8,128)} %bitcast.11), channel_id=1, source_target_pairs={{1,0},{2,1},{3,2},{0,3},{5,4},{6,5},{7,6},{4,7},{9,8},{10,9},{11,1... | collective-permute-start | bytes 196616 | tf_op jit(solution)/shard_map/ppermute | solution.py:298
  3.1 6.3 %collective-permute-start = (s32[32,512]{1,0:T(8,128)}, s32[32,512]{1,0:T(8,128)S(1)}, u32[]{:S(2)}, u32[]{:S(2)}) collective-permute-start(s32[32,512]{1,0:T(8,128)} %bitcast.12), channel_id=1, source_target_pairs={{0,1},{1,2},{2,3},{3,0},{4,5},{5,6},{6,7},{7,4},{8,9},{9,10},{10,1... | collective-permute-start | bytes 196616 | tf_op jit(solution)/shard_map/ppermute | solution.py:297
  3.6 15.9 %collective-permute-start.5 = (bf16[512,384]{1,0:T(8,128)(2,1)}, bf16[512,384]{1,0:T(8,128)(2,1)S(1)}, u32[]{:S(2)}, u32[]{:S(2)}) collective-permute-start(bf16[512,384]{1,0:T(8,128)(2,1)} %bitcast.8), channel_id=1, source_target_pairs={{0,4},{1,13},{2,6},{3,15},{4,0},{5,9},{6,2},{7,11},{8,12},{9,5},{1... | collective-permute-start | bytes 1179656 | tf_op jit(solution)/shard_map/ppermute | solution.py:305
  3.7 2.0 %copy-start.1 = (bf16[3,1536,384]{2,1,0:T(8,128)(2,1)S(1)}, bf16[3,1536,384]{2,1,0:T(8,128)(2,1)}, u32[]{:S(2)}) copy-start(bf16[3,1536,384]{2,1,0:T(8,128)(2,1)} %weight_hbm.1) | copy-start | bytes 10616836
  7.6 1.8 %copy-start.8 = (s32[1,512,32]{1,2,0:T(8,128)S(1)}, s32[1,512,32]{1,2,0:T(8,128)}, u32[]{:S(2)}) copy-start(s32[1,512,32]{1,2,0:T(8,128)} %param.8) | copy-start | bytes 196612
  9.4 5.5 %copy-start = (bf16[1536,384]{1,0:T(8,128)(2,1)S(1)}, bf16[1536,384]{1,0:T(8,128)(2,1)}, u32[]{:S(2)}) copy-start(bf16[1536,384]{1,0:T(8,128)(2,1)} %wv.5) | copy-start | bytes 3538948
  9.4 5.5 %copy-start.2 = (bf16[1536,128]{1,0:T(8,128)(2,1)S(1)}, bf16[1536,128]{1,0:T(8,128)(2,1)}, u32[]{:S(2)}) copy-start(bf16[1536,128]{1,0:T(8,128)(2,1)} %wq.5) | copy-start | bytes 1179652
  9.4 5.5 %copy-start.3 = (bf16[1536,128]{1,0:T(8,128)(2,1)S(1)}, bf16[1536,128]{1,0:T(8,128)(2,1)}, u32[]{:S(2)}) copy-start(bf16[1536,128]{1,0:T(8,128)(2,1)} %wk.5) | copy-start | bytes 1179652
  12.6 12.8 %collective-permute-start.4 = (bf16[512,384]{1,0:T(8,128)(2,1)S(1)}, bf16[512,384]{1,0:T(8,128)(2,1)S(1)}, u32[]{:S(2)}, u32[]{:S(2)}) collective-permute-start(bf16[512,384]{1,0:T(8,128)(2,1)S(1)} %get-tuple-element.51.own), channel_id=1, source_target_pairs={{0,12},{1,5},{2,14},{3,7},{4,8},{5,1},{6,10},{7,3},{8,4},{9,13},{1... | collective-permute-start | bytes 1179656 | tf_op jit(solution)/shard_map/ppermute | solution.py:305
  14.7 10.7 %collective-permute-start.7 = (bf16[512,384]{1,0:T(8,128)(2,1)S(1)}, bf16[512,384]{1,0:T(8,128)(2,1)S(1)}, u32[]{:S(2)}, u32[]{:S(2)}) collective-permute-start(bf16[512,384]{1,0:T(8,128)(2,1)S(1)} %collective-permute-done.6.c2), channel_id=1, source_target_pairs={{0,4},{1,13},{2,6},{3,15},{4,0},{5,9},{6,2},{7,11},{8,12},{9,5},{1... | collective-permute-start | bytes 1179656 | tf_op jit(solution)/shard_map/ppermute | solution.py:305
  15.5 10.8 %copy-start.4 = (bf16[1,512,384]{2,1,0:T(8,128)(2,1)S(1)}, bf16[1,512,384]{2,1,0:T(8,128)(2,1)}, u32[]{:S(2)}) copy-start(bf16[1,512,384]{2,1,0:T(8,128)(2,1)} %param.15) | copy-start | bytes 1179652
  15.5 10.7 %copy-start.9 = (bf16[384,1536]{1,0:T(8,128)(2,1)S(1)}, bf16[384,1536]{1,0:T(8,128)(2,1)}, u32[]{:S(2)}) copy-start(bf16[384,1536]{1,0:T(8,128)(2,1)} %w_ref.1) | copy-start | bytes 3538948
  17.6 12.7 %collective-permute-start.3 = (bf16[512,384]{1,0:T(8,128)(2,1)S(1)}, bf16[512,384]{1,0:T(8,128)(2,1)S(1)}, u32[]{:S(2)}, u32[]{:S(2)}) collective-permute-start(bf16[512,384]{1,0:T(8,128)(2,1)S(1)} %get-tuple-element.51.own), channel_id=1, source_target_pairs={{0,4},{1,13},{2,6},{3,15},{4,0},{5,9},{6,2},{7,11},{8,12},{9,5},{1... | collective-permute-start | bytes 1179656 | tf_op jit(solution)/shard_map/ppermute | solution.py:305
  25.4 7.8 %collective-permute-start.8 = (bf16[512,384]{1,0:T(8,128)(2,1)S(1)}, bf16[512,384]{1,0:T(8,128)(2,1)S(1)}, u32[]{:S(2)}, u32[]{:S(2)}) collective-permute-start(bf16[512,384]{1,0:T(8,128)(2,1)S(1)} %collective-permute-done.4.second), channel_id=1, source_target_pairs={{0,4},{1,13},{2,6},{3,15},{4,0},{5,9},{6,2},{7,11},{8,12},{9,5},{1... | collective-permute-start | bytes 1179656 | tf_op jit(solution)/shard_map/ppermute | solution.py:305
  27.5 7.6 %collective-permute-start.9 = (bf16[192,512]{1,0:T(8,128)(2,1)S(1)}, bf16[192,512]{1,0:T(8,128)(2,1)S(1)}, u32[]{:S(2)}, u32[]{:S(2)}) collective-permute-start(bf16[192,512]{1,0:T(8,128)(2,1)S(1)} %get-tuple-element.62), channel_id=1, source_target_pairs={{0,2},{1,3},{2,0},{3,1},{4,6},{5,7},{6,4},{7,5},{8,10},{9,11},{10,... | collective-permute-start | bytes 589832 | tf_op jit(solution)/shard_map/ppermute | solution.py:314
  35.0 9.8 %collective-permute-start.10 = (bf16[320,512]{1,0:T(8,128)(2,1)S(1)}, bf16[320,512]{1,0:T(8,128)(2,1)S(1)}, u32[]{:S(2)}, u32[]{:S(2)}) collective-permute-start(bf16[320,512]{1,0:T(8,128)(2,1)S(1)} %get-tuple-element.64), channel_id=1, source_target_pairs={{0,2},{1,3},{2,0},{3,1},{4,6},{5,7},{6,4},{7,5},{8,10},{9,11},{10,... | collective-permute-start | bytes 983048 | tf_op jit(solution)/shard_map/ppermute | solution.py:314
  36.1 9.2 %collective-permute-start.11 = (bf16[320,512]{1,0:T(8,128)(2,1)S(1)}, bf16[320,512]{1,0:T(8,128)(2,1)S(1)}, u32[]{:S(2)}, u32[]{:S(2)}) collective-permute-start(bf16[320,512]{1,0:T(8,128)(2,1)S(1)} %get-tuple-element.56.own), channel_id=1, source_target_pairs={{0,1},{1,0},{2,3},{3,2},{4,5},{5,4},{6,7},{7,6},{8,9},{9,8},{10,11... | collective-permute-start | bytes 983048 | tf_op jit(solution)/shard_map/ppermute | solution.py:311
  44.8 1.6 %collective-permute-start.12 = (bf16[320,512]{1,0:T(8,128)(2,1)S(1)}, bf16[320,512]{1,0:T(8,128)(2,1)S(1)}, u32[]{:S(2)}, u32[]{:S(2)}) collective-permute-start(bf16[320,512]{1,0:T(8,128)(2,1)S(1)} %collective-permute-done.10.par), channel_id=1, source_target_pairs={{0,1},{1,0},{2,3},{3,2},{4,5},{5,4},{6,7},{7,6},{8,9},{9,8},{10,11... | collective-permute-start | bytes 983048 | tf_op jit(solution)/shard_map/ppermute | solution.py:311
  44.8 40.5 %collective-permute-start.2 = (bf16[2304,512]{1,0:T(8,128)(2,1)S(1)}, bf16[2304,512]{1,0:T(8,128)(2,1)S(1)}, u32[]{:S(2)}, u32[]{:S(2)}) collective-permute-start(bf16[2304,512]{1,0:T(8,128)(2,1)S(1)} %get-tuple-element.49), channel_id=1, source_target_pairs={{0,1},{1,0},{2,3},{3,2},{4,5},{5,4},{6,7},{7,6},{8,9},{9,8},{10,11... | collective-permute-start | bytes 7077896 | tf_op jit(solution)/shard_map/ppermute | solution.py:311
  53.8 2.0 %collective-permute-start.13 = (bf16[256,1024]{1,0:T(8,128)(2,1)S(1)}, bf16[256,1024]{1,0:T(8,128)(2,1)S(1)}, u32[]{:S(2)}, u32[]{:S(2)}) collective-permute-start(bf16[256,1024]{1,0:T(8,128)(2,1)S(1)} %get-tuple-element.70), channel_id=1, source_target_pairs={{0,1},{1,0},{2,3},{3,2},{4,5},{5,4},{6,7},{7,6},{8,9},{9,8},{10,11... | collective-permute-start | bytes 1572872 | tf_op jit(solution)/shard_map/ppermute | solution.py:311
  55.9 9.8 %collective-permute-start.14 = (bf16[320,512]{1,0:T(8,128)(2,1)S(1)}, bf16[320,512]{1,0:T(8,128)(2,1)S(1)}, u32[]{:S(2)}, u32[]{:S(2)}) collective-permute-start(bf16[320,512]{1,0:T(8,128)(2,1)S(1)} %get-tuple-element.72), channel_id=1, source_target_pairs={{0,2},{1,3},{2,0},{3,1},{4,6},{5,7},{6,4},{7,5},{8,10},{9,11},{10,... | collective-permute-start | bytes 983048 | tf_op jit(solution)/shard_map/ppermute | solution.py:314
  66.4 7.9 %collective-permute-start.16 = (bf16[384,512]{1,0:T(8,128)(2,1)S(1)}, bf16[384,512]{1,0:T(8,128)(2,1)S(1)}, u32[]{:S(2)}, u32[]{:S(2)}) collective-permute-start(bf16[384,512]{1,0:T(8,128)(2,1)S(1)} %get-tuple-element.78), channel_id=1, source_target_pairs={{0,4},{1,13},{2,6},{3,15},{4,0},{5,9},{6,2},{7,11},{8,12},{9,5},{1... | collective-permute-start | bytes 1179656 | tf_op jit(solution)/shard_map/ppermute | solution.py:305
  68.0 12.5 %collective-permute-start.15 = (bf16[384,512]{1,0:T(8,128)(2,1)S(1)}, bf16[384,512]{1,0:T(8,128)(2,1)S(1)}, u32[]{:S(2)}, u32[]{:S(2)}) collective-permute-start(bf16[384,512]{1,0:T(8,128)(2,1)S(1)} %get-tuple-element.76), channel_id=1, source_target_pairs={{0,4},{1,13},{2,6},{3,15},{4,0},{5,9},{6,2},{7,11},{8,12},{9,5},{1... | collective-permute-start | bytes 1179656 | tf_op jit(solution)/shard_map/ppermute | solution.py:305
  74.3 9.1 %collective-permute-start.17 = (bf16[384,512]{1,0:T(8,128)(2,1)S(1)}, bf16[384,512]{1,0:T(8,128)(2,1)S(1)}, u32[]{:S(2)}, u32[]{:S(2)}) collective-permute-start(bf16[384,512]{1,0:T(8,128)(2,1)S(1)} %shard_map.94), channel_id=1, source_target_pairs={{0,12},{1,5},{2,14},{3,7},{4,8},{5,1},{6,10},{7,3},{8,4},{9,13},{1... | collective-permute-start | bytes 1179656 | tf_op jit(solution)/shard_map/ppermute | solution.py:305
  83.5 1.8 %collective-permute-start.18 = (bf16[384,512]{1,0:T(8,128)(2,1)S(1)}, bf16[384,512]{1,0:T(8,128)(2,1)S(1)}, u32[]{:S(2)}, u32[]{:S(2)}) collective-permute-start(bf16[384,512]{1,0:T(8,128)(2,1)S(1)} %shard_map.95.grad.g_mine), channel_id=1, source_target_pairs={{0,1},{1,0},{2,3},{3,2},{4,5},{5,4},{6,7},{7,6},{8,9},{9,8},{10,11... | collective-permute-start | bytes 1179656 | tf_op jit(solution)/shard_map/ppermute | solution.py:311
  85.9 8.4 %collective-permute-start.20 = (bf16[576,384]{1,0:T(8,128)(2,1)S(1)}, bf16[576,384]{1,0:T(8,128)(2,1)S(1)}, u32[]{:S(2)}, u32[]{:S(2)}) collective-permute-start(bf16[576,384]{1,0:T(8,128)(2,1)S(1)} %shard_map.100), channel_id=1, source_target_pairs={{0,2},{1,19},{2,0},{3,17},{16,18},{17,3},{18,16},{19,1},{32,34},{3... | collective-permute-start | bytes 1327112 | tf_op jit(solution)/shard_map/ppermute | solution.py:308
  87.9 12.8 %collective-permute-start.19 = (bf16[576,384]{1,0:T(8,128)(2,1)S(1)}, bf16[576,384]{1,0:T(8,128)(2,1)S(1)}, u32[]{:S(2)}, u32[]{:S(2)}) collective-permute-start(bf16[576,384]{1,0:T(8,128)(2,1)S(1)} %shard_map.98), channel_id=1, source_target_pairs={{0,2},{1,19},{2,0},{3,17},{16,18},{17,3},{18,16},{19,1},{32,34},{3... | collective-permute-start | bytes 1327112 | tf_op jit(solution)/shard_map/ppermute | solution.py:308
  94.3 9.8 %collective-permute-start.21 = (bf16[576,384]{1,0:T(8,128)(2,1)S(1)}, bf16[576,384]{1,0:T(8,128)(2,1)S(1)}, u32[]{:S(2)}, u32[]{:S(2)}) collective-permute-start(bf16[576,384]{1,0:T(8,128)(2,1)S(1)} %shard_map.101), channel_id=1, source_target_pairs={{0,18},{1,3},{2,16},{3,1},{16,2},{17,19},{18,0},{19,17},{32,50},{3... | collective-permute-start | bytes 1327112 | tf_op jit(solution)/shard_map/ppermute | solution.py:308
  104.2 7.7 %collective-permute-start.22 = (bf16[144,384]{1,0:T(8,128)(2,1)S(1)}, bf16[144,384]{1,0:T(8,128)(2,1)S(1)}, u32[]{:S(2)}, u32[]{:S(2)}) collective-permute-start(bf16[144,384]{1,0:T(8,128)(2,1)S(1)} %get-tuple-element.82), channel_id=1, source_target_pairs={{0,64},{1,65},{2,66},{3,67},{16,80},{17,81},{18,82},{19,83},{32,96... | collective-permute-start | bytes 331784 | tf_op jit(solution)/shard_map/ppermute | solution.py:317
  108.2 6.1 %collective-permute-start.23 = (bf16[144,384]{1,0:T(8,128)(2,1)S(1)}, bf16[144,384]{1,0:T(8,128)(2,1)S(1)}, u32[]{:S(2)}, u32[]{:S(2)}) collective-permute-start(bf16[144,384]{1,0:T(8,128)(2,1)S(1)} %get-tuple-element.83), channel_id=1, source_target_pairs={{0,32},{1,33},{2,34},{3,35},{16,48},{17,49},{18,50},{19,51},{32,0}... | collective-permute-start | bytes 331784 | tf_op jit(solution)/shard_map/ppermute | solution.py:317
  109.2 6.0 %collective-permute-start.24 = (bf16[144,384]{1,0:T(8,128)(2,1)S(1)}, bf16[144,384]{1,0:T(8,128)(2,1)S(1)}, u32[]{:S(2)}, u32[]{:S(2)}) collective-permute-start(bf16[144,384]{1,0:T(8,128)(2,1)S(1)} %get-tuple-element.84), channel_id=1, source_target_pairs={{0,96},{1,97},{2,98},{3,99},{16,112},{17,113},{18,114},{19,115},{3... | collective-permute-start | bytes 331784 | tf_op jit(solution)/shard_map/ppermute | solution.py:317
  (3 other events, 3.6 us)

commit v5 on v4

--- a/solution.py
+++ b/solution.py
@@ -65,13 +65,10 @@
     return jax.nn.gelu(x, approximate=True)
 
 
-def stem_kernel(marks_ref, stem_ref, weight_hbm, act_ref, weight_ref, arrived):
-    copy = pltpu.make_async_copy(weight_hbm, weight_ref, arrived)
-    copy.start()
+def stem_kernel(marks_ref, stem_ref, act_ref):
     hot = one_hot(marks_ref[...])
     for j in range(0, stem_ref.shape[1], 256):
         act_ref[:, j : j + 256] = gelu(nn(hot, stem_ref[:, j : j + 256])).astype(bf16)
-    copy.wait()
 
 
 def conv_kernel(marks_ref, low_ref, high_ref, stem_ref, act_ref, weight_ref, hidden_ref, ext_ref):
@@ -317,27 +314,26 @@
         return lax.ppermute(value, flat, [(i, i ^ (8 * d)) for i in range(32)])
 
     second = y_way(cot, 1)
-    act, conv_here = call(
-        stem_kernel, [((rows, 1536), bf16), (conv_w.shape, bf16)], marks, stem_w, conv_w,
-        scratch=[pltpu.SemaphoreType.DMA(())], flops=4e8, vmem=16, hbm=(2,),
-    )
+    (act,) = call(stem_kernel, [((rows, 1536), bf16)], marks, stem_w, flops=4e9, vmem=16)
     first = y_way(cot, 0)
     hidden, ext = call(
         conv_kernel,
         [((rows, 384), bf16), ((rows + 2 * HALO, 1536), bf16)],
-        marks, low, high, stem_w, act, conv_here,
+        marks, low, high, stem_w, act, conv_w,
         flops=2e9,
     )
-    far = y_way(second, 0)
-    cots = (cot, first, second, far)
+    cots = [cot, first, second]
 
     second = y_way(hidden, 1)
     taps_mine, taps_other = call(
         taps_kernel, [((2304, rows), bf16)] * 2, ext,
         scratch=[pltpu.VMEM((1536, rows), bf16)], flops=3e9,
     )
-    (w_t,) = call(turn_kernel, [((640, 1536), bf16)], wq, wk, wv, flops=1e9)
-    first = y_way(lax.optimization_barrier((hidden, taps_mine, w_t))[0], 0)
+    _, wv_late = lax.optimization_barrier((hidden, wv))
+    (w_t,) = call(turn_kernel, [((640, 1536), bf16)], wq, wk, wv_late, flops=1e9)
+    tied, cots, taps_mine, w_t = lax.optimization_barrier((hidden, cots, taps_mine, w_t))
+    cots = cots + [y_way(cots[2], 0)]
+    first = y_way(tied, 0)
     second, cots = lax.optimization_barrier((second, cots))
     far = y_way(second, 0)
     g_own, g_other = call(grad_kernel, [((VAL, rows), bf16)] * 2, *cots, out_w, flops=1e9)

time: 116 us -> 114 us (0.983)
  local copies, waits for them, and re-layouts: 3.87 us -> 1.88 us
    unnamed x20, local copies, waits for them, and re-layouts: 3.87 us -> 1.88 us
    ppermute x3, waiting for transfers between devices: 17.4 us -> 16.3 us  [over_chip(): return lax.ppermute(value, 'section', [(i, i ^ 2) for i in range(4)])]
where the time goes in v5:
time: 114 us; the launch traced here: 113 us
  waiting for transfers between devices  57.7 us (51%)
  starting transfers between devices  29.4 us (26%)
  Pallas kernels  24.1 us (21%)
  local copies, waits for them, and re-layouts  1.88 us (2%)
    pallas_call x22, Pallas kernels, call(): pl.pallas_call(kernel, out_shape=[jax.ShapeDtypeStruct(shape, kind) for s...  24.1 us
    ppermute x9, waiting for transfers between devices, y_way(): return lax.ppermute(value, ('tensor', 'section'), pairs)  20.8 us
    ppermute x3, waiting for transfers between devices, over_chip(): return lax.ppermute(value, 'section', [(i, i ^ 2) for i in range(4)])  16.3 us
    ppermute x9, starting transfers between devices, y_way(): return lax.ppermute(value, ('tensor', 'section'), pairs)  12 us
    ppermute x3, waiting for transfers between devices, x_way(): lax.ppermute(value, flat, [(i, i ^ 2 * (1, 3)[(i + way) % 2]) for i in ra...  10.9 us
    ppermute x3, waiting for transfers between devices, over_z(): return lax.ppermute(value, flat, [(i, i ^ 8 * d) for i in range(32)])  5.95 us
    ppermute x3, starting transfers between devices, x_way(): lax.ppermute(value, flat, [(i, i ^ 2 * (1, 3)[(i + way) % 2]) for i in ra...  5.23 us
    ppermute x3, starting transfers between devices, over_z(): return lax.ppermute(value, flat, [(i, i ^ 8 * d) for i in range(32)])  4.99 us
  transfers between devices with their start and end apart: 25, of which 17 were waited for; matrix products, arithmetic and copies ran while one was open for 0% of the time, Pallas kernels for 20%

profile of v5, /device:TPU:0, one launch (start us, length us, event | category | flops | bytes accessed | tf_op | source)
XLA Modules:
  0.0 113.3 jit_solution(1650117164097697601)
XLA Ops:
  1.0 3.0 %collective-permute-start.3 = (bf16[512,384]{1,0:T(8,128)(2,1)}, bf16[512,384]{1,0:T(8,128)(2,1)S(1)}, u32[]{:S(2)}, u32[]{:S(2)}) collective-permute-start(bf16[512,384]{1,0:T(8,128)(2,1)} %bitcast.7), channel_id=1, source_target_pairs={{0,12},{1,5},{2,14},{3,7},{4,8},{5,1},{6,10},{7,3},{8,4},{9,13},{1... | collective-permute-start | bytes 1179656 | tf_op jit(solution)/shard_map/ppermute | solution.py:302
  6.0 1.4 %shard_map.82.act_ref = bf16[512,1536]{1,0:T(8,128)(2,1)S(1)} custom-call(s32[32,512]{1,0:T(8,128)S(1)} %bitcast.13, bf16[128,1536]{1,0:T(8,128)(2,1)S(1)} %copy-done.6), custom_call_target="tpu_custom_call" | custom-call | flops 4000000000 | bytes 458752 | tf_op jit(solution)/shard_map/pallas_call | solution.py:33
  7.5 3.2 %shard_map.83 = (bf16[512,384]{1,0:T(8,128)(2,1)S(1)}, bf16[576,1536]{1,0:T(8,128)(2,1)S(1)}) custom-call(s32[32,512]{1,0:T(8,128)S(1)} %bitcast.14, s32[32,512]{1,0:T(8,128)S(1)} %collective-permute-done.low_ref, s32[32,512]{1,0:T(8,128)S(1)} %collective-permute-done.1.high_ref, bf16[128,1536]{1,0:T(8,128)(2,1)S(1)} %copy-done.7, ...), custom_call_target="tpu_custom_call" | custom-call | flops 2000000000 | bytes 5701632 | tf_op jit(solution)/shard_map/pallas_call | solution.py:33
  10.7 1.1 %collective-permute-start.6 = (bf16[512,384]{1,0:T(8,128)(2,1)S(1)}, bf16[512,384]{1,0:T(8,128)(2,1)S(1)}, u32[]{:S(2)}, u32[]{:S(2)}) collective-permute-start(bf16[512,384]{1,0:T(8,128)(2,1)S(1)} %get-tuple-element.55.own), channel_id=1, source_target_pairs={{0,12},{1,5},{2,14},{3,7},{4,8},{5,1},{6,10},{7,3},{8,4},{9,13},{1... | collective-permute-start | bytes 1179656 | tf_op jit(solution)/shard_map/ppermute | solution.py:302
  12.4 2.1 %shard_map.84 = (bf16[2304,512]{1,0:T(8,128)(2,1)S(1)}, bf16[2304,512]{1,0:T(8,128)(2,1)S(1)}) custom-call(bf16[576,1536]{1,0:T(8,128)(2,1)S(1)} %get-tuple-element.50.ext_ref), custom_call_target="tpu_custom_call" | custom-call | flops 3000000000 | bytes 1769472 | tf_op jit(solution)/shard_map/pallas_call | solution.py:33
  15.4 1.2 %collective-permute-start.5 = (bf16[512,384]{1,0:T(8,128)(2,1)S(1)}, bf16[512,384]{1,0:T(8,128)(2,1)S(1)}, u32[]{:S(2)}, u32[]{:S(2)}) collective-permute-start(bf16[512,384]{1,0:T(8,128)(2,1)S(1)} %get-tuple-element.55.own), channel_id=1, source_target_pairs={{0,4},{1,13},{2,6},{3,15},{4,0},{5,9},{6,2},{7,11},{8,12},{9,5},{1... | collective-permute-start | bytes 1179656 | tf_op jit(solution)/shard_map/ppermute | solution.py:302
  16.6 4.2 %collective-permute-done.6.second = bf16[512,384]{1,0:T(8,128)(2,1)S(1)} collective-permute-done((bf16[512,384]{1,0:T(8,128)(2,1)S(1)}, bf16[512,384]{1,0:T(8,128)(2,1)S(1)}, u32[]{:S(2)}, u32[]{:S(2)}) %collective-permute-start.6) | collective-permute-done | bytes 393248 | tf_op jit(solution)/shard_map/ppermute | solution.py:302
  20.8 1.7 %collective-permute-done.7.c3 = bf16[512,384]{1,0:T(8,128)(2,1)S(1)} collective-permute-done((bf16[512,384]{1,0:T(8,128)(2,1)S(1)}, bf16[512,384]{1,0:T(8,128)(2,1)S(1)}, u32[]{:S(2)}, u32[]{:S(2)}) %collective-permute-start.7) | collective-permute-done | bytes 393248 | tf_op jit(solution)/shard_map/ppermute | solution.py:302
  23.2 1.2 %shard_map.88 = (bf16[192,512]{1,0:T(8,128)(2,1)S(1)}, bf16[192,512]{1,0:T(8,128)(2,1)S(1)}) custom-call(bf16[512,384]{1,0:T(8,128)(2,1)S(1)} %bitcast.9, bf16[512,384]{1,0:T(8,128)(2,1)S(1)} %collective-permute-done.2.c1, bf16[512,384]{1,0:T(8,128)(2,1)S(1)} %collective-permute-done.3.c2, bf16[512,384]{1,0:T(8,128)(2,1)S(1)} %collective-permute-done.7.c3, ...), custom_call_target="tpu_custom_call" | custom-call | flops 1000000000 | bytes 2752512 | tf_op jit(solution)/shard_map/pallas_call | solution.py:33
  24.5 1.5 %collective-permute-start.9 = (bf16[192,512]{1,0:T(8,128)(2,1)S(1)}, bf16[192,512]{1,0:T(8,128)(2,1)S(1)}, u32[]{:S(2)}, u32[]{:S(2)}) collective-permute-start(bf16[192,512]{1,0:T(8,128)(2,1)S(1)} %get-tuple-element.70), channel_id=1, source_target_pairs={{0,2},{1,3},{2,0},{3,1},{4,6},{5,7},{6,4},{7,5},{8,10},{9,11},{10,... | collective-permute-start | bytes 589832 | tf_op jit(solution)/shard_map/ppermute | solution.py:311
  26.8 4.1 %collective-permute-done.8.far = bf16[512,384]{1,0:T(8,128)(2,1)S(1)} collective-permute-done((bf16[512,384]{1,0:T(8,128)(2,1)S(1)}, bf16[512,384]{1,0:T(8,128)(2,1)S(1)}, u32[]{:S(2)}, u32[]{:S(2)}) %collective-permute-start.8) | collective-permute-done | bytes 393248 | tf_op jit(solution)/shard_map/ppermute | solution.py:302
  31.9 1.5 %collective-permute-start.10 = (bf16[320,512]{1,0:T(8,128)(2,1)S(1)}, bf16[320,512]{1,0:T(8,128)(2,1)S(1)}, u32[]{:S(2)}, u32[]{:S(2)}) collective-permute-start(bf16[320,512]{1,0:T(8,128)(2,1)S(1)} %get-tuple-element.72), channel_id=1, source_target_pairs={{0,2},{1,3},{2,0},{3,1},{4,6},{5,7},{6,4},{7,5},{8,10},{9,11},{10,... | collective-permute-start | bytes 983048 | tf_op jit(solution)/shard_map/ppermute | solution.py:311
  34.0 8.2 %collective-permute-done.10.par = bf16[320,512]{1,0:T(8,128)(2,1)S(1)} collective-permute-done((bf16[320,512]{1,0:T(8,128)(2,1)S(1)}, bf16[320,512]{1,0:T(8,128)(2,1)S(1)}, u32[]{:S(2)}, u32[]{:S(2)}) %collective-permute-start.10) | collective-permute-done | bytes 327712 | tf_op jit(solution)/shard_map/ppermute | solution.py:311
  42.7 1.1 collective-permute-done.12.sib_par
  43.9 7.4 %shard_map.89 = (bf16[64,512]{1,0:T(8,128)(2,1)S(1)}, bf16[64,512]{1,0:T(8,128)(2,1)S(1)}, f32[256,1024]{1,0:T(8,128)S(1)}, bf16[256,1024]{1,0:T(8,128)(2,1)S(1)}) custom-call(bf16[320,512]{1,0:T(8,128)(2,1)S(1)} %get-tuple-element.64.own, bf16[320,512]{1,0:T(8,128)(2,1)S(1)} %collective-permute-done.10.par, ...), custom_call_target="tpu_custom_call" | custom-call | flops 8000000000 | bytes 1703936 | tf_op jit(solution)/shard_map/pallas_call | solution.py:33
  51.4 1.8 %collective-permute-done.13.kv_got = bf16[256,1024]{1,0:T(8,128)(2,1)S(1)} collective-permute-done((bf16[256,1024]{1,0:T(8,128)(2,1)S(1)}, bf16[256,1024]{1,0:T(8,128)(2,1)S(1)}, u32[]{:S(2)}, u32[]{:S(2)}) %collective-permute-start.13) | collective-permute-done | bytes 524320 | tf_op jit(solution)/shard_map/ppermute | solution.py:308
  53.3 1.8 %collective-permute-start.14 = (bf16[320,512]{1,0:T(8,128)(2,1)S(1)}, bf16[320,512]{1,0:T(8,128)(2,1)S(1)}, u32[]{:S(2)}, u32[]{:S(2)}) collective-permute-start(bf16[320,512]{1,0:T(8,128)(2,1)S(1)} %get-tuple-element.80), channel_id=1, source_target_pairs={{0,2},{1,3},{2,0},{3,1},{4,6},{5,7},{6,4},{7,5},{8,10},{9,11},{10,... | collective-permute-start | bytes 983048 | tf_op jit(solution)/shard_map/ppermute | solution.py:311
  55.1 8.1 %collective-permute-done.14.other = bf16[320,512]{1,0:T(8,128)(2,1)S(1)} collective-permute-done((bf16[320,512]{1,0:T(8,128)(2,1)S(1)}, bf16[320,512]{1,0:T(8,128)(2,1)S(1)}, u32[]{:S(2)}, u32[]{:S(2)}) %collective-permute-start.14) | collective-permute-done | bytes 327712 | tf_op jit(solution)/shard_map/ppermute | solution.py:311
  63.8 1.1 collective-permute-start.16
  65.7 1.1 collective-permute-start.15
  66.8 4.9 %collective-permute-done.16.got = bf16[384,512]{1,0:T(8,128)(2,1)S(1)} collective-permute-done((bf16[384,512]{1,0:T(8,128)(2,1)S(1)}, bf16[384,512]{1,0:T(8,128)(2,1)S(1)}, u32[]{:S(2)}, u32[]{:S(2)}) %collective-permute-start.16) | collective-permute-done | bytes 393248 | tf_op jit(solution)/shard_map/ppermute | solution.py:302
  71.7 2.7 %collective-permute-start.17 = (bf16[384,512]{1,0:T(8,128)(2,1)S(1)}, bf16[384,512]{1,0:T(8,128)(2,1)S(1)}, u32[]{:S(2)}, u32[]{:S(2)}) collective-permute-start(bf16[384,512]{1,0:T(8,128)(2,1)S(1)} %shard_map.94), channel_id=1, source_target_pairs={{0,12},{1,5},{2,14},{3,7},{4,8},{5,1},{6,10},{7,3},{8,4},{9,13},{1... | collective-permute-start | bytes 1179656 | tf_op jit(solution)/shard_map/ppermute | solution.py:302
  74.9 3.1 %collective-permute-done.15.alone = bf16[384,512]{1,0:T(8,128)(2,1)S(1)} collective-permute-done((bf16[384,512]{1,0:T(8,128)(2,1)S(1)}, bf16[384,512]{1,0:T(8,128)(2,1)S(1)}, u32[]{:S(2)}, u32[]{:S(2)}) %collective-permute-start.15) | collective-permute-done | bytes 393248 | tf_op jit(solution)/shard_map/ppermute | solution.py:302
  77.9 2.9 %collective-permute-done.17.joined = bf16[384,512]{1,0:T(8,128)(2,1)S(1)} collective-permute-done((bf16[384,512]{1,0:T(8,128)(2,1)S(1)}, bf16[384,512]{1,0:T(8,128)(2,1)S(1)}, u32[]{:S(2)}, u32[]{:S(2)}) %collective-permute-start.17) | collective-permute-done | bytes 393248 | tf_op jit(solution)/shard_map/ppermute | solution.py:302
  83.2 1.8 %collective-permute-start.20 = (bf16[576,384]{1,0:T(8,128)(2,1)S(1)}, bf16[576,384]{1,0:T(8,128)(2,1)S(1)}, u32[]{:S(2)}, u32[]{:S(2)}) collective-permute-start(bf16[576,384]{1,0:T(8,128)(2,1)S(1)} %shard_map.100), channel_id=1, source_target_pairs={{0,2},{1,19},{2,0},{3,17},{16,18},{17,3},{18,16},{19,1},{32,34},{3... | collective-permute-start | bytes 1327112 | tf_op jit(solution)/shard_map/ppermute | solution.py:305
  86.7 4.9 %collective-permute-done.20.got = bf16[576,384]{1,0:T(8,128)(2,1)S(1)} collective-permute-done((bf16[576,384]{1,0:T(8,128)(2,1)S(1)}, bf16[576,384]{1,0:T(8,128)(2,1)S(1)}, u32[]{:S(2)}, u32[]{:S(2)}) %collective-permute-start.20) | collective-permute-done | bytes 442400 | tf_op jit(solution)/shard_map/ppermute | solution.py:305
  91.7 3.0 %collective-permute-start.21 = (bf16[576,384]{1,0:T(8,128)(2,1)S(1)}, bf16[576,384]{1,0:T(8,128)(2,1)S(1)}, u32[]{:S(2)}, u32[]{:S(2)}) collective-permute-start(bf16[576,384]{1,0:T(8,128)(2,1)S(1)} %shard_map.101), channel_id=1, source_target_pairs={{0,18},{1,3},{2,16},{3,1},{16,2},{17,19},{18,0},{19,17},{32,50},{3... | collective-permute-start | bytes 1327112 | tf_op jit(solution)/shard_map/ppermute | solution.py:305
  95.5 2.7 %collective-permute-done.19.alone = bf16[576,384]{1,0:T(8,128)(2,1)S(1)} collective-permute-done((bf16[576,384]{1,0:T(8,128)(2,1)S(1)}, bf16[576,384]{1,0:T(8,128)(2,1)S(1)}, u32[]{:S(2)}, u32[]{:S(2)}) %collective-permute-start.19) | collective-permute-done | bytes 442400 | tf_op jit(solution)/shard_map/ppermute | solution.py:305
  98.2 3.3 %collective-permute-done.21.joined = bf16[576,384]{1,0:T(8,128)(2,1)S(1)} collective-permute-done((bf16[576,384]{1,0:T(8,128)(2,1)S(1)}, bf16[576,384]{1,0:T(8,128)(2,1)S(1)}, u32[]{:S(2)}, u32[]{:S(2)}) %collective-permute-start.21) | collective-permute-done | bytes 442400 | tf_op jit(solution)/shard_map/ppermute | solution.py:305
  101.6 4.0 %collective-permute-start.22 = (bf16[144,384]{1,0:T(8,128)(2,1)S(1)}, bf16[144,384]{1,0:T(8,128)(2,1)S(1)}, u32[]{:S(2)}, u32[]{:S(2)}) collective-permute-start(bf16[144,384]{1,0:T(8,128)(2,1)S(1)} %get-tuple-element.90), channel_id=1, source_target_pairs={{0,64},{1,65},{2,66},{3,67},{16,80},{17,81},{18,82},{19,83},{32,96... | collective-permute-start | bytes 331784 | tf_op jit(solution)/shard_map/ppermute | solution.py:314
  106.6 2.7 %collective-permute-done.22.r1 = bf16[144,384]{1,0:T(8,128)(2,1)S(1)} collective-permute-done((bf16[144,384]{1,0:T(8,128)(2,1)S(1)}, bf16[144,384]{1,0:T(8,128)(2,1)S(1)}, u32[]{:S(2)}, u32[]{:S(2)}) %collective-permute-start.22) | collective-permute-done | bytes 110624 | tf_op jit(solution)/shard_map/ppermute | solution.py:314
  109.3 2.3 %collective-permute-done.23.r2 = bf16[144,384]{1,0:T(8,128)(2,1)S(1)} collective-permute-done((bf16[144,384]{1,0:T(8,128)(2,1)S(1)}, bf16[144,384]{1,0:T(8,128)(2,1)S(1)}, u32[]{:S(2)}, u32[]{:S(2)}) %collective-permute-start.23) | collective-permute-done | bytes 110624 | tf_op jit(solution)/shard_map/ppermute | solution.py:314
  (60 shorter events, 18.3 us)
Async XLA Ops:
  0.0 7.4 %collective-permute-start.1 = (s32[32,512]{1,0:T(8,128)}, s32[32,512]{1,0:T(8,128)S(1)}, u32[]{:S(2)}, u32[]{:S(2)}) collective-permute-start(s32[32,512]{1,0:T(8,128)} %bitcast.11), channel_id=1, source_target_pairs={{1,0},{2,1},{3,2},{0,3},{5,4},{6,5},{7,6},{4,7},{9,8},{10,9},{11,1... | collective-permute-start | bytes 196616 | tf_op jit(solution)/shard_map/ppermute | solution.py:295
  1.0 6.4 %collective-permute-start = (s32[32,512]{1,0:T(8,128)}, s32[32,512]{1,0:T(8,128)S(1)}, u32[]{:S(2)}, u32[]{:S(2)}) collective-permute-start(s32[32,512]{1,0:T(8,128)} %bitcast.12), channel_id=1, source_target_pairs={{0,1},{1,2},{2,3},{3,0},{4,5},{5,6},{6,7},{7,4},{8,9},{9,10},{10,1... | collective-permute-start | bytes 196616 | tf_op jit(solution)/shard_map/ppermute | solution.py:294
  1.0 6.4 %copy-start.4 = (bf16[3,1536,384]{2,1,0:T(8,128)(2,1)S(1)}, bf16[3,1536,384]{2,1,0:T(8,128)(2,1)}, u32[]{:S(2)}) copy-start(bf16[3,1536,384]{2,1,0:T(8,128)(2,1)} %weight_ref.1) | copy-start | bytes 10616836
  1.0 13.4 %collective-permute-start.3 = (bf16[512,384]{1,0:T(8,128)(2,1)}, bf16[512,384]{1,0:T(8,128)(2,1)S(1)}, u32[]{:S(2)}, u32[]{:S(2)}) collective-permute-start(bf16[512,384]{1,0:T(8,128)(2,1)} %bitcast.7), channel_id=1, source_target_pairs={{0,12},{1,5},{2,14},{3,7},{4,8},{5,1},{6,10},{7,3},{8,4},{9,13},{1... | collective-permute-start | bytes 1179656 | tf_op jit(solution)/shard_map/ppermute | solution.py:302
  4.0 10.4 %collective-permute-start.2 = (bf16[512,384]{1,0:T(8,128)(2,1)}, bf16[512,384]{1,0:T(8,128)(2,1)S(1)}, u32[]{:S(2)}, u32[]{:S(2)}) collective-permute-start(bf16[512,384]{1,0:T(8,128)(2,1)} %bitcast.8), channel_id=1, source_target_pairs={{0,4},{1,13},{2,6},{3,15},{4,0},{5,9},{6,2},{7,11},{8,12},{9,5},{1... | collective-permute-start | bytes 1179656 | tf_op jit(solution)/shard_map/ppermute | solution.py:302
  6.0 1.4 %copy-start.9 = (s32[1,512,32]{1,2,0:T(8,128)S(1)}, s32[1,512,32]{1,2,0:T(8,128)}, u32[]{:S(2)}) copy-start(s32[1,512,32]{1,2,0:T(8,128)} %param.8) | copy-start | bytes 196612
  7.4 4.4 %copy-start = (bf16[1536,384]{1,0:T(8,128)(2,1)S(1)}, bf16[1536,384]{1,0:T(8,128)(2,1)}, u32[]{:S(2)}) copy-start(bf16[1536,384]{1,0:T(8,128)(2,1)} %wv.5) | copy-start | bytes 3538948
  7.4 4.4 %copy-start.1 = (bf16[1536,128]{1,0:T(8,128)(2,1)S(1)}, bf16[1536,128]{1,0:T(8,128)(2,1)}, u32[]{:S(2)}) copy-start(bf16[1536,128]{1,0:T(8,128)(2,1)} %wq.5) | copy-start | bytes 1179652
  7.4 4.4 %copy-start.2 = (bf16[1536,128]{1,0:T(8,128)(2,1)S(1)}, bf16[1536,128]{1,0:T(8,128)(2,1)}, u32[]{:S(2)}) copy-start(bf16[1536,128]{1,0:T(8,128)(2,1)} %wk.5) | copy-start | bytes 1179652
  10.7 10.1 %collective-permute-start.6 = (bf16[512,384]{1,0:T(8,128)(2,1)S(1)}, bf16[512,384]{1,0:T(8,128)(2,1)S(1)}, u32[]{:S(2)}, u32[]{:S(2)}) collective-permute-start(bf16[512,384]{1,0:T(8,128)(2,1)S(1)} %get-tuple-element.55.own), channel_id=1, source_target_pairs={{0,12},{1,5},{2,14},{3,7},{4,8},{5,1},{6,10},{7,3},{8,4},{9,13},{1... | collective-permute-start | bytes 1179656 | tf_op jit(solution)/shard_map/ppermute | solution.py:302
  12.4 10.8 %copy-start.3 = (bf16[1,512,384]{2,1,0:T(8,128)(2,1)S(1)}, bf16[1,512,384]{2,1,0:T(8,128)(2,1)}, u32[]{:S(2)}) copy-start(bf16[1,512,384]{2,1,0:T(8,128)(2,1)} %param.15) | copy-start | bytes 1179652
  12.4 10.8 %copy-start.5 = (bf16[384,1536]{1,0:T(8,128)(2,1)S(1)}, bf16[384,1536]{1,0:T(8,128)(2,1)}, u32[]{:S(2)}) copy-start(bf16[384,1536]{1,0:T(8,128)(2,1)} %w_ref.1) | copy-start | bytes 3538948
  14.5 8.0 %collective-permute-start.7 = (bf16[512,384]{1,0:T(8,128)(2,1)S(1)}, bf16[512,384]{1,0:T(8,128)(2,1)S(1)}, u32[]{:S(2)}, u32[]{:S(2)}) collective-permute-start(bf16[512,384]{1,0:T(8,128)(2,1)S(1)} %collective-permute-done.3.c2), channel_id=1, source_target_pairs={{0,4},{1,13},{2,6},{3,15},{4,0},{5,9},{6,2},{7,11},{8,12},{9,5},{1... | collective-permute-start | bytes 1179656 | tf_op jit(solution)/shard_map/ppermute | solution.py:302
  15.4 11.4 %collective-permute-start.5 = (bf16[512,384]{1,0:T(8,128)(2,1)S(1)}, bf16[512,384]{1,0:T(8,128)(2,1)S(1)}, u32[]{:S(2)}, u32[]{:S(2)}) collective-permute-start(bf16[512,384]{1,0:T(8,128)(2,1)S(1)} %get-tuple-element.55.own), channel_id=1, source_target_pairs={{0,4},{1,13},{2,6},{3,15},{4,0},{5,9},{6,2},{7,11},{8,12},{9,5},{1... | collective-permute-start | bytes 1179656 | tf_op jit(solution)/shard_map/ppermute | solution.py:302
  22.5 8.4 %collective-permute-start.8 = (bf16[512,384]{1,0:T(8,128)(2,1)S(1)}, bf16[512,384]{1,0:T(8,128)(2,1)S(1)}, u32[]{:S(2)}, u32[]{:S(2)}) collective-permute-start(bf16[512,384]{1,0:T(8,128)(2,1)S(1)} %collective-permute-done.6.second), channel_id=1, source_target_pairs={{0,4},{1,13},{2,6},{3,15},{4,0},{5,9},{6,2},{7,11},{8,12},{9,5},{1... | collective-permute-start | bytes 1179656 | tf_op jit(solution)/shard_map/ppermute | solution.py:302
  24.5 7.4 %collective-permute-start.9 = (bf16[192,512]{1,0:T(8,128)(2,1)S(1)}, bf16[192,512]{1,0:T(8,128)(2,1)S(1)}, u32[]{:S(2)}, u32[]{:S(2)}) collective-permute-start(bf16[192,512]{1,0:T(8,128)(2,1)S(1)} %get-tuple-element.70), channel_id=1, source_target_pairs={{0,2},{1,3},{2,0},{3,1},{4,6},{5,7},{6,4},{7,5},{8,10},{9,11},{10,... | collective-permute-start | bytes 589832 | tf_op jit(solution)/shard_map/ppermute | solution.py:311
  31.9 10.3 %collective-permute-start.10 = (bf16[320,512]{1,0:T(8,128)(2,1)S(1)}, bf16[320,512]{1,0:T(8,128)(2,1)S(1)}, u32[]{:S(2)}, u32[]{:S(2)}) collective-permute-start(bf16[320,512]{1,0:T(8,128)(2,1)S(1)} %get-tuple-element.72), channel_id=1, source_target_pairs={{0,2},{1,3},{2,0},{3,1},{4,6},{5,7},{6,4},{7,5},{8,10},{9,11},{10,... | collective-permute-start | bytes 983048 | tf_op jit(solution)/shard_map/ppermute | solution.py:311
  33.4 9.3 %collective-permute-start.11 = (bf16[320,512]{1,0:T(8,128)(2,1)S(1)}, bf16[320,512]{1,0:T(8,128)(2,1)S(1)}, u32[]{:S(2)}, u32[]{:S(2)}) collective-permute-start(bf16[320,512]{1,0:T(8,128)(2,1)S(1)} %get-tuple-element.64.own), channel_id=1, source_target_pairs={{0,1},{1,0},{2,3},{3,2},{4,5},{5,4},{6,7},{7,6},{8,9},{9,8},{10,11... | collective-permute-start | bytes 983048 | tf_op jit(solution)/shard_map/ppermute | solution.py:308
  42.2 1.6 %collective-permute-start.12 = (bf16[320,512]{1,0:T(8,128)(2,1)S(1)}, bf16[320,512]{1,0:T(8,128)(2,1)S(1)}, u32[]{:S(2)}, u32[]{:S(2)}) collective-permute-start(bf16[320,512]{1,0:T(8,128)(2,1)S(1)} %collective-permute-done.10.par), channel_id=1, source_target_pairs={{0,1},{1,0},{2,3},{3,2},{4,5},{5,4},{6,7},{7,6},{8,9},{9,8},{10,11... | collective-permute-start | bytes 983048 | tf_op jit(solution)/shard_map/ppermute | solution.py:308
  42.4 40.4 %collective-permute-start.4 = (bf16[2304,512]{1,0:T(8,128)(2,1)S(1)}, bf16[2304,512]{1,0:T(8,128)(2,1)S(1)}, u32[]{:S(2)}, u32[]{:S(2)}) collective-permute-start(bf16[2304,512]{1,0:T(8,128)(2,1)S(1)} %get-tuple-element.54), channel_id=1, source_target_pairs={{0,1},{1,0},{2,3},{3,2},{4,5},{5,4},{6,7},{7,6},{8,9},{9,8},{10,11... | collective-permute-start | bytes 7077896 | tf_op jit(solution)/shard_map/ppermute | solution.py:308
  51.2 2.0 %collective-permute-start.13 = (bf16[256,1024]{1,0:T(8,128)(2,1)S(1)}, bf16[256,1024]{1,0:T(8,128)(2,1)S(1)}, u32[]{:S(2)}, u32[]{:S(2)}) collective-permute-start(bf16[256,1024]{1,0:T(8,128)(2,1)S(1)} %get-tuple-element.78), channel_id=1, source_target_pairs={{0,1},{1,0},{2,3},{3,2},{4,5},{5,4},{6,7},{7,6},{8,9},{9,8},{10,11... | collective-permute-start | bytes 1572872 | tf_op jit(solution)/shard_map/ppermute | solution.py:308
  53.3 9.8 %collective-permute-start.14 = (bf16[320,512]{1,0:T(8,128)(2,1)S(1)}, bf16[320,512]{1,0:T(8,128)(2,1)S(1)}, u32[]{:S(2)}, u32[]{:S(2)}) collective-permute-start(bf16[320,512]{1,0:T(8,128)(2,1)S(1)} %get-tuple-element.80), channel_id=1, source_target_pairs={{0,2},{1,3},{2,0},{3,1},{4,6},{5,7},{6,4},{7,5},{8,10},{9,11},{10,... | collective-permute-start | bytes 983048 | tf_op jit(solution)/shard_map/ppermute | solution.py:311
  63.8 7.9 %collective-permute-start.16 = (bf16[384,512]{1,0:T(8,128)(2,1)S(1)}, bf16[384,512]{1,0:T(8,128)(2,1)S(1)}, u32[]{:S(2)}, u32[]{:S(2)}) collective-permute-start(bf16[384,512]{1,0:T(8,128)(2,1)S(1)} %get-tuple-element.86), channel_id=1, source_target_pairs={{0,4},{1,13},{2,6},{3,15},{4,0},{5,9},{6,2},{7,11},{8,12},{9,5},{1... | collective-permute-start | bytes 1179656 | tf_op jit(solution)/shard_map/ppermute | solution.py:302
  65.7 12.2 %collective-permute-start.15 = (bf16[384,512]{1,0:T(8,128)(2,1)S(1)}, bf16[384,512]{1,0:T(8,128)(2,1)S(1)}, u32[]{:S(2)}, u32[]{:S(2)}) collective-permute-start(bf16[384,512]{1,0:T(8,128)(2,1)S(1)} %get-tuple-element.84), channel_id=1, source_target_pairs={{0,4},{1,13},{2,6},{3,15},{4,0},{5,9},{6,2},{7,11},{8,12},{9,5},{1... | collective-permute-start | bytes 1179656 | tf_op jit(solution)/shard_map/ppermute | solution.py:302
  71.7 9.1 %collective-permute-start.17 = (bf16[384,512]{1,0:T(8,128)(2,1)S(1)}, bf16[384,512]{1,0:T(8,128)(2,1)S(1)}, u32[]{:S(2)}, u32[]{:S(2)}) collective-permute-start(bf16[384,512]{1,0:T(8,128)(2,1)S(1)} %shard_map.94), channel_id=1, source_target_pairs={{0,12},{1,5},{2,14},{3,7},{4,8},{5,1},{6,10},{7,3},{8,4},{9,13},{1... | collective-permute-start | bytes 1179656 | tf_op jit(solution)/shard_map/ppermute | solution.py:302
  80.9 1.8 %collective-permute-start.18 = (bf16[384,512]{1,0:T(8,128)(2,1)S(1)}, bf16[384,512]{1,0:T(8,128)(2,1)S(1)}, u32[]{:S(2)}, u32[]{:S(2)}) collective-permute-start(bf16[384,512]{1,0:T(8,128)(2,1)S(1)} %shard_map.95.grad.g_mine), channel_id=1, source_target_pairs={{0,1},{1,0},{2,3},{3,2},{4,5},{5,4},{6,7},{7,6},{8,9},{9,8},{10,11... | collective-permute-start | bytes 1179656 | tf_op jit(solution)/shard_map/ppermute | solution.py:308
  83.2 8.4 %collective-permute-start.20 = (bf16[576,384]{1,0:T(8,128)(2,1)S(1)}, bf16[576,384]{1,0:T(8,128)(2,1)S(1)}, u32[]{:S(2)}, u32[]{:S(2)}) collective-permute-start(bf16[576,384]{1,0:T(8,128)(2,1)S(1)} %shard_map.100), channel_id=1, source_target_pairs={{0,2},{1,19},{2,0},{3,17},{16,18},{17,3},{18,16},{19,1},{32,34},{3... | collective-permute-start | bytes 1327112 | tf_op jit(solution)/shard_map/ppermute | solution.py:305
  85.5 12.7 %collective-permute-start.19 = (bf16[576,384]{1,0:T(8,128)(2,1)S(1)}, bf16[576,384]{1,0:T(8,128)(2,1)S(1)}, u32[]{:S(2)}, u32[]{:S(2)}) collective-permute-start(bf16[576,384]{1,0:T(8,128)(2,1)S(1)} %shard_map.98), channel_id=1, source_target_pairs={{0,2},{1,19},{2,0},{3,17},{16,18},{17,3},{18,16},{19,1},{32,34},{3... | collective-permute-start | bytes 1327112 | tf_op jit(solution)/shard_map/ppermute | solution.py:305
  91.7 9.8 %collective-permute-start.21 = (bf16[576,384]{1,0:T(8,128)(2,1)S(1)}, bf16[576,384]{1,0:T(8,128)(2,1)S(1)}, u32[]{:S(2)}, u32[]{:S(2)}) collective-permute-start(bf16[576,384]{1,0:T(8,128)(2,1)S(1)} %shard_map.101), channel_id=1, source_target_pairs={{0,18},{1,3},{2,16},{3,1},{16,2},{17,19},{18,0},{19,17},{32,50},{3... | collective-permute-start | bytes 1327112 | tf_op jit(solution)/shard_map/ppermute | solution.py:305
  101.6 7.7 %collective-permute-start.22 = (bf16[144,384]{1,0:T(8,128)(2,1)S(1)}, bf16[144,384]{1,0:T(8,128)(2,1)S(1)}, u32[]{:S(2)}, u32[]{:S(2)}) collective-permute-start(bf16[144,384]{1,0:T(8,128)(2,1)S(1)} %get-tuple-element.90), channel_id=1, source_target_pairs={{0,64},{1,65},{2,66},{3,67},{16,80},{17,81},{18,82},{19,83},{32,96... | collective-permute-start | bytes 331784 | tf_op jit(solution)/shard_map/ppermute | solution.py:314
  105.6 6.0 %collective-permute-start.23 = (bf16[144,384]{1,0:T(8,128)(2,1)S(1)}, bf16[144,384]{1,0:T(8,128)(2,1)S(1)}, u32[]{:S(2)}, u32[]{:S(2)}) collective-permute-start(bf16[144,384]{1,0:T(8,128)(2,1)S(1)} %get-tuple-element.91), channel_id=1, source_target_pairs={{0,32},{1,33},{2,34},{3,35},{16,48},{17,49},{18,50},{19,51},{32,0}... | collective-permute-start | bytes 331784 | tf_op jit(solution)/shard_map/ppermute | solution.py:314
  106.6 6.0 %collective-permute-start.24 = (bf16[144,384]{1,0:T(8,128)(2,1)S(1)}, bf16[144,384]{1,0:T(8,128)(2,1)S(1)}, u32[]{:S(2)}, u32[]{:S(2)}) collective-permute-start(bf16[144,384]{1,0:T(8,128)(2,1)S(1)} %get-tuple-element.92), channel_id=1, source_target_pairs={{0,96},{1,97},{2,98},{3,99},{16,112},{17,113},{18,114},{19,115},{3... | collective-permute-start | bytes 331784 | tf_op jit(solution)/shard_map/ppermute | solution.py:314
  (3 other events, 3.3 us)

commit v6 on v5

--- a/solution.py
+++ b/solution.py
@@ -409,7 +409,7 @@
     own_z, z1, z2, z3 = call(
         sum_x_kernel, [((144, 384), f32)] + [((144, 384), bf16)] * 3, part, alone, joined
     )
-    got = [over_z(z2, 2), over_z(z1, 1), over_z(z3, 3)]
+    got = [over_z(z1, 1), over_z(z3, 3), over_z(z2, 2)]
     norm = 1.0 / math.sqrt(rows * 32)
     (total,) = call(functools.partial(sum_z_kernel, norm), [((144, 384), f32)], own_z, *got)
     return total.reshape(3, 48, 384).transpose(1, 0, 2)

time: 114 us -> 113 us (level)
  transfers between devices with their start and end apart: 25 -> 25, of which waited for: 17 -> 16; matrix products, arithmetic and copies ran while one was open for 0% -> 0% of each run, Pallas kernels for 20% -> 20%
where the time goes in v6:
time: 113 us
  waiting for transfers between devices  56.9 us (50%)
  starting transfers between devices  30 us (27%)
  Pallas kernels  24.1 us (21%)
  local copies, waits for them, and re-layouts  1.88 us (2%)
    pallas_call x22, Pallas kernels, call(): pl.pallas_call(kernel, out_shape=[jax.ShapeDtypeStruct(shape, kind) for s...  24.1 us
    ppermute x9, waiting for transfers between devices, y_way(): return lax.ppermute(value, ('tensor', 'section'), pairs)  20.8 us
    ppermute x3, waiting for transfers between devices, over_chip(): return lax.ppermute(value, 'section', [(i, i ^ 2) for i in range(4)])  16.3 us
    ppermute x9, starting transfers between devices, y_way(): return lax.ppermute(value, ('tensor', 'section'), pairs)  12 us
    ppermute x3, waiting for transfers between devices, x_way(): lax.ppermute(value, flat, [(i, i ^ 2 * (1, 3)[(i + way) % 2]) for i in ra...  10.9 us
    ppermute x3, starting transfers between devices, over_z(): return lax.ppermute(value, flat, [(i, i ^ 8 * d) for i in range(32)])  5.59 us
    ppermute x3, starting transfers between devices, x_way(): lax.ppermute(value, flat, [(i, i ^ 2 * (1, 3)[(i + way) % 2]) for i in ra...  5.23 us
    ppermute x3, waiting for transfers between devices, over_z(): return lax.ppermute(value, flat, [(i, i ^ 8 * d) for i in range(32)])  5.19 us
  transfers between devices with their start and end apart: 25, of which 16 were waited for; matrix products, arithmetic and copies ran while one was open for 0% of the time, Pallas kernels for 20%

profile of v6, /device:TPU:0, one launch (start us, length us, event | category | flops | bytes accessed | tf_op | source)
XLA Modules:
  0.0 113.2 jit_solution(12865051335278901679)
XLA Ops:
  1.0 3.0 %collective-permute-start.3 = (bf16[512,384]{1,0:T(8,128)(2,1)}, bf16[512,384]{1,0:T(8,128)(2,1)S(1)}, u32[]{:S(2)}, u32[]{:S(2)}) collective-permute-start(bf16[512,384]{1,0:T(8,128)(2,1)} %bitcast.7), channel_id=1, source_target_pairs={{0,12},{1,5},{2,14},{3,7},{4,8},{5,1},{6,10},{7,3},{8,4},{9,13},{1... | collective-permute-start | bytes 1179656 | tf_op jit(solution)/shard_map/ppermute | solution.py:302
  6.0 1.4 %shard_map.82.act_ref = bf16[512,1536]{1,0:T(8,128)(2,1)S(1)} custom-call(s32[32,512]{1,0:T(8,128)S(1)} %bitcast.13, bf16[128,1536]{1,0:T(8,128)(2,1)S(1)} %copy-done.6), custom_call_target="tpu_custom_call" | custom-call | flops 4000000000 | bytes 458752 | tf_op jit(solution)/shard_map/pallas_call | solution.py:33
  7.5 3.2 %shard_map.83 = (bf16[512,384]{1,0:T(8,128)(2,1)S(1)}, bf16[576,1536]{1,0:T(8,128)(2,1)S(1)}) custom-call(s32[32,512]{1,0:T(8,128)S(1)} %bitcast.14, s32[32,512]{1,0:T(8,128)S(1)} %collective-permute-done.low_ref, s32[32,512]{1,0:T(8,128)S(1)} %collective-permute-done.1.high_ref, bf16[128,1536]{1,0:T(8,128)(2,1)S(1)} %copy-done.7, ...), custom_call_target="tpu_custom_call" | custom-call | flops 2000000000 | bytes 5701632 | tf_op jit(solution)/shard_map/pallas_call | solution.py:33
  10.7 1.1 %collective-permute-start.6 = (bf16[512,384]{1,0:T(8,128)(2,1)S(1)}, bf16[512,384]{1,0:T(8,128)(2,1)S(1)}, u32[]{:S(2)}, u32[]{:S(2)}) collective-permute-start(bf16[512,384]{1,0:T(8,128)(2,1)S(1)} %get-tuple-element.55.own), channel_id=1, source_target_pairs={{0,12},{1,5},{2,14},{3,7},{4,8},{5,1},{6,10},{7,3},{8,4},{9,13},{1... | collective-permute-start | bytes 1179656 | tf_op jit(solution)/shard_map/ppermute | solution.py:302
  12.4 2.1 %shard_map.84 = (bf16[2304,512]{1,0:T(8,128)(2,1)S(1)}, bf16[2304,512]{1,0:T(8,128)(2,1)S(1)}) custom-call(bf16[576,1536]{1,0:T(8,128)(2,1)S(1)} %get-tuple-element.50.ext_ref), custom_call_target="tpu_custom_call" | custom-call | flops 3000000000 | bytes 1769472 | tf_op jit(solution)/shard_map/pallas_call | solution.py:33
  15.4 1.2 %collective-permute-start.5 = (bf16[512,384]{1,0:T(8,128)(2,1)S(1)}, bf16[512,384]{1,0:T(8,128)(2,1)S(1)}, u32[]{:S(2)}, u32[]{:S(2)}) collective-permute-start(bf16[512,384]{1,0:T(8,128)(2,1)S(1)} %get-tuple-element.55.own), channel_id=1, source_target_pairs={{0,4},{1,13},{2,6},{3,15},{4,0},{5,9},{6,2},{7,11},{8,12},{9,5},{1... | collective-permute-start | bytes 1179656 | tf_op jit(solution)/shard_map/ppermute | solution.py:302
  16.6 4.2 %collective-permute-done.6.second = bf16[512,384]{1,0:T(8,128)(2,1)S(1)} collective-permute-done((bf16[512,384]{1,0:T(8,128)(2,1)S(1)}, bf16[512,384]{1,0:T(8,128)(2,1)S(1)}, u32[]{:S(2)}, u32[]{:S(2)}) %collective-permute-start.6) | collective-permute-done | bytes 393248 | tf_op jit(solution)/shard_map/ppermute | solution.py:302
  20.8 1.7 %collective-permute-done.7.c3 = bf16[512,384]{1,0:T(8,128)(2,1)S(1)} collective-permute-done((bf16[512,384]{1,0:T(8,128)(2,1)S(1)}, bf16[512,384]{1,0:T(8,128)(2,1)S(1)}, u32[]{:S(2)}, u32[]{:S(2)}) %collective-permute-start.7) | collective-permute-done | bytes 393248 | tf_op jit(solution)/shard_map/ppermute | solution.py:302
  23.2 1.2 %shard_map.88 = (bf16[192,512]{1,0:T(8,128)(2,1)S(1)}, bf16[192,512]{1,0:T(8,128)(2,1)S(1)}) custom-call(bf16[512,384]{1,0:T(8,128)(2,1)S(1)} %bitcast.9, bf16[512,384]{1,0:T(8,128)(2,1)S(1)} %collective-permute-done.2.c1, bf16[512,384]{1,0:T(8,128)(2,1)S(1)} %collective-permute-done.3.c2, bf16[512,384]{1,0:T(8,128)(2,1)S(1)} %collective-permute-done.7.c3, ...), custom_call_target="tpu_custom_call" | custom-call | flops 1000000000 | bytes 2752512 | tf_op jit(solution)/shard_map/pallas_call | solution.py:33
  24.5 1.5 %collective-permute-start.9 = (bf16[192,512]{1,0:T(8,128)(2,1)S(1)}, bf16[192,512]{1,0:T(8,128)(2,1)S(1)}, u32[]{:S(2)}, u32[]{:S(2)}) collective-permute-start(bf16[192,512]{1,0:T(8,128)(2,1)S(1)} %get-tuple-element.70), channel_id=1, source_target_pairs={{0,2},{1,3},{2,0},{3,1},{4,6},{5,7},{6,4},{7,5},{8,10},{9,11},{10,... | collective-permute-start | bytes 589832 | tf_op jit(solution)/shard_map/ppermute | solution.py:311
  26.8 4.1 %collective-permute-done.8.far = bf16[512,384]{1,0:T(8,128)(2,1)S(1)} collective-permute-done((bf16[512,384]{1,0:T(8,128)(2,1)S(1)}, bf16[512,384]{1,0:T(8,128)(2,1)S(1)}, u32[]{:S(2)}, u32[]{:S(2)}) %collective-permute-start.8) | collective-permute-done | bytes 393248 | tf_op jit(solution)/shard_map/ppermute | solution.py:302
  31.9 1.5 %collective-permute-start.10 = (bf16[320,512]{1,0:T(8,128)(2,1)S(1)}, bf16[320,512]{1,0:T(8,128)(2,1)S(1)}, u32[]{:S(2)}, u32[]{:S(2)}) collective-permute-start(bf16[320,512]{1,0:T(8,128)(2,1)S(1)} %get-tuple-element.72), channel_id=1, source_target_pairs={{0,2},{1,3},{2,0},{3,1},{4,6},{5,7},{6,4},{7,5},{8,10},{9,11},{10,... | collective-permute-start | bytes 983048 | tf_op jit(solution)/shard_map/ppermute | solution.py:311
  34.0 8.2 %collective-permute-done.10.par = bf16[320,512]{1,0:T(8,128)(2,1)S(1)} collective-permute-done((bf16[320,512]{1,0:T(8,128)(2,1)S(1)}, bf16[320,512]{1,0:T(8,128)(2,1)S(1)}, u32[]{:S(2)}, u32[]{:S(2)}) %collective-permute-start.10) | collective-permute-done | bytes 327712 | tf_op jit(solution)/shard_map/ppermute | solution.py:311
  42.7 1.1 collective-permute-done.12.sib_par
  43.9 7.4 %shard_map.89 = (bf16[64,512]{1,0:T(8,128)(2,1)S(1)}, bf16[64,512]{1,0:T(8,128)(2,1)S(1)}, f32[256,1024]{1,0:T(8,128)S(1)}, bf16[256,1024]{1,0:T(8,128)(2,1)S(1)}) custom-call(bf16[320,512]{1,0:T(8,128)(2,1)S(1)} %get-tuple-element.64.own, bf16[320,512]{1,0:T(8,128)(2,1)S(1)} %collective-permute-done.10.par, ...), custom_call_target="tpu_custom_call" | custom-call | flops 8000000000 | bytes 1703936 | tf_op jit(solution)/shard_map/pallas_call | solution.py:33
  51.4 1.8 %collective-permute-done.13.kv_got = bf16[256,1024]{1,0:T(8,128)(2,1)S(1)} collective-permute-done((bf16[256,1024]{1,0:T(8,128)(2,1)S(1)}, bf16[256,1024]{1,0:T(8,128)(2,1)S(1)}, u32[]{:S(2)}, u32[]{:S(2)}) %collective-permute-start.13) | collective-permute-done | bytes 524320 | tf_op jit(solution)/shard_map/ppermute | solution.py:308
  53.3 1.8 %collective-permute-start.14 = (bf16[320,512]{1,0:T(8,128)(2,1)S(1)}, bf16[320,512]{1,0:T(8,128)(2,1)S(1)}, u32[]{:S(2)}, u32[]{:S(2)}) collective-permute-start(bf16[320,512]{1,0:T(8,128)(2,1)S(1)} %get-tuple-element.80), channel_id=1, source_target_pairs={{0,2},{1,3},{2,0},{3,1},{4,6},{5,7},{6,4},{7,5},{8,10},{9,11},{10,... | collective-permute-start | bytes 983048 | tf_op jit(solution)/shard_map/ppermute | solution.py:311
  55.1 8.1 %collective-permute-done.14.other = bf16[320,512]{1,0:T(8,128)(2,1)S(1)} collective-permute-done((bf16[320,512]{1,0:T(8,128)(2,1)S(1)}, bf16[320,512]{1,0:T(8,128)(2,1)S(1)}, u32[]{:S(2)}, u32[]{:S(2)}) %collective-permute-start.14) | collective-permute-done | bytes 327712 | tf_op jit(solution)/shard_map/ppermute | solution.py:311
  63.8 1.1 collective-permute-start.16
  66.8 4.9 %collective-permute-done.16.got = bf16[384,512]{1,0:T(8,128)(2,1)S(1)} collective-permute-done((bf16[384,512]{1,0:T(8,128)(2,1)S(1)}, bf16[384,512]{1,0:T(8,128)(2,1)S(1)}, u32[]{:S(2)}, u32[]{:S(2)}) %collective-permute-start.16) | collective-permute-done | bytes 393248 | tf_op jit(solution)/shard_map/ppermute | solution.py:302
  71.7 2.7 %collective-permute-start.17 = (bf16[384,512]{1,0:T(8,128)(2,1)S(1)}, bf16[384,512]{1,0:T(8,128)(2,1)S(1)}, u32[]{:S(2)}, u32[]{:S(2)}) collective-permute-start(bf16[384,512]{1,0:T(8,128)(2,1)S(1)} %shard_map.94), channel_id=1, source_target_pairs={{0,12},{1,5},{2,14},{3,7},{4,8},{5,1},{6,10},{7,3},{8,4},{9,13},{1... | collective-permute-start | bytes 1179656 | tf_op jit(solution)/shard_map/ppermute | solution.py:302
  74.9 3.1 %collective-permute-done.15.alone = bf16[384,512]{1,0:T(8,128)(2,1)S(1)} collective-permute-done((bf16[384,512]{1,0:T(8,128)(2,1)S(1)}, bf16[384,512]{1,0:T(8,128)(2,1)S(1)}, u32[]{:S(2)}, u32[]{:S(2)}) %collective-permute-start.15) | collective-permute-done | bytes 393248 | tf_op jit(solution)/shard_map/ppermute | solution.py:302
  77.9 2.9 %collective-permute-done.17.joined = bf16[384,512]{1,0:T(8,128)(2,1)S(1)} collective-permute-done((bf16[384,512]{1,0:T(8,128)(2,1)S(1)}, bf16[384,512]{1,0:T(8,128)(2,1)S(1)}, u32[]{:S(2)}, u32[]{:S(2)}) %collective-permute-start.17) | collective-permute-done | bytes 393248 | tf_op jit(solution)/shard_map/ppermute | solution.py:302
  83.2 1.8 %collective-permute-start.20 = (bf16[576,384]{1,0:T(8,128)(2,1)S(1)}, bf16[576,384]{1,0:T(8,128)(2,1)S(1)}, u32[]{:S(2)}, u32[]{:S(2)}) collective-permute-start(bf16[576,384]{1,0:T(8,128)(2,1)S(1)} %shard_map.100), channel_id=1, source_target_pairs={{0,2},{1,19},{2,0},{3,17},{16,18},{17,3},{18,16},{19,1},{32,34},{3... | collective-permute-start | bytes 1327112 | tf_op jit(solution)/shard_map/ppermute | solution.py:305
  86.7 4.9 %collective-permute-done.20.got = bf16[576,384]{1,0:T(8,128)(2,1)S(1)} collective-permute-done((bf16[576,384]{1,0:T(8,128)(2,1)S(1)}, bf16[576,384]{1,0:T(8,128)(2,1)S(1)}, u32[]{:S(2)}, u32[]{:S(2)}) %collective-permute-start.20) | collective-permute-done | bytes 442400 | tf_op jit(solution)/shard_map/ppermute | solution.py:305
  91.7 3.0 %collective-permute-start.21 = (bf16[576,384]{1,0:T(8,128)(2,1)S(1)}, bf16[576,384]{1,0:T(8,128)(2,1)S(1)}, u32[]{:S(2)}, u32[]{:S(2)}) collective-permute-start(bf16[576,384]{1,0:T(8,128)(2,1)S(1)} %shard_map.101), channel_id=1, source_target_pairs={{0,18},{1,3},{2,16},{3,1},{16,2},{17,19},{18,0},{19,17},{32,50},{3... | collective-permute-start | bytes 1327112 | tf_op jit(solution)/shard_map/ppermute | solution.py:305
  95.5 2.7 %collective-permute-done.19.alone = bf16[576,384]{1,0:T(8,128)(2,1)S(1)} collective-permute-done((bf16[576,384]{1,0:T(8,128)(2,1)S(1)}, bf16[576,384]{1,0:T(8,128)(2,1)S(1)}, u32[]{:S(2)}, u32[]{:S(2)}) %collective-permute-start.19) | collective-permute-done | bytes 442400 | tf_op jit(solution)/shard_map/ppermute | solution.py:305
  98.2 3.3 %collective-permute-done.21.joined = bf16[576,384]{1,0:T(8,128)(2,1)S(1)} collective-permute-done((bf16[576,384]{1,0:T(8,128)(2,1)S(1)}, bf16[576,384]{1,0:T(8,128)(2,1)S(1)}, u32[]{:S(2)}, u32[]{:S(2)}) %collective-permute-start.21) | collective-permute-done | bytes 442400 | tf_op jit(solution)/shard_map/ppermute | solution.py:305
  101.6 2.0 %collective-permute-start.22 = (bf16[144,384]{1,0:T(8,128)(2,1)S(1)}, bf16[144,384]{1,0:T(8,128)(2,1)S(1)}, u32[]{:S(2)}, u32[]{:S(2)}) collective-permute-start(bf16[144,384]{1,0:T(8,128)(2,1)S(1)} %get-tuple-element.90), channel_id=1, source_target_pairs={{0,32},{1,33},{2,34},{3,35},{16,48},{17,49},{18,50},{19,51},{32,0}... | collective-permute-start | bytes 331784 | tf_op jit(solution)/shard_map/ppermute | solution.py:314
  103.7 2.5 %collective-permute-start.23 = (bf16[144,384]{1,0:T(8,128)(2,1)S(1)}, bf16[144,384]{1,0:T(8,128)(2,1)S(1)}, u32[]{:S(2)}, u32[]{:S(2)}) collective-permute-start(bf16[144,384]{1,0:T(8,128)(2,1)S(1)} %get-tuple-element.91), channel_id=1, source_target_pairs={{0,96},{1,97},{2,98},{3,99},{16,112},{17,113},{18,114},{19,115},{3... | collective-permute-start | bytes 331784 | tf_op jit(solution)/shard_map/ppermute | solution.py:314
  107.2 3.2 %collective-permute-done.23.r2 = bf16[144,384]{1,0:T(8,128)(2,1)S(1)} collective-permute-done((bf16[144,384]{1,0:T(8,128)(2,1)S(1)}, bf16[144,384]{1,0:T(8,128)(2,1)S(1)}, u32[]{:S(2)}, u32[]{:S(2)}) %collective-permute-start.23) | collective-permute-done | bytes 110624 | tf_op jit(solution)/shard_map/ppermute | solution.py:314
  110.5 1.9 %collective-permute-done.24.r3 = bf16[144,384]{1,0:T(8,128)(2,1)S(1)} collective-permute-done((bf16[144,384]{1,0:T(8,128)(2,1)S(1)}, bf16[144,384]{1,0:T(8,128)(2,1)S(1)}, u32[]{:S(2)}, u32[]{:S(2)}) %collective-permute-start.24) | collective-permute-done | bytes 110624 | tf_op jit(solution)/shard_map/ppermute | solution.py:314
  (60 shorter events, 18.5 us)
Async XLA Ops:
  0.0 7.4 %collective-permute-start.1 = (s32[32,512]{1,0:T(8,128)}, s32[32,512]{1,0:T(8,128)S(1)}, u32[]{:S(2)}, u32[]{:S(2)}) collective-permute-start(s32[32,512]{1,0:T(8,128)} %bitcast.11), channel_id=1, source_target_pairs={{1,0},{2,1},{3,2},{0,3},{5,4},{6,5},{7,6},{4,7},{9,8},{10,9},{11,1... | collective-permute-start | bytes 196616 | tf_op jit(solution)/shard_map/ppermute | solution.py:295
  1.0 6.4 %collective-permute-start = (s32[32,512]{1,0:T(8,128)}, s32[32,512]{1,0:T(8,128)S(1)}, u32[]{:S(2)}, u32[]{:S(2)}) collective-permute-start(s32[32,512]{1,0:T(8,128)} %bitcast.12), channel_id=1, source_target_pairs={{0,1},{1,2},{2,3},{3,0},{4,5},{5,6},{6,7},{7,4},{8,9},{9,10},{10,1... | collective-permute-start | bytes 196616 | tf_op jit(solution)/shard_map/ppermute | solution.py:294
  1.0 6.4 %copy-start.4 = (bf16[3,1536,384]{2,1,0:T(8,128)(2,1)S(1)}, bf16[3,1536,384]{2,1,0:T(8,128)(2,1)}, u32[]{:S(2)}) copy-start(bf16[3,1536,384]{2,1,0:T(8,128)(2,1)} %weight_ref.1) | copy-start | bytes 10616836
  1.0 13.4 %collective-permute-start.3 = (bf16[512,384]{1,0:T(8,128)(2,1)}, bf16[512,384]{1,0:T(8,128)(2,1)S(1)}, u32[]{:S(2)}, u32[]{:S(2)}) collective-permute-start(bf16[512,384]{1,0:T(8,128)(2,1)} %bitcast.7), channel_id=1, source_target_pairs={{0,12},{1,5},{2,14},{3,7},{4,8},{5,1},{6,10},{7,3},{8,4},{9,13},{1... | collective-permute-start | bytes 1179656 | tf_op jit(solution)/shard_map/ppermute | solution.py:302
  4.0 10.4 %collective-permute-start.2 = (bf16[512,384]{1,0:T(8,128)(2,1)}, bf16[512,384]{1,0:T(8,128)(2,1)S(1)}, u32[]{:S(2)}, u32[]{:S(2)}) collective-permute-start(bf16[512,384]{1,0:T(8,128)(2,1)} %bitcast.8), channel_id=1, source_target_pairs={{0,4},{1,13},{2,6},{3,15},{4,0},{5,9},{6,2},{7,11},{8,12},{9,5},{1... | collective-permute-start | bytes 1179656 | tf_op jit(solution)/shard_map/ppermute | solution.py:302
  6.0 1.4 %copy-start.9 = (s32[1,512,32]{1,2,0:T(8,128)S(1)}, s32[1,512,32]{1,2,0:T(8,128)}, u32[]{:S(2)}) copy-start(s32[1,512,32]{1,2,0:T(8,128)} %param.8) | copy-start | bytes 196612
  7.4 4.4 %copy-start = (bf16[1536,384]{1,0:T(8,128)(2,1)S(1)}, bf16[1536,384]{1,0:T(8,128)(2,1)}, u32[]{:S(2)}) copy-start(bf16[1536,384]{1,0:T(8,128)(2,1)} %wv.5) | copy-start | bytes 3538948
  7.4 4.4 %copy-start.1 = (bf16[1536,128]{1,0:T(8,128)(2,1)S(1)}, bf16[1536,128]{1,0:T(8,128)(2,1)}, u32[]{:S(2)}) copy-start(bf16[1536,128]{1,0:T(8,128)(2,1)} %wq.5) | copy-start | bytes 1179652
  7.4 4.4 %copy-start.2 = (bf16[1536,128]{1,0:T(8,128)(2,1)S(1)}, bf16[1536,128]{1,0:T(8,128)(2,1)}, u32[]{:S(2)}) copy-start(bf16[1536,128]{1,0:T(8,128)(2,1)} %wk.5) | copy-start | bytes 1179652
  10.7 10.1 %collective-permute-start.6 = (bf16[512,384]{1,0:T(8,128)(2,1)S(1)}, bf16[512,384]{1,0:T(8,128)(2,1)S(1)}, u32[]{:S(2)}, u32[]{:S(2)}) collective-permute-start(bf16[512,384]{1,0:T(8,128)(2,1)S(1)} %get-tuple-element.55.own), channel_id=1, source_target_pairs={{0,12},{1,5},{2,14},{3,7},{4,8},{5,1},{6,10},{7,3},{8,4},{9,13},{1... | collective-permute-start | bytes 1179656 | tf_op jit(solution)/shard_map/ppermute | solution.py:302
  12.4 10.8 %copy-start.3 = (bf16[1,512,384]{2,1,0:T(8,128)(2,1)S(1)}, bf16[1,512,384]{2,1,0:T(8,128)(2,1)}, u32[]{:S(2)}) copy-start(bf16[1,512,384]{2,1,0:T(8,128)(2,1)} %param.15) | copy-start | bytes 1179652
  12.4 10.8 %copy-start.5 = (bf16[384,1536]{1,0:T(8,128)(2,1)S(1)}, bf16[384,1536]{1,0:T(8,128)(2,1)}, u32[]{:S(2)}) copy-start(bf16[384,1536]{1,0:T(8,128)(2,1)} %w_ref.1) | copy-start | bytes 3538948
  14.5 8.0 %collective-permute-start.7 = (bf16[512,384]{1,0:T(8,128)(2,1)S(1)}, bf16[512,384]{1,0:T(8,128)(2,1)S(1)}, u32[]{:S(2)}, u32[]{:S(2)}) collective-permute-start(bf16[512,384]{1,0:T(8,128)(2,1)S(1)} %collective-permute-done.3.c2), channel_id=1, source_target_pairs={{0,4},{1,13},{2,6},{3,15},{4,0},{5,9},{6,2},{7,11},{8,12},{9,5},{1... | collective-permute-start | bytes 1179656 | tf_op jit(solution)/shard_map/ppermute | solution.py:302
  15.4 11.4 %collective-permute-start.5 = (bf16[512,384]{1,0:T(8,128)(2,1)S(1)}, bf16[512,384]{1,0:T(8,128)(2,1)S(1)}, u32[]{:S(2)}, u32[]{:S(2)}) collective-permute-start(bf16[512,384]{1,0:T(8,128)(2,1)S(1)} %get-tuple-element.55.own), channel_id=1, source_target_pairs={{0,4},{1,13},{2,6},{3,15},{4,0},{5,9},{6,2},{7,11},{8,12},{9,5},{1... | collective-permute-start | bytes 1179656 | tf_op jit(solution)/shard_map/ppermute | solution.py:302
  22.5 8.4 %collective-permute-start.8 = (bf16[512,384]{1,0:T(8,128)(2,1)S(1)}, bf16[512,384]{1,0:T(8,128)(2,1)S(1)}, u32[]{:S(2)}, u32[]{:S(2)}) collective-permute-start(bf16[512,384]{1,0:T(8,128)(2,1)S(1)} %collective-permute-done.6.second), channel_id=1, source_target_pairs={{0,4},{1,13},{2,6},{3,15},{4,0},{5,9},{6,2},{7,11},{8,12},{9,5},{1... | collective-permute-start | bytes 1179656 | tf_op jit(solution)/shard_map/ppermute | solution.py:302
  24.5 7.4 %collective-permute-start.9 = (bf16[192,512]{1,0:T(8,128)(2,1)S(1)}, bf16[192,512]{1,0:T(8,128)(2,1)S(1)}, u32[]{:S(2)}, u32[]{:S(2)}) collective-permute-start(bf16[192,512]{1,0:T(8,128)(2,1)S(1)} %get-tuple-element.70), channel_id=1, source_target_pairs={{0,2},{1,3},{2,0},{3,1},{4,6},{5,7},{6,4},{7,5},{8,10},{9,11},{10,... | collective-permute-start | bytes 589832 | tf_op jit(solution)/shard_map/ppermute | solution.py:311
  31.9 10.3 %collective-permute-start.10 = (bf16[320,512]{1,0:T(8,128)(2,1)S(1)}, bf16[320,512]{1,0:T(8,128)(2,1)S(1)}, u32[]{:S(2)}, u32[]{:S(2)}) collective-permute-start(bf16[320,512]{1,0:T(8,128)(2,1)S(1)} %get-tuple-element.72), channel_id=1, source_target_pairs={{0,2},{1,3},{2,0},{3,1},{4,6},{5,7},{6,4},{7,5},{8,10},{9,11},{10,... | collective-permute-start | bytes 983048 | tf_op jit(solution)/shard_map/ppermute | solution.py:311
  33.4 9.3 %collective-permute-start.11 = (bf16[320,512]{1,0:T(8,128)(2,1)S(1)}, bf16[320,512]{1,0:T(8,128)(2,1)S(1)}, u32[]{:S(2)}, u32[]{:S(2)}) collective-permute-start(bf16[320,512]{1,0:T(8,128)(2,1)S(1)} %get-tuple-element.64.own), channel_id=1, source_target_pairs={{0,1},{1,0},{2,3},{3,2},{4,5},{5,4},{6,7},{7,6},{8,9},{9,8},{10,11... | collective-permute-start | bytes 983048 | tf_op jit(solution)/shard_map/ppermute | solution.py:308
  42.2 1.6 %collective-permute-start.12 = (bf16[320,512]{1,0:T(8,128)(2,1)S(1)}, bf16[320,512]{1,0:T(8,128)(2,1)S(1)}, u32[]{:S(2)}, u32[]{:S(2)}) collective-permute-start(bf16[320,512]{1,0:T(8,128)(2,1)S(1)} %collective-permute-done.10.par), channel_id=1, source_target_pairs={{0,1},{1,0},{2,3},{3,2},{4,5},{5,4},{6,7},{7,6},{8,9},{9,8},{10,11... | collective-permute-start | bytes 983048 | tf_op jit(solution)/shard_map/ppermute | solution.py:308
  42.4 40.4 %collective-permute-start.4 = (bf16[2304,512]{1,0:T(8,128)(2,1)S(1)}, bf16[2304,512]{1,0:T(8,128)(2,1)S(1)}, u32[]{:S(2)}, u32[]{:S(2)}) collective-permute-start(bf16[2304,512]{1,0:T(8,128)(2,1)S(1)} %get-tuple-element.54), channel_id=1, source_target_pairs={{0,1},{1,0},{2,3},{3,2},{4,5},{5,4},{6,7},{7,6},{8,9},{9,8},{10,11... | collective-permute-start | bytes 7077896 | tf_op jit(solution)/shard_map/ppermute | solution.py:308
  51.2 2.0 %collective-permute-start.13 = (bf16[256,1024]{1,0:T(8,128)(2,1)S(1)}, bf16[256,1024]{1,0:T(8,128)(2,1)S(1)}, u32[]{:S(2)}, u32[]{:S(2)}) collective-permute-start(bf16[256,1024]{1,0:T(8,128)(2,1)S(1)} %get-tuple-element.78), channel_id=1, source_target_pairs={{0,1},{1,0},{2,3},{3,2},{4,5},{5,4},{6,7},{7,6},{8,9},{9,8},{10,11... | collective-permute-start | bytes 1572872 | tf_op jit(solution)/shard_map/ppermute | solution.py:308
  53.3 9.8 %collective-permute-start.14 = (bf16[320,512]{1,0:T(8,128)(2,1)S(1)}, bf16[320,512]{1,0:T(8,128)(2,1)S(1)}, u32[]{:S(2)}, u32[]{:S(2)}) collective-permute-start(bf16[320,512]{1,0:T(8,128)(2,1)S(1)} %get-tuple-element.80), channel_id=1, source_target_pairs={{0,2},{1,3},{2,0},{3,1},{4,6},{5,7},{6,4},{7,5},{8,10},{9,11},{10,... | collective-permute-start | bytes 983048 | tf_op jit(solution)/shard_map/ppermute | solution.py:311
  63.8 7.9 %collective-permute-start.16 = (bf16[384,512]{1,0:T(8,128)(2,1)S(1)}, bf16[384,512]{1,0:T(8,128)(2,1)S(1)}, u32[]{:S(2)}, u32[]{:S(2)}) collective-permute-start(bf16[384,512]{1,0:T(8,128)(2,1)S(1)} %get-tuple-element.86), channel_id=1, source_target_pairs={{0,4},{1,13},{2,6},{3,15},{4,0},{5,9},{6,2},{7,11},{8,12},{9,5},{1... | collective-permute-start | bytes 1179656 | tf_op jit(solution)/shard_map/ppermute | solution.py:302
  65.7 12.2 %collective-permute-start.15 = (bf16[384,512]{1,0:T(8,128)(2,1)S(1)}, bf16[384,512]{1,0:T(8,128)(2,1)S(1)}, u32[]{:S(2)}, u32[]{:S(2)}) collective-permute-start(bf16[384,512]{1,0:T(8,128)(2,1)S(1)} %get-tuple-element.84), channel_id=1, source_target_pairs={{0,4},{1,13},{2,6},{3,15},{4,0},{5,9},{6,2},{7,11},{8,12},{9,5},{1... | collective-permute-start | bytes 1179656 | tf_op jit(solution)/shard_map/ppermute | solution.py:302
  71.7 9.1 %collective-permute-start.17 = (bf16[384,512]{1,0:T(8,128)(2,1)S(1)}, bf16[384,512]{1,0:T(8,128)(2,1)S(1)}, u32[]{:S(2)}, u32[]{:S(2)}) collective-permute-start(bf16[384,512]{1,0:T(8,128)(2,1)S(1)} %shard_map.94), channel_id=1, source_target_pairs={{0,12},{1,5},{2,14},{3,7},{4,8},{5,1},{6,10},{7,3},{8,4},{9,13},{1... | collective-permute-start | bytes 1179656 | tf_op jit(solution)/shard_map/ppermute | solution.py:302
  80.9 1.8 %collective-permute-start.18 = (bf16[384,512]{1,0:T(8,128)(2,1)S(1)}, bf16[384,512]{1,0:T(8,128)(2,1)S(1)}, u32[]{:S(2)}, u32[]{:S(2)}) collective-permute-start(bf16[384,512]{1,0:T(8,128)(2,1)S(1)} %shard_map.95.grad.g_mine), channel_id=1, source_target_pairs={{0,1},{1,0},{2,3},{3,2},{4,5},{5,4},{6,7},{7,6},{8,9},{9,8},{10,11... | collective-permute-start | bytes 1179656 | tf_op jit(solution)/shard_map/ppermute | solution.py:308
  83.2 8.4 %collective-permute-start.20 = (bf16[576,384]{1,0:T(8,128)(2,1)S(1)}, bf16[576,384]{1,0:T(8,128)(2,1)S(1)}, u32[]{:S(2)}, u32[]{:S(2)}) collective-permute-start(bf16[576,384]{1,0:T(8,128)(2,1)S(1)} %shard_map.100), channel_id=1, source_target_pairs={{0,2},{1,19},{2,0},{3,17},{16,18},{17,3},{18,16},{19,1},{32,34},{3... | collective-permute-start | bytes 1327112 | tf_op jit(solution)/shard_map/ppermute | solution.py:305
  85.5 12.7 %collective-permute-start.19 = (bf16[576,384]{1,0:T(8,128)(2,1)S(1)}, bf16[576,384]{1,0:T(8,128)(2,1)S(1)}, u32[]{:S(2)}, u32[]{:S(2)}) collective-permute-start(bf16[576,384]{1,0:T(8,128)(2,1)S(1)} %shard_map.98), channel_id=1, source_target_pairs={{0,2},{1,19},{2,0},{3,17},{16,18},{17,3},{18,16},{19,1},{32,34},{3... | collective-permute-start | bytes 1327112 | tf_op jit(solution)/shard_map/ppermute | solution.py:305
  91.7 9.8 %collective-permute-start.21 = (bf16[576,384]{1,0:T(8,128)(2,1)S(1)}, bf16[576,384]{1,0:T(8,128)(2,1)S(1)}, u32[]{:S(2)}, u32[]{:S(2)}) collective-permute-start(bf16[576,384]{1,0:T(8,128)(2,1)S(1)} %shard_map.101), channel_id=1, source_target_pairs={{0,18},{1,3},{2,16},{3,1},{16,2},{17,19},{18,0},{19,17},{32,50},{3... | collective-permute-start | bytes 1327112 | tf_op jit(solution)/shard_map/ppermute | solution.py:305
  101.6 5.6 %collective-permute-start.22 = (bf16[144,384]{1,0:T(8,128)(2,1)S(1)}, bf16[144,384]{1,0:T(8,128)(2,1)S(1)}, u32[]{:S(2)}, u32[]{:S(2)}) collective-permute-start(bf16[144,384]{1,0:T(8,128)(2,1)S(1)} %get-tuple-element.90), channel_id=1, source_target_pairs={{0,32},{1,33},{2,34},{3,35},{16,48},{17,49},{18,50},{19,51},{32,0}... | collective-permute-start | bytes 331784 | tf_op jit(solution)/shard_map/ppermute | solution.py:314
  103.7 6.8 %collective-permute-start.23 = (bf16[144,384]{1,0:T(8,128)(2,1)S(1)}, bf16[144,384]{1,0:T(8,128)(2,1)S(1)}, u32[]{:S(2)}, u32[]{:S(2)}) collective-permute-start(bf16[144,384]{1,0:T(8,128)(2,1)S(1)} %get-tuple-element.91), channel_id=1, source_target_pairs={{0,96},{1,97},{2,98},{3,99},{16,112},{17,113},{18,114},{19,115},{3... | collective-permute-start | bytes 331784 | tf_op jit(solution)/shard_map/ppermute | solution.py:314
  106.2 6.3 %collective-permute-start.24 = (bf16[144,384]{1,0:T(8,128)(2,1)S(1)}, bf16[144,384]{1,0:T(8,128)(2,1)S(1)}, u32[]{:S(2)}, u32[]{:S(2)}) collective-permute-start(bf16[144,384]{1,0:T(8,128)(2,1)S(1)} %get-tuple-element.92), channel_id=1, source_target_pairs={{0,64},{1,65},{2,66},{3,67},{16,80},{17,81},{18,82},{19,83},{32,96... | collective-permute-start | bytes 331784 | tf_op jit(solution)/shard_map/ppermute | solution.py:314
  (3 other events, 3.3 us)

commit v7 on v6

--- a/solution.py
+++ b/solution.py
@@ -65,13 +65,14 @@
     return jax.nn.gelu(x, approximate=True)
 
 
-def stem_kernel(marks_ref, stem_ref, act_ref):
+def stem_kernel(marks_ref, stem_ref, act_ref, own_ref):
     hot = one_hot(marks_ref[...])
+    own_ref[...] = nn(hot, stem_ref[:, block_at(lax.axis_index("tensor"), 384)])
     for j in range(0, stem_ref.shape[1], 256):
         act_ref[:, j : j + 256] = gelu(nn(hot, stem_ref[:, j : j + 256])).astype(bf16)
 
 
-def conv_kernel(marks_ref, low_ref, high_ref, stem_ref, act_ref, weight_ref, hidden_ref, ext_ref):
+def conv_kernel(own_ref, low_ref, high_ref, stem_ref, act_ref, weight_ref, hidden_ref, ext_ref):
     rows = act_ref.shape[0]
     section = lax.axis_index("section")
     edge = one_hot(jnp.concatenate([low_ref[:, rows - HALO :], high_ref[:, :HALO]], axis=1))
@@ -79,7 +80,7 @@
     ext_ref[0:HALO] = jnp.where(section > 0, edge_act[:HALO], 0)
     ext_ref[HALO : HALO + rows] = act_ref[...]
     ext_ref[HALO + rows :] = jnp.where(section < 3, edge_act[HALO:], 0)
-    total = nn(one_hot(marks_ref[...]), stem_ref[:, block_at(lax.axis_index("tensor"), 384)])
+    total = own_ref[...]
     for k in range(3):
         total = total + nn(ext_ref[k * HALO : k * HALO + rows], weight_ref[k])
     hidden_ref[...] = total.astype(bf16)
@@ -314,12 +315,12 @@
         return lax.ppermute(value, flat, [(i, i ^ (8 * d)) for i in range(32)])
 
     second = y_way(cot, 1)
-    (act,) = call(stem_kernel, [((rows, 1536), bf16)], marks, stem_w, flops=4e9, vmem=16)
+    act, stem_own = call(stem_kernel, [((rows, 1536), bf16), ((rows, 384), f32)], marks, stem_w, flops=4e9, vmem=16)
     first = y_way(cot, 0)
     hidden, ext = call(
         conv_kernel,
         [((rows, 384), bf16), ((rows + 2 * HALO, 1536), bf16)],
-        marks, low, high, stem_w, act, conv_w,
+        stem_own, low, high, stem_w, act, conv_w,
         flops=2e9,
     )
     cots = [cot, first, second]

time: 113 us -> 113 us (level)
  no operation moved by 1% of the time
where the time goes in v7:
time: 113 us
  waiting for transfers between devices  56.9 us (50%)
  starting transfers between devices  30.1 us (27%)
  Pallas kernels  24 us (21%)
  local copies, waits for them, and re-layouts  1.87 us (2%)
    pallas_call x22, Pallas kernels, call(): pl.pallas_call(kernel, out_shape=[jax.ShapeDtypeStruct(shape, kind) for s...  24 us
    ppermute x9, waiting for transfers between devices, y_way(): return lax.ppermute(value, ('tensor', 'section'), pairs)  20.8 us
    ppermute x3, waiting for transfers between devices, over_chip(): return lax.ppermute(value, 'section', [(i, i ^ 2) for i in range(4)])  16.3 us
    ppermute x9, starting transfers between devices, y_way(): return lax.ppermute(value, ('tensor', 'section'), pairs)  12 us
    ppermute x3, waiting for transfers between devices, x_way(): lax.ppermute(value, flat, [(i, i ^ 2 * (1, 3)[(i + way) % 2]) for i in ra...  10.9 us
    ppermute x3, starting transfers between devices, over_z(): return lax.ppermute(value, flat, [(i, i ^ 8 * d) for i in range(32)])  5.58 us
    ppermute x3, starting transfers between devices, x_way(): lax.ppermute(value, flat, [(i, i ^ 2 * (1, 3)[(i + way) % 2]) for i in ra...  5.23 us
    ppermute x3, waiting for transfers between devices, over_z(): return lax.ppermute(value, flat, [(i, i ^ 8 * d) for i in range(32)])  5.18 us
  transfers between devices with their start and end apart: 25, of which 16 were waited for; matrix products, arithmetic and copies ran while one was open for 0% of the time, Pallas kernels for 20%

profile of v7, /device:TPU:0, one launch (start us, length us, event | category | flops | bytes accessed | tf_op | source)
XLA Modules:
  0.0 113.1 jit_solution(5127845174146297850)
XLA Ops:
  1.0 3.0 %collective-permute-start.3 = (bf16[512,384]{1,0:T(8,128)(2,1)}, bf16[512,384]{1,0:T(8,128)(2,1)S(1)}, u32[]{:S(2)}, u32[]{:S(2)}) collective-permute-start(bf16[512,384]{1,0:T(8,128)(2,1)} %bitcast.7), channel_id=1, source_target_pairs={{0,12},{1,5},{2,14},{3,7},{4,8},{5,1},{6,10},{7,3},{8,4},{9,13},{1... | collective-permute-start | bytes 1179656 | tf_op jit(solution)/shard_map/ppermute | solution.py:303
  6.0 1.5 %shard_map.82 = (bf16[512,1536]{1,0:T(8,128)(2,1)S(1)}, f32[512,384]{1,0:T(8,128)S(1)}) custom-call(s32[32,512]{1,0:T(8,128)S(1)} %bitcast.13, bf16[128,1536]{1,0:T(8,128)(2,1)S(1)} %copy-done.6), custom_call_target="tpu_custom_call" | custom-call | flops 4000000000 | bytes 458752 | tf_op jit(solution)/shard_map/pallas_call | solution.py:33
  7.5 3.0 %shard_map.83 = (bf16[512,384]{1,0:T(8,128)(2,1)S(1)}, bf16[576,1536]{1,0:T(8,128)(2,1)S(1)}) custom-call(f32[512,384]{1,0:T(8,128)S(1)} %get-tuple-element.51.own_ref, s32[32,512]{1,0:T(8,128)S(1)} %collective-permute-done.low_ref, s32[32,512]{1,0:T(8,128)S(1)} %collective-permute-done.1.high_ref, bf16[128,1536]{1,0:T(8,128)(2,1)S(1)} %copy-done.7, ...), custom_call_target="tpu_custom_call" | custom-call | flops 2000000000 | bytes 6422528 | tf_op jit(solution)/shard_map/pallas_call | solution.py:33
  10.6 1.1 %collective-permute-start.6 = (bf16[512,384]{1,0:T(8,128)(2,1)S(1)}, bf16[512,384]{1,0:T(8,128)(2,1)S(1)}, u32[]{:S(2)}, u32[]{:S(2)}) collective-permute-start(bf16[512,384]{1,0:T(8,128)(2,1)S(1)} %get-tuple-element.59.own), channel_id=1, source_target_pairs={{0,12},{1,5},{2,14},{3,7},{4,8},{5,1},{6,10},{7,3},{8,4},{9,13},{1... | collective-permute-start | bytes 1179656 | tf_op jit(solution)/shard_map/ppermute | solution.py:303
  12.3 2.1 %shard_map.84 = (bf16[2304,512]{1,0:T(8,128)(2,1)S(1)}, bf16[2304,512]{1,0:T(8,128)(2,1)S(1)}) custom-call(bf16[576,1536]{1,0:T(8,128)(2,1)S(1)} %get-tuple-element.54.ext_ref), custom_call_target="tpu_custom_call" | custom-call | flops 3000000000 | bytes 1769472 | tf_op jit(solution)/shard_map/pallas_call | solution.py:33
  15.4 1.2 %collective-permute-start.5 = (bf16[512,384]{1,0:T(8,128)(2,1)S(1)}, bf16[512,384]{1,0:T(8,128)(2,1)S(1)}, u32[]{:S(2)}, u32[]{:S(2)}) collective-permute-start(bf16[512,384]{1,0:T(8,128)(2,1)S(1)} %get-tuple-element.59.own), channel_id=1, source_target_pairs={{0,4},{1,13},{2,6},{3,15},{4,0},{5,9},{6,2},{7,11},{8,12},{9,5},{1... | collective-permute-start | bytes 1179656 | tf_op jit(solution)/shard_map/ppermute | solution.py:303
  16.5 4.2 %collective-permute-done.6.second = bf16[512,384]{1,0:T(8,128)(2,1)S(1)} collective-permute-done((bf16[512,384]{1,0:T(8,128)(2,1)S(1)}, bf16[512,384]{1,0:T(8,128)(2,1)S(1)}, u32[]{:S(2)}, u32[]{:S(2)}) %collective-permute-start.6) | collective-permute-done | bytes 393248 | tf_op jit(solution)/shard_map/ppermute | solution.py:303
  20.7 1.7 %collective-permute-done.7.c3 = bf16[512,384]{1,0:T(8,128)(2,1)S(1)} collective-permute-done((bf16[512,384]{1,0:T(8,128)(2,1)S(1)}, bf16[512,384]{1,0:T(8,128)(2,1)S(1)}, u32[]{:S(2)}, u32[]{:S(2)}) %collective-permute-start.7) | collective-permute-done | bytes 393248 | tf_op jit(solution)/shard_map/ppermute | solution.py:303
  23.2 1.2 %shard_map.88 = (bf16[192,512]{1,0:T(8,128)(2,1)S(1)}, bf16[192,512]{1,0:T(8,128)(2,1)S(1)}) custom-call(bf16[512,384]{1,0:T(8,128)(2,1)S(1)} %bitcast.9, bf16[512,384]{1,0:T(8,128)(2,1)S(1)} %collective-permute-done.2.c1, bf16[512,384]{1,0:T(8,128)(2,1)S(1)} %collective-permute-done.3.c2, bf16[512,384]{1,0:T(8,128)(2,1)S(1)} %collective-permute-done.7.c3, ...), custom_call_target="tpu_custom_call" | custom-call | flops 1000000000 | bytes 2752512 | tf_op jit(solution)/shard_map/pallas_call | solution.py:33
  24.4 1.5 %collective-permute-start.9 = (bf16[192,512]{1,0:T(8,128)(2,1)S(1)}, bf16[192,512]{1,0:T(8,128)(2,1)S(1)}, u32[]{:S(2)}, u32[]{:S(2)}) collective-permute-start(bf16[192,512]{1,0:T(8,128)(2,1)S(1)} %get-tuple-element.74), channel_id=1, source_target_pairs={{0,2},{1,3},{2,0},{3,1},{4,6},{5,7},{6,4},{7,5},{8,10},{9,11},{10,... | collective-permute-start | bytes 589832 | tf_op jit(solution)/shard_map/ppermute | solution.py:312
  26.8 4.1 %collective-permute-done.8.far = bf16[512,384]{1,0:T(8,128)(2,1)S(1)} collective-permute-done((bf16[512,384]{1,0:T(8,128)(2,1)S(1)}, bf16[512,384]{1,0:T(8,128)(2,1)S(1)}, u32[]{:S(2)}, u32[]{:S(2)}) %collective-permute-start.8) | collective-permute-done | bytes 393248 | tf_op jit(solution)/shard_map/ppermute | solution.py:303
  31.8 1.6 %collective-permute-start.10 = (bf16[320,512]{1,0:T(8,128)(2,1)S(1)}, bf16[320,512]{1,0:T(8,128)(2,1)S(1)}, u32[]{:S(2)}, u32[]{:S(2)}) collective-permute-start(bf16[320,512]{1,0:T(8,128)(2,1)S(1)} %get-tuple-element.76), channel_id=1, source_target_pairs={{0,2},{1,3},{2,0},{3,1},{4,6},{5,7},{6,4},{7,5},{8,10},{9,11},{10,... | collective-permute-start | bytes 983048 | tf_op jit(solution)/shard_map/ppermute | solution.py:312
  34.0 8.2 %collective-permute-done.10.par = bf16[320,512]{1,0:T(8,128)(2,1)S(1)} collective-permute-done((bf16[320,512]{1,0:T(8,128)(2,1)S(1)}, bf16[320,512]{1,0:T(8,128)(2,1)S(1)}, u32[]{:S(2)}, u32[]{:S(2)}) %collective-permute-start.10) | collective-permute-done | bytes 327712 | tf_op jit(solution)/shard_map/ppermute | solution.py:312
  42.7 1.1 collective-permute-done.12.sib_par
  43.8 7.4 %shard_map.89 = (bf16[64,512]{1,0:T(8,128)(2,1)S(1)}, bf16[64,512]{1,0:T(8,128)(2,1)S(1)}, f32[256,1024]{1,0:T(8,128)S(1)}, bf16[256,1024]{1,0:T(8,128)(2,1)S(1)}) custom-call(bf16[320,512]{1,0:T(8,128)(2,1)S(1)} %get-tuple-element.68.own, bf16[320,512]{1,0:T(8,128)(2,1)S(1)} %collective-permute-done.10.par, ...), custom_call_target="tpu_custom_call" | custom-call | flops 8000000000 | bytes 1703936 | tf_op jit(solution)/shard_map/pallas_call | solution.py:33
  51.4 1.8 %collective-permute-done.13.kv_got = bf16[256,1024]{1,0:T(8,128)(2,1)S(1)} collective-permute-done((bf16[256,1024]{1,0:T(8,128)(2,1)S(1)}, bf16[256,1024]{1,0:T(8,128)(2,1)S(1)}, u32[]{:S(2)}, u32[]{:S(2)}) %collective-permute-start.13) | collective-permute-done | bytes 524320 | tf_op jit(solution)/shard_map/ppermute | solution.py:309
  53.3 1.8 %collective-permute-start.14 = (bf16[320,512]{1,0:T(8,128)(2,1)S(1)}, bf16[320,512]{1,0:T(8,128)(2,1)S(1)}, u32[]{:S(2)}, u32[]{:S(2)}) collective-permute-start(bf16[320,512]{1,0:T(8,128)(2,1)S(1)} %get-tuple-element.84), channel_id=1, source_target_pairs={{0,2},{1,3},{2,0},{3,1},{4,6},{5,7},{6,4},{7,5},{8,10},{9,11},{10,... | collective-permute-start | bytes 983048 | tf_op jit(solution)/shard_map/ppermute | solution.py:312
  55.0 8.1 %collective-permute-done.14.other = bf16[320,512]{1,0:T(8,128)(2,1)S(1)} collective-permute-done((bf16[320,512]{1,0:T(8,128)(2,1)S(1)}, bf16[320,512]{1,0:T(8,128)(2,1)S(1)}, u32[]{:S(2)}, u32[]{:S(2)}) %collective-permute-start.14) | collective-permute-done | bytes 327712 | tf_op jit(solution)/shard_map/ppermute | solution.py:312
  63.8 1.1 collective-permute-start.16
  66.7 4.9 %collective-permute-done.16.got = bf16[384,512]{1,0:T(8,128)(2,1)S(1)} collective-permute-done((bf16[384,512]{1,0:T(8,128)(2,1)S(1)}, bf16[384,512]{1,0:T(8,128)(2,1)S(1)}, u32[]{:S(2)}, u32[]{:S(2)}) %collective-permute-start.16) | collective-permute-done | bytes 393248 | tf_op jit(solution)/shard_map/ppermute | solution.py:303
  71.7 2.7 %collective-permute-start.17 = (bf16[384,512]{1,0:T(8,128)(2,1)S(1)}, bf16[384,512]{1,0:T(8,128)(2,1)S(1)}, u32[]{:S(2)}, u32[]{:S(2)}) collective-permute-start(bf16[384,512]{1,0:T(8,128)(2,1)S(1)} %shard_map.94), channel_id=1, source_target_pairs={{0,12},{1,5},{2,14},{3,7},{4,8},{5,1},{6,10},{7,3},{8,4},{9,13},{1... | collective-permute-start | bytes 1179656 | tf_op jit(solution)/shard_map/ppermute | solution.py:303
  74.9 3.0 %collective-permute-done.15.alone = bf16[384,512]{1,0:T(8,128)(2,1)S(1)} collective-permute-done((bf16[384,512]{1,0:T(8,128)(2,1)S(1)}, bf16[384,512]{1,0:T(8,128)(2,1)S(1)}, u32[]{:S(2)}, u32[]{:S(2)}) %collective-permute-start.15) | collective-permute-done | bytes 393248 | tf_op jit(solution)/shard_map/ppermute | solution.py:303
  77.9 2.9 %collective-permute-done.17.joined = bf16[384,512]{1,0:T(8,128)(2,1)S(1)} collective-permute-done((bf16[384,512]{1,0:T(8,128)(2,1)S(1)}, bf16[384,512]{1,0:T(8,128)(2,1)S(1)}, u32[]{:S(2)}, u32[]{:S(2)}) %collective-permute-start.17) | collective-permute-done | bytes 393248 | tf_op jit(solution)/shard_map/ppermute | solution.py:303
  83.2 1.8 %collective-permute-start.20 = (bf16[576,384]{1,0:T(8,128)(2,1)S(1)}, bf16[576,384]{1,0:T(8,128)(2,1)S(1)}, u32[]{:S(2)}, u32[]{:S(2)}) collective-permute-start(bf16[576,384]{1,0:T(8,128)(2,1)S(1)} %shard_map.100), channel_id=1, source_target_pairs={{0,2},{1,19},{2,0},{3,17},{16,18},{17,3},{18,16},{19,1},{32,34},{3... | collective-permute-start | bytes 1327112 | tf_op jit(solution)/shard_map/ppermute | solution.py:306
  86.7 4.9 %collective-permute-done.20.got = bf16[576,384]{1,0:T(8,128)(2,1)S(1)} collective-permute-done((bf16[576,384]{1,0:T(8,128)(2,1)S(1)}, bf16[576,384]{1,0:T(8,128)(2,1)S(1)}, u32[]{:S(2)}, u32[]{:S(2)}) %collective-permute-start.20) | collective-permute-done | bytes 442400 | tf_op jit(solution)/shard_map/ppermute | solution.py:306
  91.7 3.0 %collective-permute-start.21 = (bf16[576,384]{1,0:T(8,128)(2,1)S(1)}, bf16[576,384]{1,0:T(8,128)(2,1)S(1)}, u32[]{:S(2)}, u32[]{:S(2)}) collective-permute-start(bf16[576,384]{1,0:T(8,128)(2,1)S(1)} %shard_map.101), channel_id=1, source_target_pairs={{0,18},{1,3},{2,16},{3,1},{16,2},{17,19},{18,0},{19,17},{32,50},{3... | collective-permute-start | bytes 1327112 | tf_op jit(solution)/shard_map/ppermute | solution.py:306
  95.5 2.7 %collective-permute-done.19.alone = bf16[576,384]{1,0:T(8,128)(2,1)S(1)} collective-permute-done((bf16[576,384]{1,0:T(8,128)(2,1)S(1)}, bf16[576,384]{1,0:T(8,128)(2,1)S(1)}, u32[]{:S(2)}, u32[]{:S(2)}) %collective-permute-start.19) | collective-permute-done | bytes 442400 | tf_op jit(solution)/shard_map/ppermute | solution.py:306
  98.2 3.3 %collective-permute-done.21.joined = bf16[576,384]{1,0:T(8,128)(2,1)S(1)} collective-permute-done((bf16[576,384]{1,0:T(8,128)(2,1)S(1)}, bf16[576,384]{1,0:T(8,128)(2,1)S(1)}, u32[]{:S(2)}, u32[]{:S(2)}) %collective-permute-start.21) | collective-permute-done | bytes 442400 | tf_op jit(solution)/shard_map/ppermute | solution.py:306
  101.6 2.0 %collective-permute-start.22 = (bf16[144,384]{1,0:T(8,128)(2,1)S(1)}, bf16[144,384]{1,0:T(8,128)(2,1)S(1)}, u32[]{:S(2)}, u32[]{:S(2)}) collective-permute-start(bf16[144,384]{1,0:T(8,128)(2,1)S(1)} %get-tuple-element.94), channel_id=1, source_target_pairs={{0,32},{1,33},{2,34},{3,35},{16,48},{17,49},{18,50},{19,51},{32,0}... | collective-permute-start | bytes 331784 | tf_op jit(solution)/shard_map/ppermute | solution.py:315
  103.6 2.5 %collective-permute-start.23 = (bf16[144,384]{1,0:T(8,128)(2,1)S(1)}, bf16[144,384]{1,0:T(8,128)(2,1)S(1)}, u32[]{:S(2)}, u32[]{:S(2)}) collective-permute-start(bf16[144,384]{1,0:T(8,128)(2,1)S(1)} %get-tuple-element.95), channel_id=1, source_target_pairs={{0,96},{1,97},{2,98},{3,99},{16,112},{17,113},{18,114},{19,115},{3... | collective-permute-start | bytes 331784 | tf_op jit(solution)/shard_map/ppermute | solution.py:315
  107.2 3.3 %collective-permute-done.23.r2 = bf16[144,384]{1,0:T(8,128)(2,1)S(1)} collective-permute-done((bf16[144,384]{1,0:T(8,128)(2,1)S(1)}, bf16[144,384]{1,0:T(8,128)(2,1)S(1)}, u32[]{:S(2)}, u32[]{:S(2)}) %collective-permute-start.23) | collective-permute-done | bytes 110624 | tf_op jit(solution)/shard_map/ppermute | solution.py:315
  110.5 1.9 %collective-permute-done.24.r3 = bf16[144,384]{1,0:T(8,128)(2,1)S(1)} collective-permute-done((bf16[144,384]{1,0:T(8,128)(2,1)S(1)}, bf16[144,384]{1,0:T(8,128)(2,1)S(1)}, u32[]{:S(2)}, u32[]{:S(2)}) %collective-permute-start.24) | collective-permute-done | bytes 110624 | tf_op jit(solution)/shard_map/ppermute | solution.py:315
  (58 shorter events, 18.5 us)
Async XLA Ops:
  0.0 7.5 %collective-permute-start.1 = (s32[32,512]{1,0:T(8,128)}, s32[32,512]{1,0:T(8,128)S(1)}, u32[]{:S(2)}, u32[]{:S(2)}) collective-permute-start(s32[32,512]{1,0:T(8,128)} %bitcast.11), channel_id=1, source_target_pairs={{1,0},{2,1},{3,2},{0,3},{5,4},{6,5},{7,6},{4,7},{9,8},{10,9},{11,1... | collective-permute-start | bytes 196616 | tf_op jit(solution)/shard_map/ppermute | solution.py:296
  1.0 6.5 %collective-permute-start = (s32[32,512]{1,0:T(8,128)}, s32[32,512]{1,0:T(8,128)S(1)}, u32[]{:S(2)}, u32[]{:S(2)}) collective-permute-start(s32[32,512]{1,0:T(8,128)} %bitcast.12), channel_id=1, source_target_pairs={{0,1},{1,2},{2,3},{3,0},{4,5},{5,6},{6,7},{7,4},{8,9},{9,10},{10,1... | collective-permute-start | bytes 196616 | tf_op jit(solution)/shard_map/ppermute | solution.py:295
  1.0 6.5 %copy-start.4 = (bf16[3,1536,384]{2,1,0:T(8,128)(2,1)S(1)}, bf16[3,1536,384]{2,1,0:T(8,128)(2,1)}, u32[]{:S(2)}) copy-start(bf16[3,1536,384]{2,1,0:T(8,128)(2,1)} %weight_ref.1) | copy-start | bytes 10616836
  1.0 13.4 %collective-permute-start.3 = (bf16[512,384]{1,0:T(8,128)(2,1)}, bf16[512,384]{1,0:T(8,128)(2,1)S(1)}, u32[]{:S(2)}, u32[]{:S(2)}) collective-permute-start(bf16[512,384]{1,0:T(8,128)(2,1)} %bitcast.7), channel_id=1, source_target_pairs={{0,12},{1,5},{2,14},{3,7},{4,8},{5,1},{6,10},{7,3},{8,4},{9,13},{1... | collective-permute-start | bytes 1179656 | tf_op jit(solution)/shard_map/ppermute | solution.py:303
  4.0 10.4 %collective-permute-start.2 = (bf16[512,384]{1,0:T(8,128)(2,1)}, bf16[512,384]{1,0:T(8,128)(2,1)S(1)}, u32[]{:S(2)}, u32[]{:S(2)}) collective-permute-start(bf16[512,384]{1,0:T(8,128)(2,1)} %bitcast.8), channel_id=1, source_target_pairs={{0,4},{1,13},{2,6},{3,15},{4,0},{5,9},{6,2},{7,11},{8,12},{9,5},{1... | collective-permute-start | bytes 1179656 | tf_op jit(solution)/shard_map/ppermute | solution.py:303
  6.0 1.5 %copy-start.7 = (bf16[128,1536]{1,0:T(8,128)(2,1)S(1)}, bf16[128,1536]{1,0:T(8,128)(2,1)}, u32[]{:S(2)}) copy-start(bf16[128,1536]{1,0:T(8,128)(2,1)} %stem_ref.3) | copy-start | bytes 1179652
  7.5 4.2 %copy-start = (bf16[1536,384]{1,0:T(8,128)(2,1)S(1)}, bf16[1536,384]{1,0:T(8,128)(2,1)}, u32[]{:S(2)}) copy-start(bf16[1536,384]{1,0:T(8,128)(2,1)} %wv.5) | copy-start | bytes 3538948
  7.5 4.2 %copy-start.1 = (bf16[1536,128]{1,0:T(8,128)(2,1)S(1)}, bf16[1536,128]{1,0:T(8,128)(2,1)}, u32[]{:S(2)}) copy-start(bf16[1536,128]{1,0:T(8,128)(2,1)} %wq.5) | copy-start | bytes 1179652
  7.5 4.2 %copy-start.2 = (bf16[1536,128]{1,0:T(8,128)(2,1)S(1)}, bf16[1536,128]{1,0:T(8,128)(2,1)}, u32[]{:S(2)}) copy-start(bf16[1536,128]{1,0:T(8,128)(2,1)} %wk.5) | copy-start | bytes 1179652
  10.6 10.1 %collective-permute-start.6 = (bf16[512,384]{1,0:T(8,128)(2,1)S(1)}, bf16[512,384]{1,0:T(8,128)(2,1)S(1)}, u32[]{:S(2)}, u32[]{:S(2)}) collective-permute-start(bf16[512,384]{1,0:T(8,128)(2,1)S(1)} %get-tuple-element.59.own), channel_id=1, source_target_pairs={{0,12},{1,5},{2,14},{3,7},{4,8},{5,1},{6,10},{7,3},{8,4},{9,13},{1... | collective-permute-start | bytes 1179656 | tf_op jit(solution)/shard_map/ppermute | solution.py:303
  12.3 10.9 %copy-start.3 = (bf16[1,512,384]{2,1,0:T(8,128)(2,1)S(1)}, bf16[1,512,384]{2,1,0:T(8,128)(2,1)}, u32[]{:S(2)}) copy-start(bf16[1,512,384]{2,1,0:T(8,128)(2,1)} %param.15) | copy-start | bytes 1179652
  12.3 10.8 %copy-start.5 = (bf16[384,1536]{1,0:T(8,128)(2,1)S(1)}, bf16[384,1536]{1,0:T(8,128)(2,1)}, u32[]{:S(2)}) copy-start(bf16[384,1536]{1,0:T(8,128)(2,1)} %w_ref.1) | copy-start | bytes 3538948
  14.4 8.0 %collective-permute-start.7 = (bf16[512,384]{1,0:T(8,128)(2,1)S(1)}, bf16[512,384]{1,0:T(8,128)(2,1)S(1)}, u32[]{:S(2)}, u32[]{:S(2)}) collective-permute-start(bf16[512,384]{1,0:T(8,128)(2,1)S(1)} %collective-permute-done.3.c2), channel_id=1, source_target_pairs={{0,4},{1,13},{2,6},{3,15},{4,0},{5,9},{6,2},{7,11},{8,12},{9,5},{1... | collective-permute-start | bytes 1179656 | tf_op jit(solution)/shard_map/ppermute | solution.py:303
  15.4 11.4 %collective-permute-start.5 = (bf16[512,384]{1,0:T(8,128)(2,1)S(1)}, bf16[512,384]{1,0:T(8,128)(2,1)S(1)}, u32[]{:S(2)}, u32[]{:S(2)}) collective-permute-start(bf16[512,384]{1,0:T(8,128)(2,1)S(1)} %get-tuple-element.59.own), channel_id=1, source_target_pairs={{0,4},{1,13},{2,6},{3,15},{4,0},{5,9},{6,2},{7,11},{8,12},{9,5},{1... | collective-permute-start | bytes 1179656 | tf_op jit(solution)/shard_map/ppermute | solution.py:303
  22.4 8.4 %collective-permute-start.8 = (bf16[512,384]{1,0:T(8,128)(2,1)S(1)}, bf16[512,384]{1,0:T(8,128)(2,1)S(1)}, u32[]{:S(2)}, u32[]{:S(2)}) collective-permute-start(bf16[512,384]{1,0:T(8,128)(2,1)S(1)} %collective-permute-done.6.second), channel_id=1, source_target_pairs={{0,4},{1,13},{2,6},{3,15},{4,0},{5,9},{6,2},{7,11},{8,12},{9,5},{1... | collective-permute-start | bytes 1179656 | tf_op jit(solution)/shard_map/ppermute | solution.py:303
  24.4 7.4 %collective-permute-start.9 = (bf16[192,512]{1,0:T(8,128)(2,1)S(1)}, bf16[192,512]{1,0:T(8,128)(2,1)S(1)}, u32[]{:S(2)}, u32[]{:S(2)}) collective-permute-start(bf16[192,512]{1,0:T(8,128)(2,1)S(1)} %get-tuple-element.74), channel_id=1, source_target_pairs={{0,2},{1,3},{2,0},{3,1},{4,6},{5,7},{6,4},{7,5},{8,10},{9,11},{10,... | collective-permute-start | bytes 589832 | tf_op jit(solution)/shard_map/ppermute | solution.py:312
  31.8 10.3 %collective-permute-start.10 = (bf16[320,512]{1,0:T(8,128)(2,1)S(1)}, bf16[320,512]{1,0:T(8,128)(2,1)S(1)}, u32[]{:S(2)}, u32[]{:S(2)}) collective-permute-start(bf16[320,512]{1,0:T(8,128)(2,1)S(1)} %get-tuple-element.76), channel_id=1, source_target_pairs={{0,2},{1,3},{2,0},{3,1},{4,6},{5,7},{6,4},{7,5},{8,10},{9,11},{10,... | collective-permute-start | bytes 983048 | tf_op jit(solution)/shard_map/ppermute | solution.py:312
  33.4 9.3 %collective-permute-start.11 = (bf16[320,512]{1,0:T(8,128)(2,1)S(1)}, bf16[320,512]{1,0:T(8,128)(2,1)S(1)}, u32[]{:S(2)}, u32[]{:S(2)}) collective-permute-start(bf16[320,512]{1,0:T(8,128)(2,1)S(1)} %get-tuple-element.68.own), channel_id=1, source_target_pairs={{0,1},{1,0},{2,3},{3,2},{4,5},{5,4},{6,7},{7,6},{8,9},{9,8},{10,11... | collective-permute-start | bytes 983048 | tf_op jit(solution)/shard_map/ppermute | solution.py:309
  42.2 1.6 %collective-permute-start.12 = (bf16[320,512]{1,0:T(8,128)(2,1)S(1)}, bf16[320,512]{1,0:T(8,128)(2,1)S(1)}, u32[]{:S(2)}, u32[]{:S(2)}) collective-permute-start(bf16[320,512]{1,0:T(8,128)(2,1)S(1)} %collective-permute-done.10.par), channel_id=1, source_target_pairs={{0,1},{1,0},{2,3},{3,2},{4,5},{5,4},{6,7},{7,6},{8,9},{9,8},{10,11... | collective-permute-start | bytes 983048 | tf_op jit(solution)/shard_map/ppermute | solution.py:309
  42.3 40.4 %collective-permute-start.4 = (bf16[2304,512]{1,0:T(8,128)(2,1)S(1)}, bf16[2304,512]{1,0:T(8,128)(2,1)S(1)}, u32[]{:S(2)}, u32[]{:S(2)}) collective-permute-start(bf16[2304,512]{1,0:T(8,128)(2,1)S(1)} %get-tuple-element.58), channel_id=1, source_target_pairs={{0,1},{1,0},{2,3},{3,2},{4,5},{5,4},{6,7},{7,6},{8,9},{9,8},{10,11... | collective-permute-start | bytes 7077896 | tf_op jit(solution)/shard_map/ppermute | solution.py:309
  51.2 2.0 %collective-permute-start.13 = (bf16[256,1024]{1,0:T(8,128)(2,1)S(1)}, bf16[256,1024]{1,0:T(8,128)(2,1)S(1)}, u32[]{:S(2)}, u32[]{:S(2)}) collective-permute-start(bf16[256,1024]{1,0:T(8,128)(2,1)S(1)} %get-tuple-element.82), channel_id=1, source_target_pairs={{0,1},{1,0},{2,3},{3,2},{4,5},{5,4},{6,7},{7,6},{8,9},{9,8},{10,11... | collective-permute-start | bytes 1572872 | tf_op jit(solution)/shard_map/ppermute | solution.py:309
  53.3 9.8 %collective-permute-start.14 = (bf16[320,512]{1,0:T(8,128)(2,1)S(1)}, bf16[320,512]{1,0:T(8,128)(2,1)S(1)}, u32[]{:S(2)}, u32[]{:S(2)}) collective-permute-start(bf16[320,512]{1,0:T(8,128)(2,1)S(1)} %get-tuple-element.84), channel_id=1, source_target_pairs={{0,2},{1,3},{2,0},{3,1},{4,6},{5,7},{6,4},{7,5},{8,10},{9,11},{10,... | collective-permute-start | bytes 983048 | tf_op jit(solution)/shard_map/ppermute | solution.py:312
  63.8 7.9 %collective-permute-start.16 = (bf16[384,512]{1,0:T(8,128)(2,1)S(1)}, bf16[384,512]{1,0:T(8,128)(2,1)S(1)}, u32[]{:S(2)}, u32[]{:S(2)}) collective-permute-start(bf16[384,512]{1,0:T(8,128)(2,1)S(1)} %get-tuple-element.90), channel_id=1, source_target_pairs={{0,4},{1,13},{2,6},{3,15},{4,0},{5,9},{6,2},{7,11},{8,12},{9,5},{1... | collective-permute-start | bytes 1179656 | tf_op jit(solution)/shard_map/ppermute | solution.py:303
  65.6 12.2 %collective-permute-start.15 = (bf16[384,512]{1,0:T(8,128)(2,1)S(1)}, bf16[384,512]{1,0:T(8,128)(2,1)S(1)}, u32[]{:S(2)}, u32[]{:S(2)}) collective-permute-start(bf16[384,512]{1,0:T(8,128)(2,1)S(1)} %get-tuple-element.88), channel_id=1, source_target_pairs={{0,4},{1,13},{2,6},{3,15},{4,0},{5,9},{6,2},{7,11},{8,12},{9,5},{1... | collective-permute-start | bytes 1179656 | tf_op jit(solution)/shard_map/ppermute | solution.py:303
  71.7 9.1 %collective-permute-start.17 = (bf16[384,512]{1,0:T(8,128)(2,1)S(1)}, bf16[384,512]{1,0:T(8,128)(2,1)S(1)}, u32[]{:S(2)}, u32[]{:S(2)}) collective-permute-start(bf16[384,512]{1,0:T(8,128)(2,1)S(1)} %shard_map.94), channel_id=1, source_target_pairs={{0,12},{1,5},{2,14},{3,7},{4,8},{5,1},{6,10},{7,3},{8,4},{9,13},{1... | collective-permute-start | bytes 1179656 | tf_op jit(solution)/shard_map/ppermute | solution.py:303
  80.9 1.8 %collective-permute-start.18 = (bf16[384,512]{1,0:T(8,128)(2,1)S(1)}, bf16[384,512]{1,0:T(8,128)(2,1)S(1)}, u32[]{:S(2)}, u32[]{:S(2)}) collective-permute-start(bf16[384,512]{1,0:T(8,128)(2,1)S(1)} %shard_map.95.grad.g_mine), channel_id=1, source_target_pairs={{0,1},{1,0},{2,3},{3,2},{4,5},{5,4},{6,7},{7,6},{8,9},{9,8},{10,11... | collective-permute-start | bytes 1179656 | tf_op jit(solution)/shard_map/ppermute | solution.py:309
  83.2 8.4 %collective-permute-start.20 = (bf16[576,384]{1,0:T(8,128)(2,1)S(1)}, bf16[576,384]{1,0:T(8,128)(2,1)S(1)}, u32[]{:S(2)}, u32[]{:S(2)}) collective-permute-start(bf16[576,384]{1,0:T(8,128)(2,1)S(1)} %shard_map.100), channel_id=1, source_target_pairs={{0,2},{1,19},{2,0},{3,17},{16,18},{17,3},{18,16},{19,1},{32,34},{3... | collective-permute-start | bytes 1327112 | tf_op jit(solution)/shard_map/ppermute | solution.py:306
  85.5 12.7 %collective-permute-start.19 = (bf16[576,384]{1,0:T(8,128)(2,1)S(1)}, bf16[576,384]{1,0:T(8,128)(2,1)S(1)}, u32[]{:S(2)}, u32[]{:S(2)}) collective-permute-start(bf16[576,384]{1,0:T(8,128)(2,1)S(1)} %shard_map.98), channel_id=1, source_target_pairs={{0,2},{1,19},{2,0},{3,17},{16,18},{17,3},{18,16},{19,1},{32,34},{3... | collective-permute-start | bytes 1327112 | tf_op jit(solution)/shard_map/ppermute | solution.py:306
  91.7 9.8 %collective-permute-start.21 = (bf16[576,384]{1,0:T(8,128)(2,1)S(1)}, bf16[576,384]{1,0:T(8,128)(2,1)S(1)}, u32[]{:S(2)}, u32[]{:S(2)}) collective-permute-start(bf16[576,384]{1,0:T(8,128)(2,1)S(1)} %shard_map.101), channel_id=1, source_target_pairs={{0,18},{1,3},{2,16},{3,1},{16,2},{17,19},{18,0},{19,17},{32,50},{3... | collective-permute-start | bytes 1327112 | tf_op jit(solution)/shard_map/ppermute | solution.py:306
  101.6 5.6 %collective-permute-start.22 = (bf16[144,384]{1,0:T(8,128)(2,1)S(1)}, bf16[144,384]{1,0:T(8,128)(2,1)S(1)}, u32[]{:S(2)}, u32[]{:S(2)}) collective-permute-start(bf16[144,384]{1,0:T(8,128)(2,1)S(1)} %get-tuple-element.94), channel_id=1, source_target_pairs={{0,32},{1,33},{2,34},{3,35},{16,48},{17,49},{18,50},{19,51},{32,0}... | collective-permute-start | bytes 331784 | tf_op jit(solution)/shard_map/ppermute | solution.py:315
  103.6 6.9 %collective-permute-start.23 = (bf16[144,384]{1,0:T(8,128)(2,1)S(1)}, bf16[144,384]{1,0:T(8,128)(2,1)S(1)}, u32[]{:S(2)}, u32[]{:S(2)}) collective-permute-start(bf16[144,384]{1,0:T(8,128)(2,1)S(1)} %get-tuple-element.95), channel_id=1, source_target_pairs={{0,96},{1,97},{2,98},{3,99},{16,112},{17,113},{18,114},{19,115},{3... | collective-permute-start | bytes 331784 | tf_op jit(solution)/shard_map/ppermute | solution.py:315
  106.1 6.3 %collective-permute-start.24 = (bf16[144,384]{1,0:T(8,128)(2,1)S(1)}, bf16[144,384]{1,0:T(8,128)(2,1)S(1)}, u32[]{:S(2)}, u32[]{:S(2)}) collective-permute-start(bf16[144,384]{1,0:T(8,128)(2,1)S(1)} %get-tuple-element.96), channel_id=1, source_target_pairs={{0,64},{1,65},{2,66},{3,67},{16,80},{17,81},{18,82},{19,83},{32,96... | collective-permute-start | bytes 331784 | tf_op jit(solution)/shard_map/ppermute | solution.py:315
  (2 other events, 1.8 us)
